TPU v7x, 32 devices: a whole 2x2x4 slice. The times are simulated.
32 devices in a mesh: sec: 2 (over x), sp: 8 (over z, y), dp: 2 (over core).
Axes of the slice: x: 2, y: 2, z: 4, core: 2. Of those that a mesh axis runs over, the one named last changes fastest.
Arguments:
- block_data: bfloat16 [2, 2, 5, 8, 32, 512], P('sec', 'dp', None, 'sp'), may hold values from -6 to 6
- code_index: int32 [2, 6, 5, 8, 32], P('dp', None, None, 'sp'), may hold values from 0 to 7, as said below
- levels: int32 [6], replicated, may hold values from 3 to 8, as said below
- w_space: bfloat16 [2, 9, 512, 512], P('sec', None, 'sp'), may hold values from -0.09375 to 0.09375
- w_time: bfloat16 [2, 3, 512, 512], P('sec', None, 'sp'), may hold values from -0.15625 to 0.15625
- enc_proj: bfloat16 [6, 512], replicated, may hold values from -0.25 to 0.25
- dec_proj: bfloat16 [6, 512], replicated, may hold values from -2.5 to 2.5
Outputs:
- space_grad: float32 [2, 9, 512, 512], P('sec', None, 'sp')
- time_grad: float32 [2, 3, 512, 512], P('sec', None, 'sp')
- proj_grad: float32 [2, 6, 512], P('sec')
Inputs may be any that keep to these rules, and one draw needn't show every extreme that they name: levels[l] is the number of code levels of latent dimension l; 3 and 8 both occur. code_index[b, l, t, r, c] is below levels[l].
All inputs are finite; a program needn't handle non-finite values.
Results may differ from a plain program's by a relative error of at most 0.0055.
Values may be sent and summed in bfloat16 or wider, within the bound.
No kernel may reach another device: no remote copies, remote signals or barrier semaphores. Data moves between devices by JAX's collectives and lax.ppermute only.
A program may use at most 128 MiB of HBM per device.

v0:
```python
import jax
import jax.numpy as jnp
from jax import lax
from jax.sharding import PartitionSpec as P

HIGH = lax.Precision.HIGHEST


def padded_2(block, sides, width):
    for axis, dim in sides:
        count = lax.axis_size(axis)
        forward = [(i, i + 1) for i in range(count - 1)]
        backward = [(target, source) for source, target in forward]
        low = lax.ppermute(
            lax.slice_in_dim(block, block.shape[dim] - width, None, axis=dim), axis, forward
        )
        high = lax.ppermute(lax.slice_in_dim(block, 0, width, axis=dim), axis, backward)
        block = jnp.concatenate([low, block, high], axis=dim)
    return block


def shifted(block, axis, distance):
    devices = range(lax.axis_size(axis))
    route = [(i - distance, i) for i in devices if i - distance in devices]
    return lax.ppermute(block, axis, route)


def latent_values(code_index, levels):
    half_width = (levels.astype(jnp.float32) - 1.0) * 0.5
    half_width = half_width[None, :, None, None, None]
    return jnp.moveaxis((code_index.astype(jnp.float32) - half_width) / half_width, 1, -1)


def silu_slope(inputs):
    logistic = jax.nn.sigmoid(inputs)
    return logistic * (1.0 + inputs * (1.0 - logistic))


def flat_dot(operand, matrix):
    leading = operand.shape[:-1]
    flat = jnp.dot(
        operand.reshape(-1, operand.shape[-1]), matrix, preferred_element_type=jnp.float32
    )
    return flat.reshape(leading + (matrix.shape[-1],))


def high_dot(operand, matrix):
    leading = operand.shape[:-1]
    flat = jnp.dot(
        operand.reshape(-1, operand.shape[-1]),
        matrix,
        precision=HIGH,
        preferred_element_type=jnp.float32,
    )
    return flat.reshape(leading + (matrix.shape[-1],))


def space_apply(padded, kernel, row_count, col_count):
    summed = jnp.zeros(padded.shape[:2] + (row_count, col_count, kernel.shape[2]), jnp.float32)
    for tap_index in range(9):
        row_off, col_off = (tap_index // 3, tap_index % 3)
        window = padded[:, :, row_off : row_off + row_count, col_off : col_off + col_count]
        summed = summed + flat_dot(window, kernel[tap_index])
    return summed


def space_transpose(padded, kernel, row_count, col_count):
    summed = jnp.zeros(padded.shape[:2] + (row_count, col_count, kernel.shape[1]), jnp.float32)
    for tap_index in range(9):
        row_off, col_off = (tap_index // 3, tap_index % 3)
        window = padded[
            :, :, 2 - row_off : 2 - row_off + row_count, 2 - col_off : 2 - col_off + col_count
        ]
        summed = summed + flat_dot(window, kernel[tap_index].T)
    return summed


def time_apply(inputs, kernel):
    frame_count = inputs.shape[1]
    padded = jnp.pad(inputs, ((0, 0), (2, 0), (0, 0), (0, 0), (0, 0)))
    summed = jnp.zeros(inputs.shape[:-1] + (kernel.shape[2],), jnp.float32)
    for lag_index in range(3):
        summed = summed + flat_dot(
            padded[:, 2 - lag_index : 2 - lag_index + frame_count], kernel[lag_index]
        )
    return summed


def time_transpose(gradient, kernel):
    frame_count = gradient.shape[1]
    padded = jnp.pad(gradient, ((0, 0), (0, 2), (0, 0), (0, 0), (0, 0)))
    summed = jnp.zeros(gradient.shape[:-1] + (kernel.shape[1],), jnp.float32)
    for lag_index in range(3):
        summed = summed + flat_dot(
            padded[:, lag_index : lag_index + frame_count], kernel[lag_index].T
        )
    return summed


def space_kernel_grad(padded, gradient, row_count, col_count):
    flat_grad = gradient.reshape(-1, gradient.shape[-1])
    pieces = []
    for tap_index in range(9):
        row_off, col_off = (tap_index // 3, tap_index % 3)
        window = padded[:, :, row_off : row_off + row_count, col_off : col_off + col_count]
        pieces.append(
            jnp.dot(
                window.reshape(-1, window.shape[-1]).T,
                flat_grad,
                preferred_element_type=jnp.float32,
            )
        )
    return pieces


def time_kernel_grad(front_padded, gradient, frame_count):
    flat_grad = gradient.reshape(-1, gradient.shape[-1])
    pieces = []
    for lag_index in range(3):
        window = front_padded[:, 2 - lag_index : 2 - lag_index + frame_count]
        pieces.append(
            jnp.dot(
                window.reshape(-1, window.shape[-1]).T,
                flat_grad,
                preferred_element_type=jnp.float32,
            )
        )
    return pieces


def pad_columns(inputs):
    return jnp.pad(inputs, ((0, 0), (0, 0), (0, 0), (1, 1), (0, 0)))


def local(block_data, code_index, levels, w_space, w_time, enc_proj, dec_proj):
    decoder_side = lax.axis_index("sec") == 1
    features = block_data[0]
    frame_count, row_count, col_count = (features.shape[1], features.shape[2], features.shape[3])
    channel_count = features.shape[4]
    latent_count = code_index.shape[1]
    grad_scale = float(
        lax.axis_size("dp") * frame_count * row_count * lax.axis_size("sp") * col_count
    ) ** (-0.5)
    space_full, time_full = (
        lax.all_gather(w_space[0], "sp", axis=1, tiled=True),
        lax.all_gather(w_time[0], "sp", axis=1, tiled=True),
    )
    projection = jnp.where(decoder_side, dec_proj, enc_proj)
    latents = latent_values(code_index, levels)
    flat_latents = latents.reshape(-1, latent_count)
    dec_in = high_dot(latents, projection.astype(jnp.float32)).astype(jnp.bfloat16)
    block_in = jnp.where(decoder_side, dec_in, features)
    in_rows = padded_2(block_in, (("sp", 2),), 1)
    in_padded = pad_columns(in_rows)
    pre_act = space_apply(in_padded, space_full, row_count, col_count)
    hidden = jax.nn.silu(pre_act).astype(jnp.bfloat16)
    slope_values = silu_slope(pre_act)
    latent_shape = features.shape[:-1] + (latent_count,)
    zero_latent = jnp.zeros(latent_shape, jnp.float32)
    zero_proj = jnp.zeros((latent_count, channel_count), jnp.float32)

    def decoder_inner():
        return (time_transpose(features, time_full) * slope_values).astype(jnp.bfloat16)

    def skip_inner():
        return jnp.zeros(features.shape, jnp.bfloat16)

    inner_dec = lax.cond(decoder_side, decoder_inner, skip_inner)
    inner_rows = padded_2(inner_dec, (("sp", 2),), 1)

    def decoder_latent():
        input_grad = features.astype(jnp.float32) + space_transpose(
            pad_columns(inner_rows), space_full, row_count, col_count
        )
        lat_grad = high_dot(input_grad, projection.astype(jnp.float32).T)
        proj_part = jnp.dot(
            flat_latents.T,
            input_grad.reshape(-1, channel_count),
            precision=HIGH,
            preferred_element_type=jnp.float32,
        )
        return (lat_grad, proj_part)

    def skip_latent():
        return (zero_latent, zero_proj)

    latent_grad, dec_proj_grad = lax.cond(decoder_side, decoder_latent, skip_latent)
    received_grad = shifted(latent_grad, "sec", -1)

    def encoder_rest():
        block_out = features.astype(jnp.float32) + time_apply(hidden, time_full)
        bounded = high_dot(block_out, projection.astype(jnp.float32).T)
        code_grad = received_grad * (1.0 - jnp.tanh(bounded) ** 2)
        out_part = high_dot(code_grad, projection.astype(jnp.float32)).astype(jnp.bfloat16)
        inner_part = (time_transpose(out_part, time_full) * slope_values).astype(jnp.bfloat16)
        proj_part = jnp.dot(
            code_grad.reshape(-1, latent_count).T,
            block_out.reshape(-1, channel_count),
            precision=HIGH,
            preferred_element_type=jnp.float32,
        )
        return (out_part, inner_part, proj_part)

    def skip_rest():
        empty = jnp.zeros(features.shape, jnp.bfloat16)
        return (empty, empty, zero_proj)

    enc_out_grad, inner_enc, enc_proj_grad = lax.cond(decoder_side, skip_rest, encoder_rest)
    out_grad = jnp.where(decoder_side, features, enc_out_grad)
    inner_grad = jnp.where(decoder_side, inner_dec, inner_enc)
    proj_local = jnp.where(decoder_side, dec_proj_grad, enc_proj_grad)
    hidden_front = jnp.pad(hidden, ((0, 0), (2, 0), (0, 0), (0, 0), (0, 0)))
    pieces = space_kernel_grad(in_padded, inner_grad, row_count, col_count)
    pieces = pieces + time_kernel_grad(hidden_front, out_grad, frame_count)
    grad_shard = lax.psum_scatter(
        jnp.stack(pieces, axis=1) * grad_scale, "sp", scatter_dimension=0, tiled=True
    )
    grad_shard = lax.psum(grad_shard, "dp")
    proj_total = lax.psum(proj_local * grad_scale, ("sp", "dp"))
    space_grad = jnp.transpose(grad_shard[:, :9], (1, 0, 2))[None]
    time_grad = jnp.transpose(grad_shard[:, 9:], (1, 0, 2))[None]
    return (space_grad, time_grad, proj_total[None])


def solution(mesh):
    placed = (
        P("sec", "dp", None, "sp", None, None),
        P("dp", None, None, "sp", None),
        P(),
        P("sec", None, "sp", None),
        P("sec", None, "sp", None),
        P(),
        P(),
    )
    return jax.shard_map(
        local,
        mesh=mesh,
        in_specs=placed,
        out_specs=(P("sec", None, "sp", None), P("sec", None, "sp", None), P("sec", None, None)),
        check_vma=False,
    )
```

profile of v0, /device:TPU:0, one launch (start us, length us, event | category | flops | bytes accessed | tf_op | source)
XLA Modules:
  0.0 472.8 jit_solution(7302516077637549142)
XLA Ops:
  9.3 1.4 fusion.119
  12.0 5.5 %collective-permute-start = (bf16[1,5,1,32,512]{4,3,1,2,0:T(8,128)(2,1)S(1)}, bf16[1,5,1,32,512]{4,3,1,2,0:T(8,128)(2,1)S(1)}, u32[]{:S(2)}, u32[]{:S(2)}) collective-permute-start(bf16[1,5,1,32,512]{4,3,1,2,0:T(8,128)(2,1)S(1)} %bitcast.391), channel_id=1, source_target_pairs={{0,2},{2,4},{4,6},{6,8},{8,10},{10,12},{12,14},{1,3},{3,5},{5,7},{... | collective-permute-start | bytes 491528 | tf_op jit(solution)/shard_map/ppermute | solution.py:14
  17.6 2.2 collective-permute-done.1
  19.8 5.5 %collective-permute-done = bf16[1,5,1,32,512]{4,3,1,2,0:T(8,128)(2,1)S(1)} collective-permute-done((bf16[1,5,1,32,512]{4,3,1,2,0:T(8,128)(2,1)S(1)}, bf16[1,5,1,32,512]{4,3,1,2,0:T(8,128)(2,1)S(1)}, u32[]{:S(2)}, u32[]{:S(2)}) %collective-permute-start) | collective-permute-done | bytes 163872 | tf_op jit(solution)/shard_map/ppermute | solution.py:14
  25.4 67.5 %all-gather.7.cloned.1.call-done = bf16[1,9,512,512]{3,2,1,0:T(8,128)(2,1)} async-done(((bf16[1,9,64,512]{3,2,1,0:T(8,128)(2,1)}), bf16[1,9,512,512]{3,2,1,0:T(8,128)(2,1)}) %all-gather.7.cloned.1.call-update) | async-done | bytes 4718608 | tf_op jit(solution)/shard_map/all_gather | solution.py:145
  93.0 1.4 fusion.126
  94.4 1.4 fusion.125
  100.0 37.6 %all-gather.5.cloned.1.call-done = bf16[1,3,512,512]{3,2,1,0:T(8,128)(2,1)} async-done(((bf16[1,3,64,512]{3,2,1,0:T(8,128)(2,1)}), bf16[1,3,512,512]{3,2,1,0:T(8,128)(2,1)}) %all-gather.5.cloned.1.call-update) | async-done | bytes 1572880 | tf_op jit(solution)/shard_map/all_gather | solution.py:146
  138.9 4.6 collective-permute-start.2
  144.8 2.6 collective-permute-done.2
  147.5 1.4 collective-permute-start.4
  149.0 15.2 %collective-permute-done.4 = f32[1,5,1,32,6]{3,4,1,2,0:T(8,128)S(1)} collective-permute-done((f32[1,5,1,32,6]{3,4,1,2,0:T(8,128)S(1)}, f32[1,5,1,32,6]{3,4,1,2,0:T(8,128)S(1)}, u32[]{:S(2)}, u32[]{:S(2)}) %collective-permute-start.4) | collective-permute-done | bytes 3872 | tf_op jit(solution)/shard_map/ppermute | solution.py:25
  164.2 2.8 conditional.5
  167.1 1.4 fusion.116
  168.5 2.2 fusion.115
  170.7 1.3 fusion.114
  173.4 1.3 fusion.112
  176.1 1.3 fusion.110
  182.7 1.4 fusion.105
  184.1 10.7 %broadcast_multiply_fusion = f32[512,12,512]{2,0,1:T(8,128)} fusion(f32[512,12,512]{2,0,1:T(8,128)} %fusion.105), kind=kLoop, calls=%fused_computation.124 | loop fusion | flops 3145728 | bytes 25165824 | tf_op jit(solution)/shard_map/mul | solution.py:216
  194.9 207.7 %reduce-scatter.2.cloned.1.call-done = f32[64,12,512]{2,0,1:T(8,128)} async-done(((f32[512,12,512]{2,0,1:T(8,128)}), f32[64,12,512]{2,0,1:T(8,128)}) %reduce-scatter.2.cloned.1.call-update) | async-done | bytes 1572880 | tf_op jit(solution)/shard_map/reduce_scatter | solution.py:215
  402.6 59.5 %psum.15 = f32[1,6,512]{2,0,1:T(1,128)} all-reduce(f32[1,6,512]{2,0,1:T(1,128)S(1)} %broadcast_in_dim.21), channel_id=1, replica_groups=mesh['sec'=2,'sp'=8,'dp'=2] {'sp','dp'}, use_global_device_ids=true, to_apply=%region_8.9 | all-reduce | flops 3072 | bytes 24576 | tf_op jit(solution)/shard_map/psum | solution.py:219
  462.2 1.8 slice_bitcast_fusion.19
  463.9 2.4 slice_bitcast_fusion
  (67 shorter events, 21.3 us)
Async XLA Ops:
  7.2 85.8 %all-gather.7.cloned.1.call-start = ((), (), s32[]{:S(2)}) async-start(), calls=%async_computation.4 | async-start | bytes 5308416 | tf_op jit(solution)/shard_map/all_gather | solution.py:145
  7.9 129.7 %all-gather.5.cloned.1.call-start = ((), (), s32[]{:S(2)}) async-start(), calls=%async_computation.3 | async-start | bytes 1769472 | tf_op jit(solution)/shard_map/all_gather | solution.py:146
  10.7 88.4 %copy-start.6 = (bf16[5,32,512]{2,1,0:T(8,128)(2,1)}, bf16[5,32,512]{2,1,0:T(8,128)(2,1)S(1)}, u32[]{:S(2)}) copy-start(bf16[5,32,512]{2,1,0:T(8,128)(2,1)S(1)} %fusion.119) | copy-start | bytes 491524
  10.7 9.1 %collective-permute-start.1 = (bf16[1,5,1,32,512]{4,3,1,2,0:T(8,128)(2,1)S(1)}, bf16[1,5,1,32,512]{4,3,1,2,0:T(8,128)(2,1)S(1)}, u32[]{:S(2)}, u32[]{:S(2)}) collective-permute-start(bf16[1,5,1,32,512]{4,3,1,2,0:T(8,128)(2,1)S(1)} %bitcast.390), channel_id=1, source_target_pairs={{2,0},{4,2},{6,4},{8,6},{10,8},{12,10},{14,12},{3,1},{5,3},{7,5},{... | collective-permute-start | bytes 491528 | tf_op jit(solution)/shard_map/ppermute | solution.py:17
  12.0 13.3 %collective-permute-start = (bf16[1,5,1,32,512]{4,3,1,2,0:T(8,128)(2,1)S(1)}, bf16[1,5,1,32,512]{4,3,1,2,0:T(8,128)(2,1)S(1)}, u32[]{:S(2)}, u32[]{:S(2)}) collective-permute-start(bf16[1,5,1,32,512]{4,3,1,2,0:T(8,128)(2,1)S(1)} %bitcast.391), channel_id=1, source_target_pairs={{0,2},{2,4},{4,6},{6,8},{8,10},{10,12},{12,14},{1,3},{3,5},{5,7},{... | collective-permute-start | bytes 491528 | tf_op jit(solution)/shard_map/ppermute | solution.py:14
  17.5 385.0 %reduce-scatter.2.cloned.1.call-start = ((), (), s32[]{:S(2)}) async-start(), calls=%async_computation.1 | async-start | bytes 14155776 | tf_op jit(solution)/shard_map/reduce_scatter | solution.py:215
  19.8 79.8 %copy-start.4 = (bf16[1,5,1,32,512]{4,3,1,2,0:T(8,128)(2,1)}, bf16[1,5,1,32,512]{4,3,1,2,0:T(8,128)(2,1)S(1)}, u32[]{:S(2)}) copy-start(bf16[1,5,1,32,512]{4,3,1,2,0:T(8,128)(2,1)S(1)} %collective-permute-done.1) | copy-start | bytes 491524
  25.3 70.6 %copy-start.8 = (bf16[1,5,1,32,512]{4,3,1,2,0:T(8,128)(2,1)}, bf16[1,5,1,32,512]{4,3,1,2,0:T(8,128)(2,1)S(1)}, u32[]{:S(2)}) copy-start(bf16[1,5,1,32,512]{4,3,1,2,0:T(8,128)(2,1)S(1)} %collective-permute-done) | copy-start | bytes 491524
  93.0 5.5 %copy-start = (bf16[1,9,512,512]{3,2,1,0:T(8,128)(2,1)S(1)}, bf16[1,9,512,512]{3,2,1,0:T(8,128)(2,1)}, u32[]{:S(2)}) copy-start(bf16[1,9,512,512]{3,2,1,0:T(8,128)(2,1)} %all-gather.7.cloned.1.call-done) | copy-start | bytes 14155780
  97.2 40.4 %copy-start.3 = (bf16[1,1,5,1,32,512]{5,4,3,2,1,0:T(8,128)(2,1)S(1)}, bf16[1,1,5,1,32,512]{5,4,3,2,1,0:T(8,128)(2,1)}, u32[]{:S(2)}) copy-start(bf16[1,1,5,1,32,512]{5,4,3,2,1,0:T(8,128)(2,1)} %param.13) | copy-start | bytes 491524
  99.1 44.4 %copy-start.9 = (s32[1,6,5,1,32]{4,3,2,1,0:T(1,128)S(1)}, s32[1,6,5,1,32]{4,3,2,1,0:T(1,128)}, u32[]{:S(2)}) copy-start(s32[1,6,5,1,32]{4,3,2,1,0:T(1,128)} %param.14) | copy-start | bytes 11524
  137.6 7.2 %collective-permute-start.3 = (bf16[1,5,1,32,512]{4,3,1,2,0:T(8,128)(2,1)S(1)}, bf16[1,5,1,32,512]{4,3,1,2,0:T(8,128)(2,1)S(1)}, u32[]{:S(2)}, u32[]{:S(2)}) collective-permute-start(bf16[1,5,1,32,512]{4,3,1,2,0:T(8,128)(2,1)S(1)} %get-tuple-element.71), channel_id=1, source_target_pairs={{2,0},{4,2},{6,4},{8,6},{10,8},{12,10},{14,12},{3,1},{5,3},{7,5},{... | collective-permute-start | bytes 491528 | tf_op jit(solution)/shard_map/ppermute | solution.py:17
  138.9 8.5 %collective-permute-start.2 = (bf16[1,5,1,32,512]{4,3,1,2,0:T(8,128)(2,1)S(1)}, bf16[1,5,1,32,512]{4,3,1,2,0:T(8,128)(2,1)S(1)}, u32[]{:S(2)}, u32[]{:S(2)}) collective-permute-start(bf16[1,5,1,32,512]{4,3,1,2,0:T(8,128)(2,1)S(1)} %get-tuple-element.71), channel_id=1, source_target_pairs={{0,2},{2,4},{4,6},{6,8},{8,10},{10,12},{12,14},{1,3},{3,5},{5,7},{... | collective-permute-start | bytes 491528 | tf_op jit(solution)/shard_map/ppermute | solution.py:14
  147.4 16.8 %copy-start.2 = (bf16[1,3,512,512]{3,2,1,0:T(8,128)(2,1)S(1)}, bf16[1,3,512,512]{3,2,1,0:T(8,128)(2,1)}, u32[]{:S(2)}) copy-start(bf16[1,3,512,512]{3,2,1,0:T(8,128)(2,1)} %all-gather.5.cloned.1.call-done) | copy-start | bytes 4718596
  147.5 16.7 %collective-permute-start.4 = (f32[1,5,1,32,6]{3,4,1,2,0:T(8,128)S(1)}, f32[1,5,1,32,6]{3,4,1,2,0:T(8,128)S(1)}, u32[]{:S(2)}, u32[]{:S(2)}) collective-permute-start(f32[1,5,1,32,6]{3,4,1,2,0:T(8,128)S(1)} %get-tuple-element.54), channel_id=1, source_target_pairs={{16,0},{17,1},{18,2},{19,3},{20,4},{21,5},{22,6},{23,7},{24,8},{25... | collective-permute-start | bytes 11528 | tf_op jit(solution)/shard_map/ppermute | solution.py:25
  167.0 6.4 %copy-start.7 = (bf16[5,32,512]{2,1,0:T(8,128)(2,1)S(1)}, bf16[5,32,512]{2,1,0:T(8,128)(2,1)}, u32[]{:S(2)}) copy-start(bf16[5,32,512]{2,1,0:T(8,128)(2,1)} %copy-done.6) | copy-start | bytes 491524
  170.7 6.7 %copy-start.5 = (bf16[1,5,1,32,512]{4,3,1,2,0:T(8,128)(2,1)S(1)}, bf16[1,5,1,32,512]{4,3,1,2,0:T(8,128)(2,1)}, u32[]{:S(2)}) copy-start(bf16[1,5,1,32,512]{4,3,1,2,0:T(8,128)(2,1)} %copy-done.4) | copy-start | bytes 491524
  194.8 267.4 %all-reduce.8.cloned.1.call-start = ((), (), s32[]{:S(2)}) async-start(), calls=%async_computation.2 | async-start | bytes 3145728 | tf_op jit(solution)/shard_map/psum | solution.py:218
Sparse Core Ops, SparseCore 0:
  10.2 82.7 all-gather.6
  95.2 42.3 all-gather.4
  194.9 207.5 reduce-scatter.1
  404.8 19.5 all-reduce.7
where the time goes:
time: 474 us; the launch traced here: 473 us
  waiting for transfers between devices  340 us (72%)
  blocking collectives  59.5 us (13%)
  matrix products  27.8 us (6%)
  starting transfers between devices  14.2 us (3%)
  between operations  14 us (3%)
  other arithmetic  12.6 us (3%)
    reduce_scatter x1, waiting for transfers between devices, local(): lax.psum_scatter(jnp.stack(pieces, axis=1) * grad_scale, 'sp', scatter_di...  208 us
    all_gather x1, waiting for transfers between devices, local(): lax.all_gather(w_space[0], 'sp', axis=1, tiled=True)  67.5 us
    psum x1, blocking collectives, local(): proj_total = lax.psum(proj_local * grad_scale, ('sp', 'dp'))  59.5 us
    all_gather x1, waiting for transfers between devices, local(): lax.all_gather(w_time[0], 'sp', axis=1, tiled=True)  37.6 us
    ppermute x1, waiting for transfers between devices, shifted(): return lax.ppermute(block, axis, route)  15.2 us
    dot_general x9, matrix products, space_kernel_grad(): jnp.dot(window.reshape(-1, window.shape[-1]).T, flat_grad, preferred_elem...  12.9 us
    mul x1, other arithmetic, local(): jnp.stack(pieces, axis=1) * grad_scale  10.7 us
    ppermute x2, starting transfers between devices, padded_2(): lax.ppermute(lax.slice_in_dim(block, block.shape[dim] - width, None, axis...  10.1 us
  transfers between devices with their start and end apart: 9, of which 8 were waited for; matrix products, arithmetic and copies ran while one was open for 2% of the time, Pallas kernels for 0%

commit v1 on v0

v1 whole, which is shorter than its diff:
```python
import jax
import jax.numpy as jnp
from jax import lax
from jax.sharding import PartitionSpec as P

HIGH = lax.Precision.HIGHEST
F32 = jnp.float32
BF16 = jnp.bfloat16


def ring_order(count):
    return list(range(0, count, 2)) + list(range(count - 1, 0, -2))


def ring_gather(shard, axis):
    count = lax.axis_size(axis)
    order = ring_order(count)
    place = [order.index(i) for i in range(count)]
    forward = [(order[i], order[(i + 1) % count]) for i in range(count)]
    backward = [(target, source) for source, target in forward]
    here = jnp.array(place, jnp.int32)[lax.axis_index(axis)]
    order_table = jnp.array(order, jnp.int32)
    gathered = jnp.zeros((count,) + shard.shape, shard.dtype)

    def put(gathered, block, position):
        return lax.dynamic_update_index_in_dim(
            gathered, block, order_table[position % count], 0
        )

    gathered = put(gathered, shard, here)
    down = up = shard
    for step in range(1, count // 2 + 1):
        down = lax.ppermute(down, axis, forward)
        gathered = put(gathered, down, here - step + count)
        if step < count - step:
            up = lax.ppermute(up, axis, backward)
            gathered = put(gathered, up, here + step)
    return gathered


def swap_sum(values, axis):
    count = lax.axis_size(axis)
    bit = 1
    while bit < count:
        values = values + lax.ppermute(values, axis, [(i, i ^ bit) for i in range(count)])
        bit *= 2
    return values


def silu_slope(inputs):
    logistic = jax.nn.sigmoid(inputs)
    return logistic * (1.0 + inputs * (1.0 - logistic))


def dot32(left, right):
    return jnp.dot(left, right, precision=HIGH, preferred_element_type=F32)


def dot16(left, right):
    return jnp.dot(left, right, preferred_element_type=F32)


def move(values, dim, by):
    if by == 0:
        return values
    pads = [(0, 0, 0)] * values.ndim
    pads[dim] = (by, -by, 0)
    return lax.pad(values, jnp.zeros((), values.dtype), pads)


def local(block_data, code_index, levels, w_space, w_time, enc_proj, dec_proj):
    sp = lax.axis_size("sp")
    decoder = lax.axis_index("sec") == 1
    x = block_data[0, 0, :, 0]
    frames, cols, chans = x.shape
    lat = code_index.shape[1]
    own = w_space.shape[2]
    scale = float(lax.axis_size("dp") * frames * sp * cols) ** (-0.5)
    mine = lax.axis_index("sp")

    v = ring_gather(x.reshape(frames * cols, chans), "sp")
    pieces = w_space[0].reshape(9, own, sp, own).transpose(2, 1, 0, 3).reshape(sp, own, 9 * own)
    w_cat = lax.all_to_all(pieces, "sp", 0, 0, tiled=True).reshape(chans, 9 * own)
    codes = lax.all_gather(code_index[0, :, :, 0], "sp", axis=0)
    half = (levels.astype(F32) - 1.0) * 0.5
    latents = (codes.astype(F32) - half[:, None, None]) / half[:, None, None]
    latents = latents.transpose(0, 2, 3, 1).reshape(-1, lat)
    v = v.reshape(-1, chans)
    count = v.shape[0]
    grid = (sp, frames, cols)
    proj = jnp.where(decoder, dec_proj, enc_proj).astype(F32)
    wt = w_time[0]

    def conv_sum(taps):
        taps = taps.reshape(grid + (3, 3, own))
        total = 0.0
        for j in range(3):
            rows = sum(move(taps[:, :, :, i, j], 0, 1 - i) for i in range(3))
            total = total + move(rows, 2, 1 - j)
        return total.reshape(count, own)

    def spread(inner):
        inner = inner.reshape(grid + (own,))
        shifted = [move(move(inner, 0, i - 1), 2, j - 1) for i in range(3) for j in range(3)]
        return jnp.stack(shifted, axis=3).reshape(count, 9 * own)

    def later(values, k):
        return move(values.reshape(grid + (-1,)), 1, -k).reshape(count, -1)

    def earlier(values, k):
        return move(values.reshape(grid + (-1,)), 1, k).reshape(count, -1)

    def decoder_first():
        p_cat = dot32(proj, w_cat.astype(F32))
        pre = conv_sum(dot32(latents, p_cat))
        back = sum(later(dot16(v, wt[k].T), k) for k in range(3))
        inner = (back * silu_slope(pre)).astype(BF16)
        part = dot32(spread(inner).astype(F32), p_cat.T)
        return pre, inner, part.T

    def encoder_first():
        pre = conv_sum(dot16(v, w_cat))
        hidden = jax.nn.silu(pre).astype(BF16).astype(F32)
        back = dot32(wt.reshape(3 * own, chans).astype(F32), proj.T).reshape(3, own, lat)
        part = sum(dot32(earlier(hidden, k), back[k]) for k in range(3))
        return pre, jnp.zeros((count, own), BF16), part.T

    pre, inner_dec, part = lax.cond(decoder, decoder_first, encoder_first)
    total = swap_sum(part, "sp").T + dot32(v.astype(F32), proj.T)
    received = lax.ppermute(total, "sec", [(1, 0)])
    hidden = jax.nn.silu(pre).astype(BF16)
    hid_cat = jnp.stack([earlier(hidden, k) for k in range(3)], axis=1).reshape(count, 3 * own)
    own_rows = lax.dynamic_slice_in_dim(v, mine * frames * cols, frames * cols, 0).astype(F32)

    def rows_of(values):
        return lax.dynamic_slice_in_dim(values, mine * frames * cols, frames * cols, 0)

    def decoder_second():
        inner_cat = spread(inner_dec)
        short = dot32(latents.T, inner_cat.astype(F32))
        big = dot32(proj.T, short)
        time = dot16(hid_cat.T, v)
        part = dot32(short, w_cat.astype(F32).T) + dot32(rows_of(latents).T, own_rows)
        return big, time, part

    def encoder_second():
        code_grad = received * (1.0 - jnp.tanh(total) ** 2)
        flat = wt.reshape(3 * own, chans).astype(F32)
        back = dot32(proj, flat.T)
        spread_back = dot32(code_grad, back).reshape(count, 3, own)
        inner = sum(later(spread_back[:, k], k) for k in range(3)) * silu_slope(pre)
        big = dot16(v.T, spread(inner.astype(BF16)))
        short = dot32(code_grad.T, hid_cat.astype(F32))
        time = dot32(short.T, proj)
        part = dot32(short, flat) + dot32(rows_of(code_grad).T, own_rows)
        return big, time, part

    big, time, part = lax.cond(decoder, decoder_second, encoder_second)
    big = (big * scale).astype(BF16).reshape(sp, own, 9 * own)
    big = lax.all_to_all(big, "sp", 0, 0, tiled=True)
    swap = [(0, 1), (1, 0)]
    time = time * scale
    both = jnp.concatenate([big.reshape(-1, 9 * own)], 0)
    other = lax.ppermute(both, "dp", swap)
    summed = both.astype(F32) + other.astype(F32)
    space = summed.reshape(sp, own, 9, own).transpose(2, 1, 0, 3).reshape(9, own, chans)
    time = time + lax.ppermute(time, "dp", swap)
    proj_total = swap_sum(part * scale, "sp")
    proj_total = proj_total + lax.ppermute(proj_total, "dp", swap)
    return space[None], time.reshape(1, 3, own, chans), proj_total[None]


def solution(mesh):
    placed = (
        P("sec", "dp", None, "sp", None, None),
        P("dp", None, None, "sp", None),
        P(),
        P("sec", None, "sp", None),
        P("sec", None, "sp", None),
        P(),
        P(),
    )
    return jax.shard_map(
        local,
        mesh=mesh,
        in_specs=placed,
        out_specs=(P("sec", None, "sp", None), P("sec", None, "sp", None), P("sec", None, None)),
        check_vma=False,
    )
```

time: 474 us -> 250 us (0.53)
  waiting for transfers between devices: 340 us -> 82.5 us
  local copies, waits for them, and re-layouts: 4.2 us -> 56.6 us
  blocking collectives: 59.5 us -> 38.9 us
  matrix products: 27.8 us -> 12 us
  between operations: 14 us -> 22.8 us
  loops' own time: 0.09 us -> 7.73 us
  starting transfers between devices: 14.2 us -> 20.6 us
    reduce_scatter x1 -> x0, waiting for transfers between devices: 208 us -> none  [local(): lax.psum_scatter(jnp.stack(pieces, axis=1) * grad_scale, 'sp', scatter_di...]
    all_gather x2 -> x0, waiting for transfers between devices: 105 us -> none  [the longest x1 67.5 us: local(): lax.all_gather(w_space[0], 'sp', axis=1, tiled=True)]
    psum x1 -> x0, blocking collectives: 59.5 us -> none  [local(): proj_total = lax.psum(proj_local * grad_scale, ('sp', 'dp'))]
    ppermute x5 -> x17, waiting for transfers between devices: 26.8 us -> 71.1 us  [the longest x1 34 us: local(): received = lax.ppermute(total, 'sec', [(1, 0)])]
    all_gather x0 -> x1, blocking collectives: none -> 38.9 us  [local(): codes = lax.all_gather(code_index[0, :, :, 0], 'sp', axis=0)]
    reshape x0 -> x6, local copies, waits for them, and re-layouts: none -> 18.1 us  [the longest x1 8.96 us: conv_sum(): taps = taps.reshape(grid + (3, 3, own))]
    dot_general x31 -> x13, matrix products: 27.8 us -> 12 us  [the longest x11 6.75 us: dot32(): return jnp.dot(left, right, precision=HIGH, preferred_element_type=F32)]
    another operation x1 -> x7, local copies, waits for them, and re-layouts: 0.01 us -> 13.6 us  [the longest x2 6.2 us: spread(): return jnp.stack(shifted, axis=3).reshape(count, 9 * own)]
  transfers between devices with their start and end apart: 9 -> 19, of which waited for: 8 -> 12; matrix products, arithmetic and copies ran while one was open for 2% -> 4% of each run, Pallas kernels for 0% -> 0%
where the time goes in v1:
time: 250 us; the launch traced here: 249 us
  waiting for transfers between devices  82.5 us (33%)
  local copies, waits for them, and re-layouts  56.6 us (23%)
  blocking collectives  38.9 us (16%)
  between operations  22.8 us (9%)
  starting transfers between devices  20.6 us (8%)
  matrix products  12 us (5%)
  other arithmetic  8.11 us (3%)
  loops' own time  7.73 us (3%)
    all_gather x1, blocking collectives, local(): codes = lax.all_gather(code_index[0, :, :, 0], 'sp', axis=0)  38.9 us
    ppermute x1, waiting for transfers between devices, local(): received = lax.ppermute(total, 'sec', [(1, 0)])  34 us
    ppermute x6, waiting for transfers between devices, swap_sum(): lax.ppermute(values, axis, [(i, i ^ bit) for i in range(count)])  22.4 us
    ppermute x4, waiting for transfers between devices, ring_gather(): down = lax.ppermute(down, axis, forward)  13.4 us
    slice x1, local copies, waits for them, and re-layouts, conv_sum(): rows = sum((move(taps[:, :, :, i, j], 0, 1 - i) for i in range(3)))  11.7 us
    all_to_all x1, waiting for transfers between devices, local(): big = lax.all_to_all(big, 'sp', 0, 0, tiled=True)  11.5 us
    reshape x1, local copies, waits for them, and re-layouts, conv_sum(): taps = taps.reshape(grid + (3, 3, own))  8.96 us
    another operation x1, loops' own time, local(): pre, inner_dec, part = lax.cond(decoder, decoder_first, encoder_first)  7.51 us
  transfers between devices with their start and end apart: 19, of which 12 were waited for; matrix products, arithmetic and copies ran while one was open for 4% of the time, Pallas kernels for 0%

profile of v1, /device:TPU:0, one launch (start us, length us, event | category | flops | bytes accessed | tf_op | source)
XLA Modules:
  0.0 249.3 jit_solution(928997282834642380)
XLA Ops:
  0.6 3.1 %collective-permute-start = (bf16[160,512]{1,0:T(8,128)(2,1)}, bf16[160,512]{1,0:T(8,128)(2,1)S(1)}, u32[]{:S(2)}, u32[]{:S(2)}) collective-permute-start(bf16[160,512]{1,0:T(8,128)(2,1)} %bitcast.334), channel_id=1, source_target_pairs={{0,4},{4,8},{8,12},{12,14},{14,10},{10,6},{6,2},{2,0},{1,5},{5,9},... | collective-permute-start | bytes 491528 | tf_op jit(solution)/shard_map/ppermute | solution.py:33
  8.2 6.3 %all-to-all-start = ((bf16[8,64,576]{2,1,0:T(8,128)(2,1)}), bf16[8,64,576]{2,1,0:T(8,128)(2,1)S(1)}, u32[]{:S(2)}, u32[]{:S(2)}) async-start(bf16[8,64,576]{2,1,0:T(8,128)(2,1)} %copy.182), calls=%async_computation | async-start | bytes 1310720 | tf_op jit(solution)/shard_map/all_to_all | solution.py:83
  14.5 38.9 %all-gather = s32[8,6,5,1,32]{4,3,2,1,0:T(1,128)S(1)} all-gather(s32[1,6,5,1,32]{4,3,2,1,0:T(1,128)S(1)} %copy-done.11), channel_id=2, replica_groups=mesh['sec'=2,'sp'=8,'dp'=2] {'sp'}, dimensions={0}, use_global_device_ids=true | all-gather | bytes 34560 | tf_op jit(solution)/shard_map/all_gather | solution.py:84
  79.0 4.9 %collective-permute-done.2 = bf16[160,512]{1,0:T(8,128)(2,1)S(1)} collective-permute-done((bf16[160,512]{1,0:T(8,128)(2,1)S(1)}, bf16[160,512]{1,0:T(8,128)(2,1)S(1)}, u32[]{:S(2)}, u32[]{:S(2)}) %collective-permute-start.2) | collective-permute-done | bytes 163872 | tf_op jit(solution)/shard_map/ppermute | solution.py:33
  85.9 3.2 %collective-permute-done.4 = bf16[160,512]{1,0:T(8,128)(2,1)S(1)} collective-permute-done((bf16[160,512]{1,0:T(8,128)(2,1)S(1)}, bf16[160,512]{1,0:T(8,128)(2,1)S(1)}, u32[]{:S(2)}, u32[]{:S(2)}) %collective-permute-start.4) | collective-permute-done | bytes 163872 | tf_op jit(solution)/shard_map/ppermute | solution.py:33
  89.2 5.3 %collective-permute-done.6 = bf16[160,512]{1,0:T(8,128)(2,1)S(1)} collective-permute-done((bf16[160,512]{1,0:T(8,128)(2,1)S(1)}, bf16[160,512]{1,0:T(8,128)(2,1)S(1)}, u32[]{:S(2)}, u32[]{:S(2)}) %collective-permute-start.6) | collective-permute-done | bytes 163872 | tf_op jit(solution)/shard_map/ppermute | solution.py:33
  94.6 34.0 %conditional.2 = (bf16[1280,64]{0,1:T(8,128)(2,1)S(1)}, f32[6,1280]{1,0:T(8,128)S(1)}, f32[8,5,32,64]{3,2,1,0:T(8,128)S(1)}) conditional(s32[]{:T(128)} %convert_element_type.69, (bf16[1,3,64,512]{3,2,1,0:T(8,128)(2,1)S(1)}, f32[6,512]{1,0:T(8,128)S(1)}, bf16[1280,512]{1,0:T(8,128)(2,1)S(1)}, bf16[512,576]{1,0:T(8,128)(2,1)S(1)}) %tuple.94, ...), branch_computations={%region_0.1_spmd, %region_1.2_spmd} | conditional | flops 780909568 | bytes 53002888 | solution.py:128
  94.6 2.9 %fusion.97 = f32[1280,576]{1,0:T(8,128)} fusion(bf16[1280,512]{1,0:T(8,128)(2,1)S(1)} %get-tuple-element.75, bf16[512,576]{1,0:T(8,128)(2,1)S(1)} %get-tuple-element.76), kind=kOutput, calls=%fused_computation.184 | convolution fusion | flops 754974720 | bytes 4849664 | tf_op jit(solution)/shard_map/cond/branch_0_fun/dot_general | solution.py:60
  97.5 9.0 %reshape.137 = f32[8,5,32,3,3,64]{5,4,3,2,1,0:T(4,128)} reshape(f32[1280,576]{1,0:T(8,128)} %fusion.97) | data formatting | bytes 5898240 | tf_op jit(solution)/shard_map/cond/branch_0_fun/reshape | solution.py:95
  106.5 11.7 %fusion.84 = (f32[8,5,32,1,1,64]{5,4,3,2,1,0:T(1,128)S(1)}, f32[8,5,32,1,1,64]{5,4,3,2,1,0:T(1,128)S(1)}, f32[8,5,32,1,1,64]{5,4,3,2,1,0:T(1,128)S(1)}, f32[8,5,...) fusion(f32[8,5,32,3,3,64]{5,4,3,2,1,0:T(4,128)} %reshape.137), kind=kLoop, calls=%fused_computation.171 | loop fusion | bytes 5898240 | tf_op jit(solution)/shard_map/cond/branch_0_fun/slice | solution.py:98
  128.8 3.8 %collective-permute-done.7 = f32[6,1280]{1,0:T(8,128)S(1)} collective-permute-done((f32[6,1280]{1,0:T(8,128)S(1)}, f32[6,1280]{1,0:T(8,128)S(1)}, u32[]{:S(2)}, u32[]{:S(2)}) %collective-permute-start.7) | collective-permute-done | bytes 30752 | tf_op jit(solution)/shard_map/ppermute | solution.py:45
  132.8 3.8 %collective-permute-done.8 = f32[6,1280]{1,0:T(8,128)S(1)} collective-permute-done((f32[6,1280]{1,0:T(8,128)S(1)}, f32[6,1280]{1,0:T(8,128)S(1)}, u32[]{:S(2)}, u32[]{:S(2)}) %collective-permute-start.8) | collective-permute-done | bytes 30752 | tf_op jit(solution)/shard_map/ppermute | solution.py:45
  136.8 4.8 %collective-permute-done.9 = f32[6,1280]{1,0:T(8,128)S(1)} collective-permute-done((f32[6,1280]{1,0:T(8,128)S(1)}, f32[6,1280]{1,0:T(8,128)S(1)}, u32[]{:S(2)}, u32[]{:S(2)}) %collective-permute-start.9) | collective-permute-done | bytes 30752 | tf_op jit(solution)/shard_map/ppermute | solution.py:45
  146.6 34.0 %collective-permute-done.10 = f32[1280,6]{0,1:T(8,128)} collective-permute-done((f32[1280,6]{0,1:T(8,128)}, f32[1280,6]{0,1:T(8,128)}, u32[]{:S(2)}, u32[]{:S(2)}) %collective-permute-start.10) | collective-permute-done | bytes 30752 | tf_op jit(solution)/shard_map/ppermute | solution.py:130
  180.7 30.6 %conditional.3 = (f32[192,512]{1,0:T(8,128)S(1)}, f32[6,512]{1,0:T(8,128)S(1)}, f32[512,576]{1,0:T(8,128)}) conditional(s32[]{:T(128)} %convert_element_type.69, (f32[1280,6]{0,1:T(8,128)}, f32[1280,6]{0,1:T(8,128)}, bf16[1,3,64,512]{3,2,1,0:T(8,128)(2,1)}, f32[6,512]{1,0:T(8,128)S(1)}, f32[8,5,32,64]{3,2,1,0:T(8,128)S(1)}, ...), branch_computations={%region_2.3_spmd, %region_3.4_spmd} | conditional | flops 818423296 | bytes 27480678 | solution.py:158
  192.6 6.1 %copy.179 = bf16[8,5,32,9,64]{4,3,2,1,0:T(8,128)(2,1)} copy(bf16[8,5,32,9,64]{4,2,1,0,3:T(8,128)(2,1)S(1)} %fusion.58) | data formatting | bytes 2949120 | tf_op jit(solution)/shard_map/cond/branch_0_fun/stack | solution.py:105
  198.6 7.0 %reshape.148 = bf16[1280,576]{1,0:T(8,128)(2,1)} reshape(bf16[8,5,32,9,64]{4,3,2,1,0:T(8,128)(2,1)} %copy.179) | data formatting | bytes 2949120 | tf_op jit(solution)/shard_map/cond/branch_0_fun/reshape | solution.py:105
  205.7 2.4 convolution_bitcast_fusion.1
  213.6 3.5 %all-to-all-start.1 = ((bf16[8,64,576]{2,1,0:T(8,128)(2,1)}), bf16[8,64,576]{2,1,0:T(8,128)(2,1)S(1)}, u32[]{:S(2)}, u32[]{:S(2)}) async-start(bf16[8,64,576]{2,1,0:T(8,128)(2,1)} %bitcast.99), calls=%async_computation.1 | async-start | bytes 1310720 | tf_op jit(solution)/shard_map/all_to_all | solution.py:160
  217.2 11.5 %all-to-all-done.1 = bf16[8,64,576]{2,1,0:T(8,128)(2,1)S(1)} async-done(((bf16[8,64,576]{2,1,0:T(8,128)(2,1)}), bf16[8,64,576]{2,1,0:T(8,128)(2,1)S(1)}, u32[]{:S(2)}, u32[]{:S(2)}) %all-to-all-start.1) | async-done | bytes 589856 | tf_op jit(solution)/shard_map/all_to_all | solution.py:160
  230.6 2.3 collective-permute-done.13
  232.9 3.7 %collective-permute-done.14 = f32[6,512]{1,0:T(8,128)S(1)} collective-permute-done((f32[6,512]{1,0:T(8,128)S(1)}, f32[6,512]{1,0:T(8,128)S(1)}, u32[]{:S(2)}, u32[]{:S(2)}) %collective-permute-start.14) | collective-permute-done | bytes 12320 | tf_op jit(solution)/shard_map/ppermute | solution.py:45
  237.2 4.0 %collective-permute-done.15 = f32[6,512]{1,0:T(8,128)S(1)} collective-permute-done((f32[6,512]{1,0:T(8,128)S(1)}, f32[6,512]{1,0:T(8,128)S(1)}, u32[]{:S(2)}, u32[]{:S(2)}) %collective-permute-start.15) | collective-permute-done | bytes 12320 | tf_op jit(solution)/shard_map/ppermute | solution.py:45
  246.6 2.8 %broadcast_in_dim_reshape.3 = f32[1,9,64,512]{3,2,1,0:T(8,128)} reshape(f32[9,64,8,64]{3,2,1,0:T(8,128)} %copy.192) | data formatting | bytes 2359296 | tf_op jit(solution)/shard_map/broadcast_in_dim;reshape | solution.py:170
  (116 shorter events, 43.9 us)
Async XLA Ops:
  0.6 76.2 %collective-permute-start = (bf16[160,512]{1,0:T(8,128)(2,1)}, bf16[160,512]{1,0:T(8,128)(2,1)S(1)}, u32[]{:S(2)}, u32[]{:S(2)}) collective-permute-start(bf16[160,512]{1,0:T(8,128)(2,1)} %bitcast.334), channel_id=1, source_target_pairs={{0,4},{4,8},{8,12},{12,14},{14,10},{10,6},{6,2},{2,0},{1,5},{5,9},... | collective-permute-start | bytes 491528 | tf_op jit(solution)/shard_map/ppermute | solution.py:33
  3.7 73.2 %collective-permute-start.1 = (bf16[160,512]{1,0:T(8,128)(2,1)}, bf16[160,512]{1,0:T(8,128)(2,1)S(1)}, u32[]{:S(2)}, u32[]{:S(2)}) collective-permute-start(bf16[160,512]{1,0:T(8,128)(2,1)} %bitcast.335), channel_id=1, source_target_pairs={{4,0},{8,4},{12,8},{14,12},{10,14},{6,10},{2,6},{0,2},{5,1},{9,5},... | collective-permute-start | bytes 491528 | tf_op jit(solution)/shard_map/ppermute | solution.py:36
  5.5 48.0 %copy-start.8 = (bf16[6,512]{1,0:T(8,128)(2,1)S(1)}, bf16[6,512]{1,0:T(8,128)(2,1)}, u32[]{:S(2)}) copy-start(bf16[6,512]{1,0:T(8,128)(2,1)} %param.19) | copy-start | bytes 18436
  5.5 48.0 %copy-start.13 = (s32[8]{0:T(128)S(1)}, s32[8]{0:T(128)}, u32[]{:S(2)}) copy-start(s32[8]{0:T(128)} %constant.156.clone) | copy-start | bytes 100
  5.5 55.2 %copy-start.10 = (s32[8]{0:T(128)S(1)}, s32[8]{0:T(128)}, u32[]{:S(2)}) copy-start(s32[8]{0:T(128)} %constant.157.clone) | copy-start | bytes 100
  6.9 69.9 %copy-start.7 = (bf16[1,1,5,1,32,512]{5,4,3,2,1,0:T(8,128)(2,1)S(1)}, bf16[1,1,5,1,32,512]{5,4,3,2,1,0:T(8,128)(2,1)}, u32[]{:S(2)}) copy-start(bf16[1,1,5,1,32,512]{5,4,3,2,1,0:T(8,128)(2,1)} %param.13) | copy-start | bytes 491524
  8.2 86.4 %all-to-all-start = ((bf16[8,64,576]{2,1,0:T(8,128)(2,1)}), bf16[8,64,576]{2,1,0:T(8,128)(2,1)S(1)}, u32[]{:S(2)}, u32[]{:S(2)}) async-start(bf16[8,64,576]{2,1,0:T(8,128)(2,1)} %copy.182), calls=%async_computation | async-start | bytes 1310720 | tf_op jit(solution)/shard_map/all_to_all | solution.py:83
  14.4 80.1 %copy-start.2 = (bf16[1,3,64,512]{3,2,1,0:T(8,128)(2,1)S(1)}, bf16[1,3,64,512]{3,2,1,0:T(8,128)(2,1)}, u32[]{:S(2)}) copy-start(bf16[1,3,64,512]{3,2,1,0:T(8,128)(2,1)} %param.17) | copy-start | bytes 589828
  76.8 7.0 %collective-permute-start.2 = (bf16[160,512]{1,0:T(8,128)(2,1)S(1)}, bf16[160,512]{1,0:T(8,128)(2,1)S(1)}, u32[]{:S(2)}, u32[]{:S(2)}) collective-permute-start(bf16[160,512]{1,0:T(8,128)(2,1)S(1)} %collective-permute-done), channel_id=1, source_target_pairs={{0,4},{4,8},{8,12},{12,14},{14,10},{10,6},{6,2},{2,0},{1,5},{5,9},... | collective-permute-start | bytes 491528 | tf_op jit(solution)/shard_map/ppermute | solution.py:33
  76.9 6.9 %collective-permute-start.3 = (bf16[160,512]{1,0:T(8,128)(2,1)S(1)}, bf16[160,512]{1,0:T(8,128)(2,1)S(1)}, u32[]{:S(2)}, u32[]{:S(2)}) collective-permute-start(bf16[160,512]{1,0:T(8,128)(2,1)S(1)} %collective-permute-done.1), channel_id=1, source_target_pairs={{4,0},{8,4},{12,8},{14,12},{10,14},{6,10},{2,6},{0,2},{5,1},{9,5},... | collective-permute-start | bytes 491528 | tf_op jit(solution)/shard_map/ppermute | solution.py:36
  83.9 5.3 %collective-permute-start.4 = (bf16[160,512]{1,0:T(8,128)(2,1)S(1)}, bf16[160,512]{1,0:T(8,128)(2,1)S(1)}, u32[]{:S(2)}, u32[]{:S(2)}) collective-permute-start(bf16[160,512]{1,0:T(8,128)(2,1)S(1)} %collective-permute-done.2), channel_id=1, source_target_pairs={{0,4},{4,8},{8,12},{12,14},{14,10},{10,6},{6,2},{2,0},{1,5},{5,9},... | collective-permute-start | bytes 491528 | tf_op jit(solution)/shard_map/ppermute | solution.py:33
  83.9 5.3 %collective-permute-start.5 = (bf16[160,512]{1,0:T(8,128)(2,1)S(1)}, bf16[160,512]{1,0:T(8,128)(2,1)S(1)}, u32[]{:S(2)}, u32[]{:S(2)}) collective-permute-start(bf16[160,512]{1,0:T(8,128)(2,1)S(1)} %collective-permute-done.3), channel_id=1, source_target_pairs={{4,0},{8,4},{12,8},{14,12},{10,14},{6,10},{2,6},{0,2},{5,1},{9,5},... | collective-permute-start | bytes 491528 | tf_op jit(solution)/shard_map/ppermute | solution.py:36
  89.2 5.3 %collective-permute-start.6 = (bf16[160,512]{1,0:T(8,128)(2,1)S(1)}, bf16[160,512]{1,0:T(8,128)(2,1)S(1)}, u32[]{:S(2)}, u32[]{:S(2)}) collective-permute-start(bf16[160,512]{1,0:T(8,128)(2,1)S(1)} %collective-permute-done.4), channel_id=1, source_target_pairs={{0,4},{4,8},{8,12},{12,14},{14,10},{10,6},{6,2},{2,0},{1,5},{5,9},... | collective-permute-start | bytes 491528 | tf_op jit(solution)/shard_map/ppermute | solution.py:33
  128.6 4.1 %collective-permute-start.7 = (f32[6,1280]{1,0:T(8,128)S(1)}, f32[6,1280]{1,0:T(8,128)S(1)}, u32[]{:S(2)}, u32[]{:S(2)}) collective-permute-start(f32[6,1280]{1,0:T(8,128)S(1)} %get-tuple-element.108), channel_id=1, source_target_pairs={{0,2},{2,0},{4,6},{6,4},{8,10},{10,8},{12,14},{14,12},{1,3},{3,1},... | collective-permute-start | bytes 92168 | tf_op jit(solution)/shard_map/ppermute | solution.py:45
  132.6 4.0 %collective-permute-start.8 = (f32[6,1280]{1,0:T(8,128)S(1)}, f32[6,1280]{1,0:T(8,128)S(1)}, u32[]{:S(2)}, u32[]{:S(2)}) collective-permute-start(f32[6,1280]{1,0:T(8,128)S(1)} %add.416), channel_id=1, source_target_pairs={{0,4},{2,6},{4,0},{6,2},{8,12},{10,14},{12,8},{14,10},{1,5},{3,7},... | collective-permute-start | bytes 92168 | tf_op jit(solution)/shard_map/ppermute | solution.py:45
  136.7 4.9 %collective-permute-start.9 = (f32[6,1280]{1,0:T(8,128)S(1)}, f32[6,1280]{1,0:T(8,128)S(1)}, u32[]{:S(2)}, u32[]{:S(2)}) collective-permute-start(f32[6,1280]{1,0:T(8,128)S(1)} %add.417), channel_id=1, source_target_pairs={{0,8},{2,10},{4,12},{6,14},{8,0},{10,2},{12,4},{14,6},{1,9},{3,11}... | collective-permute-start | bytes 92168 | tf_op jit(solution)/shard_map/ppermute | solution.py:45
  142.6 38.1 %collective-permute-start.10 = (f32[1280,6]{0,1:T(8,128)}, f32[1280,6]{0,1:T(8,128)}, u32[]{:S(2)}, u32[]{:S(2)}) collective-permute-start(f32[1280,6]{0,1:T(8,128)} %convolution_add_fusion.5), channel_id=1, source_target_pairs={{16,0},{17,1},{18,2},{19,3},{20,4},{21,5},{22,6},{23,7},{24,8},{25... | collective-permute-start | bytes 92168 | tf_op jit(solution)/shard_map/ppermute | solution.py:130
  213.6 15.2 %all-to-all-start.1 = ((bf16[8,64,576]{2,1,0:T(8,128)(2,1)}), bf16[8,64,576]{2,1,0:T(8,128)(2,1)S(1)}, u32[]{:S(2)}, u32[]{:S(2)}) async-start(bf16[8,64,576]{2,1,0:T(8,128)(2,1)} %bitcast.99), calls=%async_computation.1 | async-start | bytes 1310720 | tf_op jit(solution)/shard_map/all_to_all | solution.py:160
  217.2 25.9 %collective-permute-start.12 = (f32[192,512]{1,0:T(8,128)S(1)}, f32[192,512]{1,0:T(8,128)S(1)}, u32[]{:S(2)}, u32[]{:S(2)}) collective-permute-start(f32[192,512]{1,0:T(8,128)S(1)} %broadcast_multiply_fusion), channel_id=1, source_target_pairs={{0,1},{1,0},{2,3},{3,2},{4,5},{5,4},{6,7},{7,6},{8,9},{9,8},{10,11... | collective-permute-start | bytes 1179656 | tf_op jit(solution)/shard_map/ppermute | solution.py:167
  229.0 14.9 %collective-permute-start.11 = (bf16[512,576]{0,1:T(8,128)(2,1)S(1)}, bf16[512,576]{0,1:T(8,128)(2,1)S(1)}, u32[]{:S(2)}, u32[]{:S(2)}) collective-permute-start(bf16[512,576]{0,1:T(8,128)(2,1)S(1)} %copy.190), channel_id=1, source_target_pairs={{0,1},{1,0},{2,3},{3,2},{4,5},{5,4},{6,7},{7,6},{8,9},{9,8},{10,11... | collective-permute-start | bytes 1769480 | tf_op jit(solution)/shard_map/ppermute | solution.py:164
  229.0 3.8 %collective-permute-start.13 = (f32[6,512]{1,0:T(8,128)S(1)}, f32[6,512]{1,0:T(8,128)S(1)}, u32[]{:S(2)}, u32[]{:S(2)}) collective-permute-start(f32[6,512]{1,0:T(8,128)S(1)} %broadcast_multiply_fusion.1), channel_id=1, source_target_pairs={{0,2},{2,0},{4,6},{6,4},{8,10},{10,8},{12,14},{14,12},{1,3},{3,1},... | collective-permute-start | bytes 36872 | tf_op jit(solution)/shard_map/ppermute | solution.py:45
  232.9 3.7 %collective-permute-start.14 = (f32[6,512]{1,0:T(8,128)S(1)}, f32[6,512]{1,0:T(8,128)S(1)}, u32[]{:S(2)}, u32[]{:S(2)}) collective-permute-start(f32[6,512]{1,0:T(8,128)S(1)} %fusion.78), channel_id=1, source_target_pairs={{0,4},{2,6},{4,0},{6,2},{8,12},{10,14},{12,8},{14,10},{1,5},{3,7},... | collective-permute-start | bytes 36872 | tf_op jit(solution)/shard_map/ppermute | solution.py:45
  236.6 4.6 %collective-permute-start.15 = (f32[6,512]{1,0:T(8,128)S(1)}, f32[6,512]{1,0:T(8,128)S(1)}, u32[]{:S(2)}, u32[]{:S(2)}) collective-permute-start(f32[6,512]{1,0:T(8,128)S(1)} %add.426), channel_id=1, source_target_pairs={{0,8},{2,10},{4,12},{6,14},{8,0},{10,2},{12,4},{14,6},{1,9},{3,11}... | collective-permute-start | bytes 36872 | tf_op jit(solution)/shard_map/ppermute | solution.py:45
  241.2 1.2 collective-permute-start.16
  (5 other events, 122.3 us)

commit v2 on v1

v2 whole, which is shorter than its diff:
```python
import functools

import jax
import jax.numpy as jnp
from jax import lax
from jax.experimental import pallas as pl
from jax.experimental.pallas import tpu as pltpu
from jax.sharding import PartitionSpec as P

F32 = jnp.float32
BF16 = jnp.bfloat16
LANES = 128
NN = (((1,), (0,)), ((), ()))
NT = (((1,), (1,)), ((), ()))
TN = (((0,), (0,)), ((), ()))
VMEM_BYTES = 56 * 1024 * 1024


def up_to(value, multiple):
    return -(-value // multiple) * multiple


def ring_place(index, count):
    return jnp.where(index % 2 == 0, index // 2, count - (index + 1) // 2)


def ring_device(place, count):
    place = lax.rem(place + 2 * count, count)
    return jnp.where(place < count // 2, 2 * place, 2 * (count - place) - 1)


def ring_gather(shard, axis):
    count = lax.axis_size(axis)
    order = list(range(0, count, 2)) + list(range(count - 1, 0, -2))
    forward = [(order[i], order[(i + 1) % count]) for i in range(count)]
    backward = [(target, source) for source, target in forward]
    blocks, steps = [shard], [0]
    down = up = shard
    for step in range(1, count // 2 + 1):
        down = lax.ppermute(down, axis, forward)
        blocks.append(down)
        steps.append(-step)
        if step < count - step:
            up = lax.ppermute(up, axis, backward)
            blocks.append(up)
            steps.append(step)
    return blocks, steps


def swap_sum(values, axis):
    count = lax.axis_size(axis)
    bit = 1
    while bit < count:
        values = values + lax.ppermute(values, axis, [(i, i ^ bit) for i in range(count)])
        bit *= 2
    return values


def dot(left, right, dims):
    return lax.dot_general(left, right, dims, preferred_element_type=F32)


def thirds(values):
    high = values.astype(BF16).astype(F32)
    rest = values - high
    middle = rest.astype(BF16).astype(F32)
    return high, middle, rest - middle


def stack3(values):
    return jnp.concatenate(thirds(values), axis=0).astype(BF16)


def sum3(stacked):
    rows = stacked.shape[0] // 3
    return stacked[:rows] + stacked[rows : 2 * rows] + stacked[2 * rows :]


def lanes_down(values, by):
    by = by % LANES
    return values if by == 0 else pltpu.roll(values, LANES - by, 1)


def spots(parts, own):
    return [((p * own) // LANES, (p * own) % LANES) for p in range(parts)]


def col_move(values, by, cols):
    if by == 0:
        return values
    rows = values.shape[0]
    col = lax.broadcasted_iota(jnp.int32, values.shape, 0) % cols
    edge = 0 if by > 0 else cols - 1
    return jnp.where(col == edge, 0.0, pltpu.roll(values, by % rows, 0))


def frames_move(values, by, cols):
    if by == 0:
        return values
    zeros = jnp.zeros((abs(by) * cols, values.shape[1]), values.dtype)
    if by > 0:
        return jnp.concatenate([zeros, values[: -by * cols]], axis=0)
    return jnp.concatenate([values[-by * cols :], zeros], axis=0)


def merge(pieces, own):
    blocks = [None] * (spots(len(pieces), own)[-1][0] + 1)
    for piece, (block, offset) in zip(pieces, spots(len(pieces), own)):
        moved = lanes_down(piece, -offset)
        blocks[block] = moved if blocks[block] is None else blocks[block] + moved
    return blocks


class Sizes:
    def __init__(self, sp, frames, cols, chans, own, lat):
        self.sp, self.frames, self.cols = sp, frames, cols
        self.chans, self.own, self.lat = chans, own, lat
        self.row = frames * cols
        self.count = sp * self.row
        self.wide = up_to(9 * own, LANES)
        self.thin = up_to(3 * own, LANES)


def load_rows(z, steps, chunks, v, codes, sems):
    place = ring_place(lax.axis_index("sp"), z.sp)
    started = []
    for k, (chunk, step) in enumerate(zip(chunks, steps)):
        row = ring_device(place + step, z.sp)
        copy = pltpu.make_async_copy(
            chunk.at[pl.ds(0, z.row)],
            v.at[pl.ds(pl.multiple_of(row * z.row, z.row), z.row)],
            sems.at[0, k],
        )
        copy.start()
        started.append(copy)
        copy = pltpu.make_async_copy(chunk.at[pl.ds(z.row, 16)], codes.at[row], sems.at[1, k])
        copy.start()
        started.append(copy)
    return started


def rows_at(r, z):
    return pl.ds(pl.multiple_of(r * z.row, z.row), z.row)


def conv_row(z, taps, r):
    total = None
    for j in range(3):
        by_offset = {}
        for i in range(3):
            block, offset = spots(9, z.own)[3 * i + j]
            value = taps[r + i, :, block * LANES : (block + 1) * LANES]
            by_offset[offset] = by_offset.get(offset, 0.0) + value
        column = sum(lanes_down(value, offset) for offset, value in by_offset.items())
        column = col_move(column, 1 - j, z.cols)
        total = column if total is None else total + column
    return total


def later_row(z, taps, r):
    total = None
    for k, (block, offset) in enumerate(spots(3, z.own)):
        value = taps[rows_at(r, z), block * LANES : (block + 1) * LANES]
        value = frames_move(lanes_down(value, offset), -k, z.cols)
        total = value if total is None else total + value
    return total


def keep_own(z, values):
    lane = lax.broadcasted_iota(jnp.int32, values.shape, 1)
    return jnp.where(lane < z.own, values, 0.0)


def put_shifts(z, inner, shifts, r):
    for j in range(3):
        shifts[j, r + 1] = col_move(inner, j - 1, z.cols).astype(BF16)


def spread(z, shifts, inner_cat):
    def body(r, carry):
        pieces = [
            shifts[j, r + 2 - i].astype(F32) for i in range(3) for j in range(3)
        ]
        for b, block in enumerate(merge(pieces, z.own)):
            inner_cat[rows_at(r, z), b * LANES : (b + 1) * LANES] = block.astype(BF16)
        return carry

    lax.fori_loop(0, z.sp, body, 0)


def zero_ends(z, padded):
    padded[0] = jnp.zeros(padded.shape[1:], padded.dtype)
    padded[z.sp + 1] = jnp.zeros(padded.shape[1:], padded.dtype)


def in_blocks(z, action):
    step = 8 if z.sp % 8 == 0 else 1
    if z.sp == step:
        action(0, step)
    else:

        def body(b, carry):
            action(b * step, step)
            return carry

        lax.fori_loop(0, z.sp // step, body, 0)


def position_codes(z, codes, out):
    def body(r, carry):
        block = codes[r].astype(F32)[:, : up_to(z.row, LANES)]
        block = jnp.concatenate([block] * 3 + [jnp.zeros((LANES - 48, block.shape[1]), F32)], 0)
        out[rows_at(r, z)] = block.T[: z.row].astype(BF16)
        return carry

    lax.fori_loop(0, z.sp, body, 0)


def first_kernel(z, steps, *refs):
    n = len(steps)
    chunks, (w_cat, wt, proj, halves) = refs[:n], refs[n : n + 4]
    part, hid_cat, slope, inner_out = refs[n + 4 : n + 8]
    v, codes, taps, shifts, inner_cat, pos, thin, sems = refs[n + 8 :]
    started = load_rows(z, steps, chunks, v, codes, sems)
    decoder = lax.axis_index("sec") == 1
    first = lax.axis_index("sp") == 0
    zero_ends(z, taps)
    for copy in started:
        copy.wait()
    whole = dot(proj[...], v[...], NT)[:8]

    def store_hidden(pre, logistic, r):
        hidden = keep_own(z, (pre * logistic).astype(BF16).astype(F32))
        moved = [frames_move(hidden, k, z.cols) for k in range(3)]
        for b, block in enumerate(merge(moved, z.own)):
            hid_cat[rows_at(r, z), b * LANES : (b + 1) * LANES] = block.astype(BF16)

    def finish(weights, cat):
        stacked = jnp.concatenate([weights[:8]] * 1, axis=0)
        partial = sum3(dot(stack3(stacked), cat, NT))
        part[...] = partial + jnp.where(first, whole, 0.0)

    @pl.when(decoder)
    def _():
        for j in range(3):
            zero_ends(z, shifts.at[j])
        p_cat = dot(proj[...], w_cat[...], NN)
        half = halves[:, :1]
        row = lax.broadcasted_iota(jnp.int32, p_cat.shape, 0)
        scaled = jnp.where(
            row == z.lat, -jnp.sum(p_cat, axis=0, keepdims=True), p_cat / half
        )
        table = jnp.concatenate(
            list(thirds(scaled)) + [jnp.zeros((LANES - 48, z.wide), F32)], axis=0
        ).astype(BF16)
        position_codes(z, codes, pos)

        def block(r0, rows):
            place = pl.ds(pl.multiple_of(r0 * z.row, rows * z.row), rows * z.row)
            taps[pl.ds(r0 + 1, rows)] = dot(pos[place], table, NN).reshape(rows, z.row, z.wide)
            thin[place] = dot(v[place], wt[...], NT)

        in_blocks(z, block)

        def body(r, carry):
            pre = conv_row(z, taps, r)
            logistic = 1.0 / (1.0 + jnp.exp(-pre))
            store_hidden(pre, logistic, r)
            rate = logistic * (1.0 + pre * (1.0 - logistic))
            inner = keep_own(z, (later_row(z, thin, r) * rate).astype(BF16).astype(F32))
            put_shifts(z, inner, shifts, r)
            inner_out[r] = inner.astype(BF16)
            return carry

        lax.fori_loop(0, z.sp, body, 0)
        spread(z, shifts, inner_cat)
        finish(p_cat, inner_cat[...])

    @pl.when(jnp.logical_not(decoder))
    def _():
        def block(r0, rows):
            place = pl.ds(pl.multiple_of(r0 * z.row, rows * z.row), rows * z.row)
            taps[pl.ds(r0 + 1, rows)] = dot(v[place], w_cat[...], NN).reshape(
                rows, z.row, z.wide
            )

        in_blocks(z, block)

        def body(r, carry):
            pre = conv_row(z, taps, r)
            logistic = 1.0 / (1.0 + jnp.exp(-pre))
            store_hidden(pre, logistic, r)
            slope[r] = logistic * (1.0 + pre * (1.0 - logistic))
            return carry

        lax.fori_loop(0, z.sp, body, 0)
        finish(dot(proj[...], wt[...], NT), hid_cat[...])


def second_kernel(z, steps, scale, *refs):
    n = len(steps)
    chunks = refs[:n]
    w_cat, wt, proj, halves, hid_cat, slope, inner_in, total, received = refs[n : n + 9]
    big, time, part = refs[n + 9 : n + 12]
    v, codes, shifts, inner_cat, pos, thin, sems = refs[n + 12 :]
    started = load_rows(z, steps, chunks, v, codes, sems)
    decoder = lax.axis_index("sec") == 1
    first = lax.axis_index("sp") == 0
    for j in range(3):
        zero_ends(z, shifts.at[j])
    for copy in started:
        copy.wait()

    @pl.when(decoder)
    def _():
        position_codes(z, codes, pos)

        def body(r, carry):
            put_shifts(z, inner_in[r].astype(F32), shifts, r)
            return carry

        lax.fori_loop(0, z.sp, body, 0)
        spread(z, shifts, inner_cat)
        half = halves[:8, :1]

        def latent_rows(raw):
            row = lax.broadcasted_iota(jnp.int32, raw.shape, 0)
            return jnp.where(row < z.lat, raw / half - raw[z.lat : z.lat + 1], 0.0)

        short = latent_rows(dot(pos[...], inner_cat[...], TN)[:8])
        proj8 = proj[:8].astype(F32)
        proj24 = jnp.concatenate([proj8] * 3, axis=0).astype(BF16)
        big[...] = (dot(proj24, stack3(short), TN) * scale).astype(BF16)
        time[...] = dot(hid_cat[...], v[...], TN)[: 3 * z.own] * scale
        whole = latent_rows(dot(pos[...], v[...], TN)[:8])
        partial = sum3(dot(stack3(short), w_cat[...], NT))
        part[...] = (partial + jnp.where(first, whole, 0.0)) * scale

    @pl.when(jnp.logical_not(decoder))
    def _():
        bounded = jnp.tanh(total[...])
        grad = received[...] * (1.0 - bounded * bounded)
        back = dot(proj[...], wt[...], NT)[:8]
        gh, gm, gl = thirds(grad)
        bh, bm, bl = thirds(back)
        left = jnp.concatenate([gh, gh, gm, gh, gl, gm], axis=0).astype(BF16)
        right = jnp.concatenate([bh, bm, bh, bl, bh, bm], axis=0).astype(BF16)
        thin[...] = dot(left, right, TN)

        def body(r, carry):
            inner = keep_own(z, later_row(z, thin, r) * slope[r])
            put_shifts(z, inner, shifts, r)
            return carry

        lax.fori_loop(0, z.sp, body, 0)
        spread(z, shifts, inner_cat)
        big[...] = (dot(v[...], inner_cat[...], TN) * scale).astype(BF16)
        grad3 = jnp.concatenate([gh, gm, gl], axis=0).astype(BF16)
        short = sum3(dot(grad3, hid_cat[...], NN))
        short3 = stack3(short)
        proj8 = proj[:8].astype(F32)
        proj24 = jnp.concatenate([proj8] * 3, axis=0).astype(BF16)
        time[...] = dot(short3, proj24, TN)[: 3 * z.own] * scale
        whole = sum3(dot(grad3, v[...], NN))
        partial = sum3(dot(short3, wt[...], NN))
        part[...] = (partial + jnp.where(first, whole, 0.0)) * scale


def last_kernel(z, mine, other, time_mine, time_other, space, time):
    time[...] = time_mine[...] + time_other[...]
    per = LANES // z.own
    for tap, (block, offset) in enumerate(spots(9, z.own)):
        for m in range(z.chans // LANES):
            total = None
            for p in range(per):
                at = (m * per + p, slice(None), slice(block * LANES, (block + 1) * LANES))
                value = mine[at].astype(F32) + other[at].astype(F32)
                value = lanes_down(value, offset - p * z.own)
                if total is None:
                    total = value
                else:
                    lane = lax.broadcasted_iota(jnp.int32, value.shape, 1)
                    total = jnp.where(lane < p * z.own, total, value)
            space[tap, :, m * LANES : (m + 1) * LANES] = total


VM = pl.BlockSpec(memory_space=pltpu.VMEM)
ANY = pl.BlockSpec(memory_space=pl.ANY)


def shaped(shape, dtype):
    return jax.ShapeDtypeStruct(shape, dtype)


def local(block_data, code_index, levels, w_space, w_time, enc_proj, dec_proj):
    frames, cols, chans = block_data.shape[2], block_data.shape[4], block_data.shape[5]
    lat, own = code_index.shape[1], w_space.shape[2]
    z = Sizes(lax.axis_size("sp"), frames, cols, chans, own, lat)
    scale = float(lax.axis_size("dp") * z.count) ** (-0.5)
    decoder = lax.axis_index("sec") == 1
    params = pltpu.CompilerParams(vmem_limit_bytes=VMEM_BYTES)

    code_rows = code_index.reshape(lat, z.row).astype(BF16)
    ones = jnp.ones((1, z.row), BF16)
    code_rows = jnp.concatenate([code_rows, ones], axis=0)
    code_rows = jnp.pad(code_rows, ((0, 16 - lat - 1), (0, chans - z.row)))
    shard = jnp.concatenate([block_data.reshape(z.row, chans), code_rows], axis=0)
    chunks, steps = ring_gather(shard, "sp")
    pieces = w_space[0].reshape(9, own, z.sp, own).transpose(2, 1, 0, 3)
    pieces = pieces.reshape(z.sp, own, 9 * own)
    pieces = jnp.pad(pieces, ((0, 0), (0, 0), (0, z.wide - 9 * own)))
    w_cat = lax.all_to_all(pieces, "sp", 0, 0, tiled=True).reshape(chans, z.wide)
    wt = jnp.pad(w_time.reshape(3 * own, chans), ((0, z.thin - 3 * own), (0, 0)))
    proj = jnp.pad(jnp.where(decoder, dec_proj, enc_proj), ((0, 16 - lat), (0, 0)))
    half = jnp.pad((levels.astype(F32) - 1.0) * 0.5, (0, 16 - lat), constant_values=1.0)
    halves = jnp.broadcast_to(half[:, None], (16, LANES))

    part, hid_cat, slope, inner = pl.pallas_call(
        functools.partial(first_kernel, z, steps),
        out_shape=(
            shaped((8, z.count), F32),
            shaped((z.count, z.thin), BF16),
            shaped((z.sp, z.row, LANES), F32),
            shaped((z.sp, z.row, LANES), BF16),
        ),
        in_specs=[ANY] * z.sp + [VM] * 4,
        out_specs=(VM,) * 4,
        scratch_shapes=[
            pltpu.VMEM((z.count, chans), BF16),
            pltpu.VMEM((z.sp, 16, chans), BF16),
            pltpu.VMEM((z.sp + 2, z.row, z.wide), F32),
            pltpu.VMEM((3, z.sp + 2, z.row, LANES), BF16),
            pltpu.VMEM((z.count, z.wide), BF16),
            pltpu.VMEM((z.count, LANES), BF16),
            pltpu.VMEM((z.count, z.thin), F32),
            pltpu.SemaphoreType.DMA((2, z.sp)),
        ],
        compiler_params=params,
        name="first",
    )(*chunks, w_cat, wt, proj, halves)
    total = swap_sum(part, "sp")
    received = lax.ppermute(total, "sec", [(1, 0)])
    big, time, part = pl.pallas_call(
        functools.partial(second_kernel, z, steps, scale),
        out_shape=(
            shaped((chans, z.wide), BF16),
            shaped((3 * own, chans), F32),
            shaped((8, chans), F32),
        ),
        in_specs=[ANY] * z.sp + [VM] * 9,
        out_specs=(VM,) * 3,
        scratch_shapes=[
            pltpu.VMEM((z.count, chans), BF16),
            pltpu.VMEM((z.sp, 16, chans), BF16),
            pltpu.VMEM((3, z.sp + 2, z.row, LANES), BF16),
            pltpu.VMEM((z.count, z.wide), BF16),
            pltpu.VMEM((z.count, LANES), BF16),
            pltpu.VMEM((z.count, z.thin), F32),
            pltpu.SemaphoreType.DMA((2, z.sp)),
        ],
        compiler_params=params,
        name="second",
    )(*chunks, w_cat, wt, proj, halves, hid_cat, slope, inner, total, received)
    swap = [(0, 1), (1, 0)]
    big = lax.all_to_all(big.reshape(z.sp, own, z.wide), "sp", 0, 0, tiled=True)
    space, time = pl.pallas_call(
        functools.partial(last_kernel, z),
        out_shape=(shaped((9, own, chans), F32), shaped((3 * own, chans), F32)),
        in_specs=[VM] * 4,
        out_specs=(VM,) * 2,
        compiler_params=params,
        name="last",
    )(big, lax.ppermute(big, "dp", swap), time, lax.ppermute(time, "dp", swap))
    part = swap_sum(part, "sp")
    part = part + lax.ppermute(part, "dp", swap)
    return space[None], time.reshape(1, 3, own, chans), part[None, :lat]


def solution(mesh):
    placed = (
        P("sec", "dp", None, "sp", None, None),
        P("dp", None, None, "sp", None),
        P(),
        P("sec", None, "sp", None),
        P("sec", None, "sp", None),
        P(),
        P(),
    )
    return jax.shard_map(
        local,
        mesh=mesh,
        in_specs=placed,
        out_specs=(P("sec", None, "sp", None), P("sec", None, "sp", None), P("sec", None, None)),
        check_vma=False,
    )
```

time: 250 us -> 124 us (0.50)
  local copies, waits for them, and re-layouts: 56.6 us -> 9.75 us
  waiting for transfers between devices: 82.5 us -> 45.4 us
  between operations: 22.8 us -> 0.83 us
  blocking collectives: 38.9 us -> 17 us
  Pallas kernels: 0 us -> 19.6 us
  matrix products: 12 us -> 0 us
  starting transfers between devices: 20.6 us -> 30.4 us
  loops' own time: 7.73 us -> 0 us
  other arithmetic: 8.11 us -> 0.91 us
    all_gather x1 -> x0, blocking collectives: 38.9 us -> none  [local(): codes = lax.all_gather(code_index[0, :, :, 0], 'sp', axis=0)]
    ppermute x1, waiting for transfers between devices: 34 us -> 5.43 us  [local(): received = lax.ppermute(total, 'sec', [(1, 0)])]
    pallas_call x0 -> x3, Pallas kernels: none -> 19.6 us  [the longest x1 8.34 us: local(): pl.pallas_call(functools.partial(second_kernel, z, steps, scale), out_sha...]
    reshape x6 -> x0, local copies, waits for them, and re-layouts: 18.1 us -> none  [the longest x1 8.96 us: conv_sum(): taps = taps.reshape(grid + (3, 3, own))]
    all_to_all x0 -> x1, blocking collectives: none -> 17 us  [local(): big = lax.all_to_all(big.reshape(z.sp, own, z.wide), 'sp', 0, 0, tiled=True)]
    slice x2 -> x0, local copies, waits for them, and re-layouts: 12.6 us -> none  [the longest x1 11.7 us: conv_sum(): rows = sum((move(taps[:, :, :, i, j], 0, 1 - i) for i in range(3)))]
    dot_general x13 -> x0, matrix products: 12 us -> none  [the longest x11 6.75 us: dot32(): return jnp.dot(left, right, precision=HIGH, preferred_element_type=F32)]
    all_to_all x2 -> x1, waiting for transfers between devices: 11.5 us -> 0.01 us  [local(): lax.all_to_all(pieces, 'sp', 0, 0, tiled=True).reshape(chans, z.wide)]
  transfers between devices with their start and end apart: 19 -> 18, of which waited for: 12 -> 13; matrix products, arithmetic and copies ran while one was open for 4% -> 2% of each run, Pallas kernels for 0% -> 0%
where the time goes in v2:
time: 124 us
  waiting for transfers between devices  45.4 us (37%)
  starting transfers between devices  30.4 us (25%)
  Pallas kernels  19.6 us (16%)
  blocking collectives  17 us (14%)
  local copies, waits for them, and re-layouts  9.75 us (8%)
    ppermute x4, waiting for transfers between devices, ring_gather(): down = lax.ppermute(down, axis, forward)  20.9 us
    all_to_all x1, blocking collectives, local(): big = lax.all_to_all(big.reshape(z.sp, own, z.wide), 'sp', 0, 0, tiled=True)  17 us
    ppermute x6, waiting for transfers between devices, swap_sum(): lax.ppermute(values, axis, [(i, i ^ bit) for i in range(count)])  16.1 us
    ppermute x4, starting transfers between devices, ring_gather(): down = lax.ppermute(down, axis, forward)  10.2 us
    ppermute x6, starting transfers between devices, swap_sum(): lax.ppermute(values, axis, [(i, i ^ bit) for i in range(count)])  9.48 us
    pallas_call x1, Pallas kernels, local(): pl.pallas_call(functools.partial(second_kernel, z, steps, scale), out_sha...  8.34 us
    pallas_call x1, Pallas kernels, local(): pl.pallas_call(functools.partial(first_kernel, z, steps), out_shape=(shap...  8.26 us
    all_to_all x1, starting transfers between devices, local(): lax.all_to_all(pieces, 'sp', 0, 0, tiled=True).reshape(chans, z.wide)  7.42 us
  transfers between devices with their start and end apart: 18, of which 13 were waited for; matrix products, arithmetic and copies ran while one was open for 2% of the time, Pallas kernels for 0%

profile of v2, /device:TPU:0, one launch (start us, length us, event | category | flops | bytes accessed | tf_op | source)
XLA Modules:
  0.0 123.9 jit_solution(1747814112604381995)
XLA Ops:
  0.6 1.7 %reshape_squeeze.3 = bf16[9,64,8,64]{3,2,1,0:T(8,128)(2,1)S(1)} reshape(bf16[1,9,64,512]{3,2,1,0:T(8,128)(2,1)} %param.10) | data formatting | bytes 1179648 | tf_op jit(solution)/shard_map/reshape;squeeze | solution.py:409
  5.3 7.4 %all-to-all-start = ((bf16[8,64,640]{2,1,0:T(8,128)(2,1)}), bf16[8,64,640]{2,1,0:T(8,128)(2,1)S(1)}, u32[]{:S(2)}, u32[]{:S(2)}) async-start(bf16[8,64,640]{2,1,0:T(8,128)(2,1)} %pad.22.clone), calls=%async_computation | async-start | bytes 1310720 | tf_op jit(solution)/shard_map/all_to_all | solution.py:412
  12.9 2.1 %collective-permute-start = (bf16[176,512]{1,0:T(8,128)(2,1)S(1)}, bf16[176,512]{1,0:T(8,128)(2,1)S(1)}, u32[]{:S(2)}, u32[]{:S(2)}) collective-permute-start(bf16[176,512]{1,0:T(8,128)(2,1)S(1)} %pad_maximum_fusion.refs_0_), channel_id=1, source_target_pairs={{0,4},{4,8},{8,12},{12,14},{14,10},{10,6},{6,2},{2,0},{1,5},{5,9},... | collective-permute-start | bytes 540680 | tf_op jit(solution)/shard_map/ppermute | solution.py:40
  15.0 12.2 %collective-permute-done.refs_1_ = bf16[176,512]{1,0:T(8,128)(2,1)S(1)} collective-permute-done((bf16[176,512]{1,0:T(8,128)(2,1)S(1)}, bf16[176,512]{1,0:T(8,128)(2,1)S(1)}, u32[]{:S(2)}, u32[]{:S(2)}) %collective-permute-start) | collective-permute-done | bytes 180256 | tf_op jit(solution)/shard_map/ppermute | solution.py:40
  27.2 5.0 %collective-permute-start.2 = (bf16[176,512]{1,0:T(8,128)(2,1)S(1)}, bf16[176,512]{1,0:T(8,128)(2,1)S(1)}, u32[]{:S(2)}, u32[]{:S(2)}) collective-permute-start(bf16[176,512]{1,0:T(8,128)(2,1)S(1)} %collective-permute-done.refs_1_), channel_id=1, source_target_pairs={{0,4},{4,8},{8,12},{12,14},{14,10},{10,6},{6,2},{2,0},{1,5},{5,9},... | collective-permute-start | bytes 540680 | tf_op jit(solution)/shard_map/ppermute | solution.py:40
  32.3 3.5 %collective-permute-done.2.refs_3_ = bf16[176,512]{1,0:T(8,128)(2,1)S(1)} collective-permute-done((bf16[176,512]{1,0:T(8,128)(2,1)S(1)}, bf16[176,512]{1,0:T(8,128)(2,1)S(1)}, u32[]{:S(2)}, u32[]{:S(2)}) %collective-permute-start.2) | collective-permute-done | bytes 180256 | tf_op jit(solution)/shard_map/ppermute | solution.py:40
  35.8 2.5 %collective-permute-start.4 = (bf16[176,512]{1,0:T(8,128)(2,1)S(1)}, bf16[176,512]{1,0:T(8,128)(2,1)S(1)}, u32[]{:S(2)}, u32[]{:S(2)}) collective-permute-start(bf16[176,512]{1,0:T(8,128)(2,1)S(1)} %collective-permute-done.2.refs_3_), channel_id=1, source_target_pairs={{0,4},{4,8},{8,12},{12,14},{14,10},{10,6},{6,2},{2,0},{1,5},{5,9},... | collective-permute-start | bytes 540680 | tf_op jit(solution)/shard_map/ppermute | solution.py:40
  41.1 2.0 %collective-permute-done.4.refs_5_ = bf16[176,512]{1,0:T(8,128)(2,1)S(1)} collective-permute-done((bf16[176,512]{1,0:T(8,128)(2,1)S(1)}, bf16[176,512]{1,0:T(8,128)(2,1)S(1)}, u32[]{:S(2)}, u32[]{:S(2)}) %collective-permute-start.4) | collective-permute-done | bytes 180256 | tf_op jit(solution)/shard_map/ppermute | solution.py:40
  43.8 1.8 %collective-permute-done.5.refs_6_ = bf16[176,512]{1,0:T(8,128)(2,1)S(1)} collective-permute-done((bf16[176,512]{1,0:T(8,128)(2,1)S(1)}, bf16[176,512]{1,0:T(8,128)(2,1)S(1)}, u32[]{:S(2)}, u32[]{:S(2)}) %collective-permute-start.5) | collective-permute-done | bytes 180256 | tf_op jit(solution)/shard_map/ppermute | solution.py:44
  45.6 3.1 %collective-permute-done.6.refs_7_ = bf16[176,512]{1,0:T(8,128)(2,1)S(1)} collective-permute-done((bf16[176,512]{1,0:T(8,128)(2,1)S(1)}, bf16[176,512]{1,0:T(8,128)(2,1)S(1)}, u32[]{:S(2)}, u32[]{:S(2)}) %collective-permute-start.6) | collective-permute-done | bytes 180256 | tf_op jit(solution)/shard_map/ppermute | solution.py:40
  49.6 8.3 %first.1 = (f32[8,1280]{1,0:T(8,128)}, bf16[1280,256]{1,0:T(8,128)(2,1)}, f32[8,160,128]{2,1,0:T(8,128)}, bf16[8,160,128]{2,1,0:T(8,128)(2,1)}) custom-call(bf16[176,512]{1,0:T(8,128)(2,1)} %copy-done.2, bf16[176,512]{1,0:T(8,128)(2,1)} %copy-done.3, bf16[176,512]{1,0:T(8,128)(2,1)} %copy-done.4, bf16[176,512]{1,0:T(8,128)(2,1)} %copy-done.5, ...), custom_call_target="tpu_custom_call" | custom-call | tf_op jit(solution)/shard_map/first/pallas_call | solution.py:418
  57.9 2.4 %collective-permute-start.7 = (f32[8,1280]{1,0:T(8,128)}, f32[8,1280]{1,0:T(8,128)S(1)}, u32[]{:S(2)}, u32[]{:S(2)}) collective-permute-start(f32[8,1280]{1,0:T(8,128)} %get-tuple-element.15), channel_id=1, source_target_pairs={{0,2},{2,0},{4,6},{6,4},{8,10},{10,8},{12,14},{14,12},{1,3},{3,1},... | collective-permute-start | bytes 122888 | tf_op jit(solution)/shard_map/ppermute | solution.py:54
  60.2 2.2 %collective-permute-done.7 = f32[8,1280]{1,0:T(8,128)S(1)} collective-permute-done((f32[8,1280]{1,0:T(8,128)}, f32[8,1280]{1,0:T(8,128)S(1)}, u32[]{:S(2)}, u32[]{:S(2)}) %collective-permute-start.7) | collective-permute-done | bytes 40992 | tf_op jit(solution)/shard_map/ppermute | solution.py:54
  63.2 2.0 %collective-permute-start.8 = (f32[8,1280]{1,0:T(8,128)S(1)}, f32[8,1280]{1,0:T(8,128)S(1)}, u32[]{:S(2)}, u32[]{:S(2)}) collective-permute-start(f32[8,1280]{1,0:T(8,128)S(1)} %add.34), channel_id=1, source_target_pairs={{0,4},{2,6},{4,0},{6,2},{8,12},{10,14},{12,8},{14,10},{1,5},{3,7},... | collective-permute-start | bytes 122888 | tf_op jit(solution)/shard_map/ppermute | solution.py:54
  65.2 2.0 %collective-permute-done.8 = f32[8,1280]{1,0:T(8,128)S(1)} collective-permute-done((f32[8,1280]{1,0:T(8,128)S(1)}, f32[8,1280]{1,0:T(8,128)S(1)}, u32[]{:S(2)}, u32[]{:S(2)}) %collective-permute-start.8) | collective-permute-done | bytes 40992 | tf_op jit(solution)/shard_map/ppermute | solution.py:54
  67.2 2.2 %collective-permute-start.9 = (f32[8,1280]{1,0:T(8,128)S(1)}, f32[8,1280]{1,0:T(8,128)S(1)}, u32[]{:S(2)}, u32[]{:S(2)}) collective-permute-start(f32[8,1280]{1,0:T(8,128)S(1)} %add.35), channel_id=1, source_target_pairs={{0,8},{2,10},{4,12},{6,14},{8,0},{10,2},{12,4},{14,6},{1,9},{3,11}... | collective-permute-start | bytes 122888 | tf_op jit(solution)/shard_map/ppermute | solution.py:54
  69.4 2.7 %collective-permute-done.9 = f32[8,1280]{1,0:T(8,128)S(1)} collective-permute-done((f32[8,1280]{1,0:T(8,128)S(1)}, f32[8,1280]{1,0:T(8,128)S(1)}, u32[]{:S(2)}, u32[]{:S(2)}) %collective-permute-start.9) | collective-permute-done | bytes 40992 | tf_op jit(solution)/shard_map/ppermute | solution.py:54
  73.4 5.4 %collective-permute-done.10.refs_16_ = f32[8,1280]{1,0:T(8,128)S(1)} collective-permute-done((f32[8,1280]{1,0:T(8,128)S(1)}, f32[8,1280]{1,0:T(8,128)S(1)}, u32[]{:S(2)}, u32[]{:S(2)}) %collective-permute-start.10) | collective-permute-done | bytes 40992 | tf_op jit(solution)/shard_map/ppermute | solution.py:442
  79.5 8.3 %second.1 = (bf16[512,640]{1,0:T(8,128)(2,1)}, f32[192,512]{1,0:T(8,128)}, f32[8,512]{1,0:T(8,128)}) custom-call(bf16[176,512]{1,0:T(8,128)(2,1)} %copy-done.2, bf16[176,512]{1,0:T(8,128)(2,1)} %copy-done.3, bf16[176,512]{1,0:T(8,128)(2,1)} %copy-done.4, bf16[176,512]{1,0:T(8,128)(2,1)} %copy-done.5, bf16[176,512]{1,0:T(8,128)(2,1)} %copy-done.6, ...), custom_call_target="tpu_custom_call" | custom-call | tf_op jit(solution)/shard_map/second/pallas_call | solution.py:443
  87.8 17.0 %all_to_all.10.mine = bf16[8,64,640]{2,1,0:T(8,128)(2,1)S(1)} all-to-all(bf16[8,64,640]{2,1,0:T(8,128)(2,1)} %bitcast.16), channel_id=1, replica_groups=mesh['sec'=2,'sp'=8,'dp'=2] {'sp'}, dimensions={0} | all-to-all | bytes 1310720 | tf_op jit(solution)/shard_map/all_to_all | solution.py:465
  106.4 2.6 %collective-permute-done.13 = f32[8,512]{1,0:T(8,128)S(1)} collective-permute-done((f32[8,512]{1,0:T(8,128)S(1)}, f32[8,512]{1,0:T(8,128)S(1)}, u32[]{:S(2)}, u32[]{:S(2)}) %collective-permute-start.13) | collective-permute-done | bytes 16416 | tf_op jit(solution)/shard_map/ppermute | solution.py:54
  110.0 2.8 %collective-permute-done.14 = f32[8,512]{1,0:T(8,128)S(1)} collective-permute-done((f32[8,512]{1,0:T(8,128)S(1)}, f32[8,512]{1,0:T(8,128)S(1)}, u32[]{:S(2)}, u32[]{:S(2)}) %collective-permute-start.14) | collective-permute-done | bytes 16416 | tf_op jit(solution)/shard_map/ppermute | solution.py:54
  113.7 3.7 %collective-permute-done.15 = f32[8,512]{1,0:T(8,128)S(1)} collective-permute-done((f32[8,512]{1,0:T(8,128)S(1)}, f32[8,512]{1,0:T(8,128)S(1)}, u32[]{:S(2)}, u32[]{:S(2)}) %collective-permute-start.15) | collective-permute-done | bytes 16416 | tf_op jit(solution)/shard_map/ppermute | solution.py:54
  120.8 3.0 %last.1 = (f32[9,64,512]{2,1,0:T(8,128)}, f32[192,512]{1,0:T(8,128)}) custom-call(bf16[8,64,640]{2,1,0:T(8,128)(2,1)} %copy-done.1, bf16[8,64,640]{2,1,0:T(8,128)(2,1)} %copy-done.10, f32[192,512]{1,0:T(8,128)} %get-tuple-element.17.time_mine, f32[192,512]{1,0:T(8,128)} %copy-done.12), custom_call_target="tpu_custom_call" | custom-call | tf_op jit(solution)/shard_map/last/pallas_call | solution.py:466
  (82 shorter events, 17.0 us)
Async XLA Ops:
  5.3 33.0 %copy-start.19 = (bf16[6,512]{1,0:T(8,128)(2,1)S(1)}, bf16[6,512]{1,0:T(8,128)(2,1)}, u32[]{:S(2)}) copy-start(bf16[6,512]{1,0:T(8,128)(2,1)} %param.13) | copy-start | bytes 18436
  5.3 33.0 %copy-start.20 = (bf16[6,512]{1,0:T(8,128)(2,1)S(1)}, bf16[6,512]{1,0:T(8,128)(2,1)}, u32[]{:S(2)}) copy-start(bf16[6,512]{1,0:T(8,128)(2,1)} %param.12) | copy-start | bytes 18436
  5.3 33.6 %copy-start.13 = (bf16[1,3,64,512]{3,2,1,0:T(8,128)(2,1)S(1)}, bf16[1,3,64,512]{3,2,1,0:T(8,128)(2,1)}, u32[]{:S(2)}) copy-start(bf16[1,3,64,512]{3,2,1,0:T(8,128)(2,1)} %param.11) | copy-start | bytes 589828
  5.3 38.5 %copy-start.21 = (s32[6]{0:T(128)S(1)}, s32[6]{0:T(128)}, u32[]{:S(2)}) copy-start(s32[6]{0:T(128)} %param.9) | copy-start | bytes 76
  5.3 43.4 %all-to-all-start = ((bf16[8,64,640]{2,1,0:T(8,128)(2,1)}), bf16[8,64,640]{2,1,0:T(8,128)(2,1)S(1)}, u32[]{:S(2)}, u32[]{:S(2)}) async-start(bf16[8,64,640]{2,1,0:T(8,128)(2,1)} %pad.22.clone), calls=%async_computation | async-start | bytes 1310720 | tf_op jit(solution)/shard_map/all_to_all | solution.py:412
  12.9 36.6 %copy-start.2 = (bf16[176,512]{1,0:T(8,128)(2,1)}, bf16[176,512]{1,0:T(8,128)(2,1)S(1)}, u32[]{:S(2)}) copy-start(bf16[176,512]{1,0:T(8,128)(2,1)S(1)} %pad_maximum_fusion.refs_0_) | copy-start | bytes 540676
  12.9 14.3 %collective-permute-start = (bf16[176,512]{1,0:T(8,128)(2,1)S(1)}, bf16[176,512]{1,0:T(8,128)(2,1)S(1)}, u32[]{:S(2)}, u32[]{:S(2)}) collective-permute-start(bf16[176,512]{1,0:T(8,128)(2,1)S(1)} %pad_maximum_fusion.refs_0_), channel_id=1, source_target_pairs={{0,4},{4,8},{8,12},{12,14},{14,10},{10,6},{6,2},{2,0},{1,5},{5,9},... | collective-permute-start | bytes 540680 | tf_op jit(solution)/shard_map/ppermute | solution.py:40
  15.0 17.3 %collective-permute-start.1 = (bf16[176,512]{1,0:T(8,128)(2,1)S(1)}, bf16[176,512]{1,0:T(8,128)(2,1)S(1)}, u32[]{:S(2)}, u32[]{:S(2)}) collective-permute-start(bf16[176,512]{1,0:T(8,128)(2,1)S(1)} %pad_maximum_fusion.refs_0_), channel_id=1, source_target_pairs={{4,0},{8,4},{12,8},{14,12},{10,14},{6,10},{2,6},{0,2},{5,1},{9,5},... | collective-permute-start | bytes 540680 | tf_op jit(solution)/shard_map/ppermute | solution.py:44
  27.2 22.2 %copy-start.3 = (bf16[176,512]{1,0:T(8,128)(2,1)}, bf16[176,512]{1,0:T(8,128)(2,1)S(1)}, u32[]{:S(2)}) copy-start(bf16[176,512]{1,0:T(8,128)(2,1)S(1)} %collective-permute-done.refs_1_) | copy-start | bytes 540676
  27.2 8.5 %collective-permute-start.2 = (bf16[176,512]{1,0:T(8,128)(2,1)S(1)}, bf16[176,512]{1,0:T(8,128)(2,1)S(1)}, u32[]{:S(2)}, u32[]{:S(2)}) collective-permute-start(bf16[176,512]{1,0:T(8,128)(2,1)S(1)} %collective-permute-done.refs_1_), channel_id=1, source_target_pairs={{0,4},{4,8},{8,12},{12,14},{14,10},{10,6},{6,2},{2,0},{1,5},{5,9},... | collective-permute-start | bytes 540680 | tf_op jit(solution)/shard_map/ppermute | solution.py:40
  32.3 7.3 %collective-permute-start.3 = (bf16[176,512]{1,0:T(8,128)(2,1)S(1)}, bf16[176,512]{1,0:T(8,128)(2,1)S(1)}, u32[]{:S(2)}, u32[]{:S(2)}) collective-permute-start(bf16[176,512]{1,0:T(8,128)(2,1)S(1)} %collective-permute-done.1.refs_2_), channel_id=1, source_target_pairs={{4,0},{8,4},{12,8},{14,12},{10,14},{6,10},{2,6},{0,2},{5,1},{9,5},... | collective-permute-start | bytes 540680 | tf_op jit(solution)/shard_map/ppermute | solution.py:44
  35.8 7.4 %collective-permute-start.4 = (bf16[176,512]{1,0:T(8,128)(2,1)S(1)}, bf16[176,512]{1,0:T(8,128)(2,1)S(1)}, u32[]{:S(2)}, u32[]{:S(2)}) collective-permute-start(bf16[176,512]{1,0:T(8,128)(2,1)S(1)} %collective-permute-done.2.refs_3_), channel_id=1, source_target_pairs={{0,4},{4,8},{8,12},{12,14},{14,10},{10,6},{6,2},{2,0},{1,5},{5,9},... | collective-permute-start | bytes 540680 | tf_op jit(solution)/shard_map/ppermute | solution.py:40
  39.6 6.0 %collective-permute-start.5 = (bf16[176,512]{1,0:T(8,128)(2,1)S(1)}, bf16[176,512]{1,0:T(8,128)(2,1)S(1)}, u32[]{:S(2)}, u32[]{:S(2)}) collective-permute-start(bf16[176,512]{1,0:T(8,128)(2,1)S(1)} %collective-permute-done.3.refs_4_), channel_id=1, source_target_pairs={{4,0},{8,4},{12,8},{14,12},{10,14},{6,10},{2,6},{0,2},{5,1},{9,5},... | collective-permute-start | bytes 540680 | tf_op jit(solution)/shard_map/ppermute | solution.py:44
  43.1 5.6 %collective-permute-start.6 = (bf16[176,512]{1,0:T(8,128)(2,1)S(1)}, bf16[176,512]{1,0:T(8,128)(2,1)S(1)}, u32[]{:S(2)}, u32[]{:S(2)}) collective-permute-start(bf16[176,512]{1,0:T(8,128)(2,1)S(1)} %collective-permute-done.4.refs_5_), channel_id=1, source_target_pairs={{0,4},{4,8},{8,12},{12,14},{14,10},{10,6},{6,2},{2,0},{1,5},{5,9},... | collective-permute-start | bytes 540680 | tf_op jit(solution)/shard_map/ppermute | solution.py:40
  57.9 4.5 %collective-permute-start.7 = (f32[8,1280]{1,0:T(8,128)}, f32[8,1280]{1,0:T(8,128)S(1)}, u32[]{:S(2)}, u32[]{:S(2)}) collective-permute-start(f32[8,1280]{1,0:T(8,128)} %get-tuple-element.15), channel_id=1, source_target_pairs={{0,2},{2,0},{4,6},{6,4},{8,10},{10,8},{12,14},{14,12},{1,3},{3,1},... | collective-permute-start | bytes 122888 | tf_op jit(solution)/shard_map/ppermute | solution.py:54
  63.2 4.0 %collective-permute-start.8 = (f32[8,1280]{1,0:T(8,128)S(1)}, f32[8,1280]{1,0:T(8,128)S(1)}, u32[]{:S(2)}, u32[]{:S(2)}) collective-permute-start(f32[8,1280]{1,0:T(8,128)S(1)} %add.34), channel_id=1, source_target_pairs={{0,4},{2,6},{4,0},{6,2},{8,12},{10,14},{12,8},{14,10},{1,5},{3,7},... | collective-permute-start | bytes 122888 | tf_op jit(solution)/shard_map/ppermute | solution.py:54
  67.2 4.9 %collective-permute-start.9 = (f32[8,1280]{1,0:T(8,128)S(1)}, f32[8,1280]{1,0:T(8,128)S(1)}, u32[]{:S(2)}, u32[]{:S(2)}) collective-permute-start(f32[8,1280]{1,0:T(8,128)S(1)} %add.35), channel_id=1, source_target_pairs={{0,8},{2,10},{4,12},{6,14},{8,0},{10,2},{12,4},{14,6},{1,9},{3,11}... | collective-permute-start | bytes 122888 | tf_op jit(solution)/shard_map/ppermute | solution.py:54
  72.1 6.7 %collective-permute-start.10 = (f32[8,1280]{1,0:T(8,128)S(1)}, f32[8,1280]{1,0:T(8,128)S(1)}, u32[]{:S(2)}, u32[]{:S(2)}) collective-permute-start(f32[8,1280]{1,0:T(8,128)S(1)} %add.36.refs_15_), channel_id=1, source_target_pairs={{16,0},{17,1},{18,2},{19,3},{20,4},{21,5},{22,6},{23,7},{24,8},{25... | collective-permute-start | bytes 122888 | tf_op jit(solution)/shard_map/ppermute | solution.py:442
  104.8 14.5 %collective-permute-start.11 = (bf16[8,64,640]{2,1,0:T(8,128)(2,1)S(1)}, bf16[8,64,640]{2,1,0:T(8,128)(2,1)S(1)}, u32[]{:S(2)}, u32[]{:S(2)}) collective-permute-start(bf16[8,64,640]{2,1,0:T(8,128)(2,1)S(1)} %all_to_all.10.mine), channel_id=1, source_target_pairs={{0,1},{1,0},{2,3},{3,2},{4,5},{5,4},{6,7},{7,6},{8,9},{9,8},{10,11... | collective-permute-start | bytes 1966088 | tf_op jit(solution)/shard_map/ppermute | solution.py:473
  104.8 14.4 %collective-permute-start.12 = (f32[192,512]{1,0:T(8,128)S(1)}, f32[192,512]{1,0:T(8,128)S(1)}, u32[]{:S(2)}, u32[]{:S(2)}) collective-permute-start(f32[192,512]{1,0:T(8,128)S(1)} %copy-done.11), channel_id=1, source_target_pairs={{0,1},{1,0},{2,3},{3,2},{4,5},{5,4},{6,7},{7,6},{8,9},{9,8},{10,11... | collective-permute-start | bytes 1179656 | tf_op jit(solution)/shard_map/ppermute | solution.py:473
  105.3 3.7 %collective-permute-start.13 = (f32[8,512]{1,0:T(8,128)S(1)}, f32[8,512]{1,0:T(8,128)S(1)}, u32[]{:S(2)}, u32[]{:S(2)}) collective-permute-start(f32[8,512]{1,0:T(8,128)S(1)} %copy-done.17), channel_id=1, source_target_pairs={{0,2},{2,0},{4,6},{6,4},{8,10},{10,8},{12,14},{14,12},{1,3},{3,1},... | collective-permute-start | bytes 49160 | tf_op jit(solution)/shard_map/ppermute | solution.py:54
  109.1 3.7 %collective-permute-start.14 = (f32[8,512]{1,0:T(8,128)S(1)}, f32[8,512]{1,0:T(8,128)S(1)}, u32[]{:S(2)}, u32[]{:S(2)}) collective-permute-start(f32[8,512]{1,0:T(8,128)S(1)} %add.37), channel_id=1, source_target_pairs={{0,4},{2,6},{4,0},{6,2},{8,12},{10,14},{12,8},{14,10},{1,5},{3,7},... | collective-permute-start | bytes 49160 | tf_op jit(solution)/shard_map/ppermute | solution.py:54
  112.8 4.6 %collective-permute-start.15 = (f32[8,512]{1,0:T(8,128)S(1)}, f32[8,512]{1,0:T(8,128)S(1)}, u32[]{:S(2)}, u32[]{:S(2)}) collective-permute-start(f32[8,512]{1,0:T(8,128)S(1)} %add.38), channel_id=1, source_target_pairs={{0,8},{2,10},{4,12},{6,14},{8,0},{10,2},{12,4},{14,6},{1,9},{3,11}... | collective-permute-start | bytes 49160 | tf_op jit(solution)/shard_map/ppermute | solution.py:54
  117.4 1.2 collective-permute-start.16
  (16 other events, 127.7 us)

commit v3 on v2

--- a/solution.py
+++ b/solution.py
@@ -29,22 +29,42 @@
     return jnp.where(place < count // 2, 2 * place, 2 * (count - place) - 1)
 
 
-def ring_gather(shard, axis):
-    count = lax.axis_size(axis)
+def ring_maps(count):
     order = list(range(0, count, 2)) + list(range(count - 1, 0, -2))
     forward = [(order[i], order[(i + 1) % count]) for i in range(count)]
-    backward = [(target, source) for source, target in forward]
-    blocks, steps = [shard], [0]
-    down = up = shard
+    return forward, [(target, source) for source, target in forward]
+
+
+def ring_exchange(shard, ahead, behind, own_piece):
+    count = lax.axis_size("sp")
+    up, down = ring_maps(count)
+    swap = [(0, 1), (1, 0)]
+    first = shard
+    shards, shard_steps = [shard], [0]
+    mine, other, piece_steps = [own_piece], [lax.ppermute(own_piece, "dp", swap)], [0]
+    second = shard
     for step in range(1, count // 2 + 1):
-        down = lax.ppermute(down, axis, forward)
-        blocks.append(down)
-        steps.append(-step)
+        first = lax.ppermute(first, "sp", up)
+        shards.append(first)
+        shard_steps.append(-step)
         if step < count - step:
-            up = lax.ppermute(up, axis, backward)
-            blocks.append(up)
-            steps.append(step)
-    return blocks, steps
+            second = lax.ppermute(second, "sp", down)
+            shards.append(second)
+            shard_steps.append(step)
+        fresh = []
+        behind = lax.ppermute(behind, "sp", down)
+        fresh.append(behind[0])
+        piece_steps.append(step)
+        behind = behind[1:]
+        if step < count - step:
+            ahead = lax.ppermute(ahead, "sp", up)
+            fresh.append(ahead[0])
+            piece_steps.append(-step)
+            ahead = ahead[1:]
+        both = lax.ppermute(jnp.stack(fresh), "dp", swap)
+        mine += fresh
+        other += [both[i] for i in range(len(fresh))]
+    return shards, shard_steps, mine, other, piece_steps
 
 
 def swap_sum(values, axis):
@@ -119,23 +139,46 @@
         self.count = sp * self.row
         self.wide = up_to(9 * own, LANES)
         self.thin = up_to(3 * own, LANES)
-
-
-def load_rows(z, steps, chunks, v, codes, sems):
+        self.half = own // 2
+        code_rows = frames * lat
+        self.code_rows = up_to(code_rows, 16)
+        self.half_pad = up_to(self.half, 16)
+        if self.wide - 9 * own >= cols and self.half >= code_rows:
+            self.code_row, self.code_lane = 0, 9 * own
+            self.piece_rows = self.half
+        else:
+            self.code_row, self.code_lane = up_to(self.half, 16), 0
+            self.piece_rows = self.code_row + up_to(code_rows, 16)
+        self.carries = self.wide - 9 * own >= LANES // 2 and own * (LANES // 2) >= 8 * chans
+
+
+def load_shards(z, steps, shards, v, sems):
     place = ring_place(lax.axis_index("sp"), z.sp)
     started = []
-    for k, (chunk, step) in enumerate(zip(chunks, steps)):
+    for k, (shard, step) in enumerate(zip(shards, steps)):
         row = ring_device(place + step, z.sp)
-        copy = pltpu.make_async_copy(
-            chunk.at[pl.ds(0, z.row)],
-            v.at[pl.ds(pl.multiple_of(row * z.row, z.row), z.row)],
-            sems.at[0, k],
-        )
+        copy = pltpu.make_async_copy(shard, v.at[rows_at(row, z)], sems.at[k])
         copy.start()
         started.append(copy)
-        copy = pltpu.make_async_copy(chunk.at[pl.ds(z.row, 16)], codes.at[row], sems.at[1, k])
-        copy.start()
-        started.append(copy)
+    return started
+
+
+def load_pieces(z, steps, mine, other, halves, codes, sems):
+    place = ring_place(lax.axis_index("sp"), z.sp)
+    core = lax.axis_index("dp")
+    started = []
+    for k, (one, two, step) in enumerate(zip(mine, other, steps)):
+        row = ring_device(place + step, z.sp)
+        for at, (source, target) in enumerate(
+            (
+                (one.at[pl.ds(0, z.half_pad)], halves.at[row, core]),
+                (two.at[pl.ds(0, z.half_pad)], halves.at[row, 1 - core]),
+                (one.at[pl.ds(z.code_row, z.code_rows)], codes.at[row]),
+            )
+        ):
+            copy = pltpu.make_async_copy(source, target, sems.at[at, k])
+            copy.start()
+            started.append(copy)
     return started
 
 
@@ -207,26 +250,96 @@
 
 
 def position_codes(z, codes, out):
+    block, offset = z.code_lane // LANES, z.code_lane % LANES
+
     def body(r, carry):
-        block = codes[r].astype(F32)[:, : up_to(z.row, LANES)]
-        block = jnp.concatenate([block] * 3 + [jnp.zeros((LANES - 48, block.shape[1]), F32)], 0)
-        out[rows_at(r, z)] = block.T[: z.row].astype(BF16)
+        raw = codes[r, :, block * LANES : (block + 1) * LANES].astype(F32)
+        raw = jnp.concatenate([raw, jnp.zeros((LANES - z.code_rows, LANES), F32)], axis=0)
+        turned = raw.T[offset : offset + z.cols]
+        lane = lax.broadcasted_iota(jnp.int32, turned.shape, 1)
+        frames = []
+        for t in range(z.frames):
+            values = lanes_down(turned, t * z.lat)
+            values = jnp.where(lane < z.lat, values, jnp.where(lane == z.lat, 1.0, 0.0))
+            frames.append(
+                values + pltpu.roll(values, 16, 1) + pltpu.roll(values, 32, 1)
+            )
+        out[rows_at(r, z)] = jnp.concatenate(frames, axis=0).astype(BF16)
         return carry
 
     lax.fori_loop(0, z.sp, body, 0)
 
 
-def first_kernel(z, steps, *refs):
-    n = len(steps)
-    chunks, (w_cat, wt, proj, halves) = refs[:n], refs[n : n + 4]
-    part, hid_cat, slope, inner_out = refs[n + 4 : n + 8]
-    v, codes, taps, shifts, inner_cat, pos, thin, sems = refs[n + 8 :]
-    started = load_rows(z, steps, chunks, v, codes, sems)
+def piece_kernel(z, w, codes, ahead, behind, own_piece):
+    place = ring_place(lax.axis_index("sp"), z.sp)
+    core = lax.axis_index("dp")
+    lane = lax.broadcasted_iota(jnp.int32, (z.half, LANES), 1)
+    code_block = codes[...]
+    for j in range(z.sp):
+        block, offset = (j * z.own) // LANES, (j * z.own) % LANES
+        taps = []
+        for tap in range(9):
+            at = slice(block * LANES, (block + 1) * LANES)
+            if z.half == z.half_pad:
+                value = w[tap, pl.ds(pl.multiple_of(core * z.half, z.half), z.half), at]
+                value = value.astype(F32)
+            else:
+                value = w[tap, :, at].astype(F32)
+                value = jnp.where(core == 0, value[: z.half], value[z.half :])
+            value = lanes_down(value, offset)
+            taps.append(jnp.where(lane < z.own, value, 0.0))
+        blocks = merge(taps, z.own)
+        if z.code_row == 0:
+            blocks[-1] = blocks[-1] + code_block
+        distance = lax.rem(ring_place(jnp.int32(j), z.sp) - place + z.sp, z.sp)
+
+        def store(target, index):
+            for b, value in enumerate(blocks):
+                at = slice(b * LANES, (b + 1) * LANES)
+                if index is None:
+                    target[: z.half, at] = value.astype(BF16)
+                else:
+                    target[index, : z.half, at] = value.astype(BF16)
+            if z.code_row:
+                tail = slice(z.code_row, z.piece_rows)
+                if index is None:
+                    target[tail, :LANES] = code_block.astype(BF16)
+                else:
+                    target[index, tail, :LANES] = code_block.astype(BF16)
+
+        @pl.when(distance == 0)
+        def _():
+            store(own_piece, None)
+
+        @pl.when(jnp.logical_and(distance > 0, distance < z.sp // 2))
+        def _():
+            store(ahead, distance - 1)
+
+        @pl.when(distance >= z.sp // 2)
+        def _():
+            store(behind, z.sp - distance - 1)
+
+
+def first_kernel(z, steps, piece_steps, *refs):
+    n = z.sp
+    shards, mine, other = refs[:n], refs[n : 2 * n], refs[2 * n : 3 * n]
+    wt, proj, halves = refs[3 * n : 3 * n + 3]
+    part, hid_cat, slope, inner_out, w_cat, pos = refs[3 * n + 3 : 3 * n + 9]
+    v, w_halves, codes, taps, shifts, inner_cat, thin, sems, piece_sems = refs[3 * n + 9 :]
+    started = load_pieces(z, piece_steps, mine, other, w_halves, codes, piece_sems)
+    started += load_shards(z, steps, shards, v, sems)
     decoder = lax.axis_index("sec") == 1
     first = lax.axis_index("sp") == 0
     zero_ends(z, taps)
     for copy in started:
         copy.wait()
+    if z.half == z.half_pad:
+        w_cat[...] = w_halves[...].reshape(z.chans, z.wide)
+    else:
+        for j in range(z.sp):
+            for core in range(2):
+                rows = slice(j * z.own + core * z.half, j * z.own + (core + 1) * z.half)
+                w_cat[rows] = w_halves[j, core, : z.half]
     whole = dot(proj[...], v[...], NT)[:8]
 
     def store_hidden(pre, logistic, r):
@@ -236,8 +349,7 @@
             hid_cat[rows_at(r, z), b * LANES : (b + 1) * LANES] = block.astype(BF16)
 
     def finish(weights, cat):
-        stacked = jnp.concatenate([weights[:8]] * 1, axis=0)
-        partial = sum3(dot(stack3(stacked), cat, NT))
+        partial = sum3(dot(stack3(weights[:8]), cat, NT))
         part[...] = partial + jnp.where(first, whole, 0.0)
 
     @pl.when(decoder)
@@ -299,11 +411,11 @@
 
 def second_kernel(z, steps, scale, *refs):
     n = len(steps)
-    chunks = refs[:n]
-    w_cat, wt, proj, halves, hid_cat, slope, inner_in, total, received = refs[n : n + 9]
-    big, time, part = refs[n + 9 : n + 12]
-    v, codes, shifts, inner_cat, pos, thin, sems = refs[n + 12 :]
-    started = load_rows(z, steps, chunks, v, codes, sems)
+    shards = refs[:n]
+    w_cat, pos, wt, proj, halves, hid_cat, slope, inner_in, total, received = refs[n : n + 10]
+    big, time, part = refs[n + 10 : n + 13]
+    v, shifts, inner_cat, thin, sems = refs[n + 13 :]
+    started = load_shards(z, steps, shards, v, sems)
     decoder = lax.axis_index("sec") == 1
     first = lax.axis_index("sp") == 0
     for j in range(3):
@@ -311,10 +423,27 @@
     for copy in started:
         copy.wait()
 
+    def put_out(kernel_grad, proj_part):
+        part[...] = proj_part
+        if not z.carries:
+            big[...] = kernel_grad.astype(BF16)
+            return
+        side = z.wide - LANES
+        big[:, :side] = kernel_grad[:, :side].astype(BF16)
+        pieces = []
+        for b in range(2 * z.chans // LANES):
+            block = proj_part[:, (b // 2) * LANES : (b // 2 + 1) * LANES]
+            pieces.append(block if b % 2 else pltpu.roll(block, LANES // 2, 1))
+        carried = jnp.concatenate(pieces, axis=0)
+        lane = lax.broadcasted_iota(jnp.int32, carried.shape, 1)
+        for j in range(z.sp):
+            rows = slice(j * z.own, (j + 1) * z.own)
+            big[rows, side:] = jnp.where(
+                lane < LANES // 2, kernel_grad[rows, side:], carried
+            ).astype(BF16)
+
     @pl.when(decoder)
     def _():
-        position_codes(z, codes, pos)
-
         def body(r, carry):
             put_shifts(z, inner_in[r].astype(F32), shifts, r)
             return carry
@@ -330,11 +459,11 @@
         short = latent_rows(dot(pos[...], inner_cat[...], TN)[:8])
         proj8 = proj[:8].astype(F32)
         proj24 = jnp.concatenate([proj8] * 3, axis=0).astype(BF16)
-        big[...] = (dot(proj24, stack3(short), TN) * scale).astype(BF16)
+        kernel_grad = dot(proj24, stack3(short), TN) * scale
         time[...] = dot(hid_cat[...], v[...], TN)[: 3 * z.own] * scale
         whole = latent_rows(dot(pos[...], v[...], TN)[:8])
         partial = sum3(dot(stack3(short), w_cat[...], NT))
-        part[...] = (partial + jnp.where(first, whole, 0.0)) * scale
+        put_out(kernel_grad, (partial + jnp.where(first, whole, 0.0)) * scale)
 
     @pl.when(jnp.logical_not(decoder))
     def _():
@@ -354,7 +483,7 @@
 
         lax.fori_loop(0, z.sp, body, 0)
         spread(z, shifts, inner_cat)
-        big[...] = (dot(v[...], inner_cat[...], TN) * scale).astype(BF16)
+        kernel_grad = dot(v[...], inner_cat[...], TN) * scale
         grad3 = jnp.concatenate([gh, gm, gl], axis=0).astype(BF16)
         short = sum3(dot(grad3, hid_cat[...], NN))
         short3 = stack3(short)
@@ -363,11 +492,23 @@
         time[...] = dot(short3, proj24, TN)[: 3 * z.own] * scale
         whole = sum3(dot(grad3, v[...], NN))
         partial = sum3(dot(short3, wt[...], NN))
-        part[...] = (partial + jnp.where(first, whole, 0.0)) * scale
-
-
-def last_kernel(z, mine, other, time_mine, time_other, space, time):
+        put_out(kernel_grad, (partial + jnp.where(first, whole, 0.0)) * scale)
+
+
+def last_kernel(z, mine, other, time_mine, time_other, space, time, part):
     time[...] = time_mine[...] + time_other[...]
+    if z.carries:
+        side = slice(z.wide - LANES, z.wide)
+        carried = 0.0
+        for j in range(z.sp):
+            carried = carried + (mine[j, :, side].astype(F32) + other[j, :, side].astype(F32))
+        lane = lax.broadcasted_iota(jnp.int32, (8, LANES), 1)
+        for m in range(z.chans // LANES):
+            low = pltpu.roll(carried[16 * m : 16 * m + 8], LANES // 2, 1)
+            high = carried[16 * m + 8 : 16 * m + 16]
+            part[:, m * LANES : (m + 1) * LANES] = jnp.where(lane < LANES // 2, low, high)
+    else:
+        part[...] = jnp.zeros(part.shape, F32)
     per = LANES // z.own
     for tap, (block, offset) in enumerate(spots(9, z.own)):
         for m in range(z.chans // LANES):
@@ -400,46 +541,61 @@
     decoder = lax.axis_index("sec") == 1
     params = pltpu.CompilerParams(vmem_limit_bytes=VMEM_BYTES)
 
-    code_rows = code_index.reshape(lat, z.row).astype(BF16)
-    ones = jnp.ones((1, z.row), BF16)
-    code_rows = jnp.concatenate([code_rows, ones], axis=0)
-    code_rows = jnp.pad(code_rows, ((0, 16 - lat - 1), (0, chans - z.row)))
-    shard = jnp.concatenate([block_data.reshape(z.row, chans), code_rows], axis=0)
-    chunks, steps = ring_gather(shard, "sp")
-    pieces = w_space[0].reshape(9, own, z.sp, own).transpose(2, 1, 0, 3)
-    pieces = pieces.reshape(z.sp, own, 9 * own)
-    pieces = jnp.pad(pieces, ((0, 0), (0, 0), (0, z.wide - 9 * own)))
-    w_cat = lax.all_to_all(pieces, "sp", 0, 0, tiled=True).reshape(chans, z.wide)
+    codes = jnp.transpose(code_index[0, :, :, 0], (1, 0, 2)).reshape(frames * lat, cols)
+    left = z.code_lane % LANES
+    codes = jnp.pad(
+        codes.astype(F32),
+        ((0, (z.half if z.code_row == 0 else z.code_rows) - frames * lat), (left, LANES - left - cols)),
+    )
+    ahead, behind, own_piece = pl.pallas_call(
+        functools.partial(piece_kernel, z),
+        out_shape=(
+            shaped((z.sp // 2 - 1, z.piece_rows, z.wide), BF16),
+            shaped((z.sp // 2, z.piece_rows, z.wide), BF16),
+            shaped((z.piece_rows, z.wide), BF16),
+        ),
+        in_specs=[VM] * 2,
+        out_specs=(VM,) * 3,
+        compiler_params=params,
+        name="pieces",
+    )(w_space[0], codes)
+    shards, steps, mine, other, piece_steps = ring_exchange(
+        block_data.reshape(z.row, chans), ahead, behind, own_piece
+    )
     wt = jnp.pad(w_time.reshape(3 * own, chans), ((0, z.thin - 3 * own), (0, 0)))
     proj = jnp.pad(jnp.where(decoder, dec_proj, enc_proj), ((0, 16 - lat), (0, 0)))
     half = jnp.pad((levels.astype(F32) - 1.0) * 0.5, (0, 16 - lat), constant_values=1.0)
     halves = jnp.broadcast_to(half[:, None], (16, LANES))
 
-    part, hid_cat, slope, inner = pl.pallas_call(
-        functools.partial(first_kernel, z, steps),
+    part, hid_cat, slope, inner, w_cat, pos = pl.pallas_call(
+        functools.partial(first_kernel, z, steps, piece_steps),
         out_shape=(
             shaped((8, z.count), F32),
             shaped((z.count, z.thin), BF16),
             shaped((z.sp, z.row, LANES), F32),
             shaped((z.sp, z.row, LANES), BF16),
+            shaped((chans, z.wide), BF16),
+            shaped((z.count, LANES), BF16),
         ),
-        in_specs=[ANY] * z.sp + [VM] * 4,
-        out_specs=(VM,) * 4,
+        in_specs=[ANY] * (3 * z.sp) + [VM] * 3,
+        out_specs=(VM,) * 6,
         scratch_shapes=[
             pltpu.VMEM((z.count, chans), BF16),
-            pltpu.VMEM((z.sp, 16, chans), BF16),
+            pltpu.VMEM((z.sp, 2, z.half_pad, z.wide), BF16),
+            pltpu.VMEM((z.sp, z.code_rows, z.wide), BF16),
             pltpu.VMEM((z.sp + 2, z.row, z.wide), F32),
             pltpu.VMEM((3, z.sp + 2, z.row, LANES), BF16),
             pltpu.VMEM((z.count, z.wide), BF16),
-            pltpu.VMEM((z.count, LANES), BF16),
             pltpu.VMEM((z.count, z.thin), F32),
-            pltpu.SemaphoreType.DMA((2, z.sp)),
+            pltpu.SemaphoreType.DMA((z.sp,)),
+            pltpu.SemaphoreType.DMA((3, z.sp)),
         ],
         compiler_params=params,
         name="first",
-    )(*chunks, w_cat, wt, proj, halves)
+    )(*shards, *mine, *other, wt, proj, halves)
+    swap = [(0, 1), (1, 0)]
     total = swap_sum(part, "sp")
-    received = lax.ppermute(total, "sec", [(1, 0)])
+    received = lax.ppermute(total, "sec", swap)
     big, time, part = pl.pallas_call(
         functools.partial(second_kernel, z, steps, scale),
         out_shape=(
@@ -447,32 +603,36 @@
             shaped((3 * own, chans), F32),
             shaped((8, chans), F32),
         ),
-        in_specs=[ANY] * z.sp + [VM] * 9,
+        in_specs=[ANY] * z.sp + [VM] * 10,
         out_specs=(VM,) * 3,
         scratch_shapes=[
             pltpu.VMEM((z.count, chans), BF16),
-            pltpu.VMEM((z.sp, 16, chans), BF16),
             pltpu.VMEM((3, z.sp + 2, z.row, LANES), BF16),
             pltpu.VMEM((z.count, z.wide), BF16),
-            pltpu.VMEM((z.count, LANES), BF16),
             pltpu.VMEM((z.count, z.thin), F32),
-            pltpu.SemaphoreType.DMA((2, z.sp)),
+            pltpu.SemaphoreType.DMA((z.sp,)),
         ],
         compiler_params=params,
         name="second",
-    )(*chunks, w_cat, wt, proj, halves, hid_cat, slope, inner, total, received)
-    swap = [(0, 1), (1, 0)]
+    )(*shards, w_cat, pos, wt, proj, halves, hid_cat, slope, inner, total, received)
     big = lax.all_to_all(big.reshape(z.sp, own, z.wide), "sp", 0, 0, tiled=True)
-    space, time = pl.pallas_call(
+    space, time, carried = pl.pallas_call(
         functools.partial(last_kernel, z),
-        out_shape=(shaped((9, own, chans), F32), shaped((3 * own, chans), F32)),
+        out_shape=(
+            shaped((9, own, chans), F32),
+            shaped((3 * own, chans), F32),
+            shaped((8, chans), F32),
+        ),
         in_specs=[VM] * 4,
-        out_specs=(VM,) * 2,
+        out_specs=(VM,) * 3,
         compiler_params=params,
         name="last",
     )(big, lax.ppermute(big, "dp", swap), time, lax.ppermute(time, "dp", swap))
-    part = swap_sum(part, "sp")
-    part = part + lax.ppermute(part, "dp", swap)
+    if z.carries:
+        part = carried
+    else:
+        part = swap_sum(part, "sp")
+        part = part + lax.ppermute(part, "dp", swap)
     return space[None], time.reshape(1, 3, own, chans), part[None, :lat]
 
 

time: 124 us -> 108 us (0.87)
  waiting for transfers between devices: 45.4 us -> 24.6 us
  starting transfers between devices: 30.4 us -> 26.2 us
  Pallas kernels: 19.6 us -> 23.1 us
  local copies, waits for them, and re-layouts: 9.75 us -> 12.2 us
  blocking collectives: 17 us -> 18.5 us
  other arithmetic: 0.91 us -> 2.26 us
    ppermute x9 -> x20, waiting for transfers between devices: 29.3 us -> 14 us  [the longest x4 4.31 us: ring_exchange(): first = lax.ppermute(first, 'sp', up)]
    ppermute x9 -> x20, starting transfers between devices: 13 us -> 21 us  [the longest x3 5.39 us: ring_exchange(): ahead = lax.ppermute(ahead, 'sp', up)]
    ppermute x6 -> x3, waiting for transfers between devices: 16.1 us -> 8.45 us  [swap_sum(): lax.ppermute(values, axis, [(i, i ^ bit) for i in range(count)])]
    all_to_all x1 -> x0, starting transfers between devices: 7.42 us -> none  [local(): lax.all_to_all(pieces, 'sp', 0, 0, tiled=True).reshape(chans, z.wide)]
    ppermute x6 -> x3, starting transfers between devices: 9.48 us -> 4.73 us  [swap_sum(): lax.ppermute(values, axis, [(i, i ^ bit) for i in range(count)])]
    pallas_call x1 -> x2, Pallas kernels: 8.26 us -> 11.6 us  [the longest x1 8.85 us: local(): pl.pallas_call(functools.partial(first_kernel, z, steps, piece_steps), ou...]
    slice x0 -> x8, local copies, waits for them, and re-layouts: none -> 3.14 us  [the longest x3 1.86 us: ring_exchange(): fresh.append(behind[0])]
    another operation x2 -> x0, local copies, waits for them, and re-layouts: 3.06 us -> none  [local(): pieces = w_space[0].reshape(9, own, z.sp, own).transpose(2, 1, 0, 3)]
  transfers between devices with their start and end apart: 18 -> 25, of which waited for: 13 -> 11; matrix products, arithmetic and copies ran while one was open for 2% -> 9% of each run, Pallas kernels for 0% -> 3%
where the time goes in v3:
time: 108 us
  starting transfers between devices  26.2 us (24%)
  waiting for transfers between devices  24.6 us (23%)
  Pallas kernels  23.1 us (21%)
  blocking collectives  18.5 us (17%)
  local copies, waits for them, and re-layouts  12.2 us (11%)
  other arithmetic  2.26 us (2%)
    all_to_all x1, blocking collectives, local(): big = lax.all_to_all(big.reshape(z.sp, own, z.wide), 'sp', 0, 0, tiled=True)  18.5 us
    pallas_call x1, Pallas kernels, local(): pl.pallas_call(functools.partial(first_kernel, z, steps, piece_steps), ou...  8.85 us
    pallas_call x1, Pallas kernels, local(): pl.pallas_call(functools.partial(second_kernel, z, steps, scale), out_sha...  8.45 us
    ppermute x3, waiting for transfers between devices, swap_sum(): lax.ppermute(values, axis, [(i, i ^ bit) for i in range(count)])  8.45 us
    ppermute x3, starting transfers between devices, ring_exchange(): ahead = lax.ppermute(ahead, 'sp', up)  5.39 us
    ppermute x3, starting transfers between devices, ring_exchange(): second = lax.ppermute(second, 'sp', down)  5.15 us
    ppermute x1, starting transfers between devices, local(): received = lax.ppermute(total, 'sec', swap)  4.83 us
    ppermute x3, starting transfers between devices, swap_sum(): lax.ppermute(values, axis, [(i, i ^ bit) for i in range(count)])  4.73 us
  transfers between devices with their start and end apart: 25, of which 11 were waited for; matrix products, arithmetic and copies ran while one was open for 9% of the time, Pallas kernels for 3%

profile of v3, /device:TPU:0, one launch (start us, length us, event | category | flops | bytes accessed | tf_op | source)
XLA Modules:
  0.0 107.8 jit_solution(9433893952013480310)
XLA Ops:
  0.6 3.0 %collective-permute-start.1 = (bf16[160,512]{1,0:T(8,128)(2,1)}, bf16[160,512]{1,0:T(8,128)(2,1)S(1)}, u32[]{:S(2)}, u32[]{:S(2)}) collective-permute-start(bf16[160,512]{1,0:T(8,128)(2,1)} %bitcast.37), channel_id=1, source_target_pairs={{4,0},{8,4},{12,8},{14,12},{10,14},{6,10},{2,6},{0,2},{5,1},{9,5},... | collective-permute-start | bytes 491528 | tf_op jit(solution)/shard_map/ppermute | solution.py:51
  5.2 2.7 %pieces.1 = (bf16[3,32,640]{2,1,0:T(8,128)(2,1)}, bf16[4,32,640]{2,1,0:T(8,128)(2,1)}, bf16[32,640]{1,0:T(8,128)(2,1)}) custom-call(bf16[9,64,512]{2,1,0:T(8,128)(2,1)} %bitcast.42, f32[32,128]{1,0:T(8,128)} %pad.16.codes), custom_call_target="tpu_custom_call" | custom-call | tf_op jit(solution)/shard_map/pieces/pallas_call | solution.py:550
  7.9 2.0 %collective-permute-start.8 = (bf16[3,32,640]{2,1,0:T(8,128)(2,1)}, bf16[3,32,640]{2,1,0:T(8,128)(2,1)S(1)}, u32[]{:S(2)}, u32[]{:S(2)}) collective-permute-start(bf16[3,32,640]{2,1,0:T(8,128)(2,1)} %get-tuple-element.19), channel_id=1, source_target_pairs={{0,4},{4,8},{8,12},{12,14},{14,10},{10,6},{6,2},{2,0},{1,5},{5,9},... | collective-permute-start | bytes 368648 | tf_op jit(solution)/shard_map/ppermute | solution.py:60
  11.3 1.6 %pad.17.refs_24_.refs_10_ = bf16[256,512]{1,0:T(8,128)(2,1)} pad(bf16[192,512]{1,0:T(8,128)(2,1)} %bitcast.43, bf16[]{:T(256)} %constant.6.clone.1), padding=0_64x0_0 | pad | bytes 458754 | tf_op jit(solution)/shard_map/jit(_pad)/pad | solution.py:565
  14.0 1.8 %collective-permute-start.10 = (bf16[2,32,640]{2,1,0:T(8,128)(2,1)S(1)}, bf16[2,32,640]{2,1,0:T(8,128)(2,1)S(1)}, u32[]{:S(2)}, u32[]{:S(2)}) collective-permute-start(bf16[2,32,640]{2,1,0:T(8,128)(2,1)S(1)} %slice.72), channel_id=1, source_target_pairs={{0,4},{4,8},{8,12},{12,14},{14,10},{10,6},{6,2},{2,0},{1,5},{5,9},... | collective-permute-start | bytes 245768 | tf_op jit(solution)/shard_map/ppermute | solution.py:60
  17.6 1.7 %collective-permute-start.3 = (bf16[160,512]{1,0:T(8,128)(2,1)S(1)}, bf16[160,512]{1,0:T(8,128)(2,1)S(1)}, u32[]{:S(2)}, u32[]{:S(2)}) collective-permute-start(bf16[160,512]{1,0:T(8,128)(2,1)S(1)} %collective-permute-done.1.refs_2_), channel_id=1, source_target_pairs={{4,0},{8,4},{12,8},{14,12},{10,14},{6,10},{2,6},{0,2},{5,1},{9,5},... | collective-permute-start | bytes 491528 | tf_op jit(solution)/shard_map/ppermute | solution.py:51
  21.0 1.6 %collective-permute-start.12 = (bf16[1,32,640]{2,1,0:T(8,128)(2,1)S(1)}, bf16[1,32,640]{2,1,0:T(8,128)(2,1)S(1)}, u32[]{:S(2)}, u32[]{:S(2)}) collective-permute-start(bf16[1,32,640]{2,1,0:T(8,128)(2,1)S(1)} %get-tuple-element.52), channel_id=1, source_target_pairs={{0,4},{4,8},{8,12},{12,14},{14,10},{10,6},{6,2},{2,0},{1,5},{5,9},... | collective-permute-start | bytes 122888 | tf_op jit(solution)/shard_map/ppermute | solution.py:60
  24.4 2.6 %collective-permute-done.3.refs_4_ = bf16[160,512]{1,0:T(8,128)(2,1)S(1)} collective-permute-done((bf16[160,512]{1,0:T(8,128)(2,1)S(1)}, bf16[160,512]{1,0:T(8,128)(2,1)S(1)}, u32[]{:S(2)}, u32[]{:S(2)}) %collective-permute-start.3) | collective-permute-done | bytes 163872 | tf_op jit(solution)/shard_map/ppermute | solution.py:51
  28.3 1.6 %collective-permute-start.4 = (bf16[160,512]{1,0:T(8,128)(2,1)S(1)}, bf16[160,512]{1,0:T(8,128)(2,1)S(1)}, u32[]{:S(2)}, u32[]{:S(2)}) collective-permute-start(bf16[160,512]{1,0:T(8,128)(2,1)S(1)} %collective-permute-done.2.refs_3_), channel_id=1, source_target_pairs={{0,4},{4,8},{8,12},{12,14},{14,10},{10,6},{6,2},{2,0},{1,5},{5,9},... | collective-permute-start | bytes 491528 | tf_op jit(solution)/shard_map/ppermute | solution.py:47
  31.7 2.8 %collective-permute-done.13 = bf16[1,32,640]{2,1,0:T(8,128)(2,1)S(1)} collective-permute-done((bf16[1,32,640]{2,1,0:T(8,128)(2,1)S(1)}, bf16[1,32,640]{2,1,0:T(8,128)(2,1)S(1)}, u32[]{:S(2)}, u32[]{:S(2)}) %collective-permute-start.13) | collective-permute-done | bytes 40992 | tf_op jit(solution)/shard_map/ppermute | solution.py:55
  34.5 1.6 %collective-permute-start.6 = (bf16[160,512]{1,0:T(8,128)(2,1)S(1)}, bf16[160,512]{1,0:T(8,128)(2,1)S(1)}, u32[]{:S(2)}, u32[]{:S(2)}) collective-permute-start(bf16[160,512]{1,0:T(8,128)(2,1)S(1)} %collective-permute-done.4.refs_5_), channel_id=1, source_target_pairs={{0,4},{4,8},{8,12},{12,14},{14,10},{10,6},{6,2},{2,0},{1,5},{5,9},... | collective-permute-start | bytes 491528 | tf_op jit(solution)/shard_map/ppermute | solution.py:47
  36.8 4.3 %collective-permute-done.6.refs_7_ = bf16[160,512]{1,0:T(8,128)(2,1)S(1)} collective-permute-done((bf16[160,512]{1,0:T(8,128)(2,1)S(1)}, bf16[160,512]{1,0:T(8,128)(2,1)S(1)}, u32[]{:S(2)}, u32[]{:S(2)}) %collective-permute-start.6) | collective-permute-done | bytes 163872 | tf_op jit(solution)/shard_map/ppermute | solution.py:47
  41.9 8.9 %first.1 = (f32[8,1280]{1,0:T(8,128)}, bf16[1280,256]{1,0:T(8,128)(2,1)}, f32[8,160,128]{2,1,0:T(8,128)}, bf16[8,160,128]{2,1,0:T(8,128)(2,1)}, bf16[512,640]{1,0:T(8,128)(2,1)}, /*index=5*/bf16[1280,128]{1,0:T(8,128)(2,1)}) custom-call(bf16[160,512]{1,0:T(8,128)(2,1)} %bitcast.39, bf16[160,512]{1,0:T(8,128)(2,1)} %copy-done.2, bf16[160,512]{1,0:T(8,128)(2,1)} %copy-done.1, ...), custom_call_target="tpu_custom_call" | custom-call | tf_op jit(solution)/shard_map/first/pallas_call | solution.py:570
  51.3 3.8 %collective-permute-done.19 = f32[8,1280]{1,0:T(8,128)S(1)} collective-permute-done((f32[8,1280]{1,0:T(8,128)}, f32[8,1280]{1,0:T(8,128)S(1)}, u32[]{:S(2)}, u32[]{:S(2)}) %collective-permute-start.19) | collective-permute-done | bytes 40992 | tf_op jit(solution)/shard_map/ppermute | solution.py:74
  55.8 1.6 %collective-permute-start.20 = (f32[8,1280]{1,0:T(8,128)S(1)}, f32[8,1280]{1,0:T(8,128)S(1)}, u32[]{:S(2)}, u32[]{:S(2)}) collective-permute-start(f32[8,1280]{1,0:T(8,128)S(1)} %add.18), channel_id=1, source_target_pairs={{0,4},{2,6},{4,0},{6,2},{8,12},{10,14},{12,8},{14,10},{1,5},{3,7},... | collective-permute-start | bytes 122888 | tf_op jit(solution)/shard_map/ppermute | solution.py:74
  57.4 2.4 %collective-permute-done.20 = f32[8,1280]{1,0:T(8,128)S(1)} collective-permute-done((f32[8,1280]{1,0:T(8,128)S(1)}, f32[8,1280]{1,0:T(8,128)S(1)}, u32[]{:S(2)}, u32[]{:S(2)}) %collective-permute-start.20) | collective-permute-done | bytes 40992 | tf_op jit(solution)/shard_map/ppermute | solution.py:74
  59.8 2.6 %collective-permute-start.21 = (f32[8,1280]{1,0:T(8,128)S(1)}, f32[8,1280]{1,0:T(8,128)S(1)}, u32[]{:S(2)}, u32[]{:S(2)}) collective-permute-start(f32[8,1280]{1,0:T(8,128)S(1)} %add.19), channel_id=1, source_target_pairs={{0,8},{2,10},{4,12},{6,14},{8,0},{10,2},{12,4},{14,6},{1,9},{3,11}... | collective-permute-start | bytes 122888 | tf_op jit(solution)/shard_map/ppermute | solution.py:74
  62.5 2.3 %collective-permute-done.21 = f32[8,1280]{1,0:T(8,128)S(1)} collective-permute-done((f32[8,1280]{1,0:T(8,128)S(1)}, f32[8,1280]{1,0:T(8,128)S(1)}, u32[]{:S(2)}, u32[]{:S(2)}) %collective-permute-start.21) | collective-permute-done | bytes 40992 | tf_op jit(solution)/shard_map/ppermute | solution.py:74
  64.7 4.8 %collective-permute-start.22 = (f32[8,1280]{1,0:T(8,128)S(1)}, f32[8,1280]{1,0:T(8,128)S(1)}, u32[]{:S(2)}, u32[]{:S(2)}) collective-permute-start(f32[8,1280]{1,0:T(8,128)S(1)} %add.20.refs_16_), channel_id=1, source_target_pairs={{0,16},{16,0},{1,17},{17,1},{2,18},{18,2},{3,19},{19,3},{4,20},{20... | collective-permute-start | bytes 122888 | tf_op jit(solution)/shard_map/ppermute | solution.py:598
  69.6 2.0 %collective-permute-done.22.refs_17_ = f32[8,1280]{1,0:T(8,128)S(1)} collective-permute-done((f32[8,1280]{1,0:T(8,128)S(1)}, f32[8,1280]{1,0:T(8,128)S(1)}, u32[]{:S(2)}, u32[]{:S(2)}) %collective-permute-start.22) | collective-permute-done | bytes 40992 | tf_op jit(solution)/shard_map/ppermute | solution.py:598
  72.2 8.5 %second.1 = (bf16[512,640]{1,0:T(8,128)(2,1)}, f32[192,512]{1,0:T(8,128)}, f32[8,512]{1,0:T(8,128)}) custom-call(bf16[160,512]{1,0:T(8,128)(2,1)} %bitcast.40, bf16[160,512]{1,0:T(8,128)(2,1)} %copy-done.2, bf16[160,512]{1,0:T(8,128)(2,1)} %copy-done.1, bf16[160,512]{1,0:T(8,128)(2,1)} %copy-done.4, bf16[160,512]{1,0:T(8,128)(2,1)} %copy-done.3, ...), custom_call_target="tpu_custom_call" | custom-call | tf_op jit(solution)/shard_map/second/pallas_call | solution.py:599
  80.6 18.5 %all_to_all.5.mine = bf16[8,64,640]{2,1,0:T(8,128)(2,1)S(1)} all-to-all(bf16[8,64,640]{2,1,0:T(8,128)(2,1)} %bitcast.41), channel_id=1, replica_groups=mesh['sec'=2,'sp'=8,'dp'=2] {'sp'}, dimensions={0} | all-to-all | bytes 1310720 | tf_op jit(solution)/shard_map/all_to_all | solution.py:618
  99.6 2.1 %collective-permute-done.24.time_other = f32[192,512]{1,0:T(8,128)S(1)} collective-permute-done((f32[192,512]{1,0:T(8,128)S(1)}, f32[192,512]{1,0:T(8,128)S(1)}, u32[]{:S(2)}, u32[]{:S(2)}) %collective-permute-start.24) | collective-permute-done | bytes 393248 | tf_op jit(solution)/shard_map/ppermute | solution.py:630
  103.4 3.0 %last.1 = (f32[9,64,512]{2,1,0:T(8,128)}, f32[192,512]{1,0:T(8,128)}, f32[8,512]{1,0:T(8,128)}) custom-call(bf16[8,64,640]{2,1,0:T(8,128)(2,1)} %copy-done, bf16[8,64,640]{2,1,0:T(8,128)(2,1)} %copy-done.8, f32[192,512]{1,0:T(8,128)} %get-tuple-element.27.time_mine, f32[192,512]{1,0:T(8,128)} %copy-done.10), custom_call_target="tpu_custom_call" | custom-call | tf_op jit(solution)/shard_map/last/pallas_call | solution.py:619
  (95 shorter events, 19.0 us)
Async XLA Ops:
  0.6 16.6 %collective-permute-start.1 = (bf16[160,512]{1,0:T(8,128)(2,1)}, bf16[160,512]{1,0:T(8,128)(2,1)S(1)}, u32[]{:S(2)}, u32[]{:S(2)}) collective-permute-start(bf16[160,512]{1,0:T(8,128)(2,1)} %bitcast.37), channel_id=1, source_target_pairs={{4,0},{8,4},{12,8},{14,12},{10,14},{6,10},{2,6},{0,2},{5,1},{9,5},... | collective-permute-start | bytes 491528 | tf_op jit(solution)/shard_map/ppermute | solution.py:51
  3.7 13.9 %collective-permute-start = (bf16[160,512]{1,0:T(8,128)(2,1)}, bf16[160,512]{1,0:T(8,128)(2,1)S(1)}, u32[]{:S(2)}, u32[]{:S(2)}) collective-permute-start(bf16[160,512]{1,0:T(8,128)(2,1)} %bitcast.38), channel_id=1, source_target_pairs={{0,4},{4,8},{8,12},{12,14},{14,10},{10,6},{6,2},{2,0},{1,5},{5,9},... | collective-permute-start | bytes 491528 | tf_op jit(solution)/shard_map/ppermute | solution.py:47
  7.9 28.9 %collective-permute-start.14 = (bf16[32,640]{1,0:T(8,128)(2,1)}, bf16[32,640]{1,0:T(8,128)(2,1)S(1)}, u32[]{:S(2)}, u32[]{:S(2)}) collective-permute-start(bf16[32,640]{1,0:T(8,128)(2,1)} %get-tuple-element.17.refs_8_), channel_id=1, source_target_pairs={{0,1},{1,0},{2,3},{3,2},{4,5},{5,4},{6,7},{7,6},{8,9},{9,8},{10,11... | collective-permute-start | bytes 122888 | tf_op jit(solution)/shard_map/ppermute | solution.py:44
  7.9 6.1 %collective-permute-start.8 = (bf16[3,32,640]{2,1,0:T(8,128)(2,1)}, bf16[3,32,640]{2,1,0:T(8,128)(2,1)S(1)}, u32[]{:S(2)}, u32[]{:S(2)}) collective-permute-start(bf16[3,32,640]{2,1,0:T(8,128)(2,1)} %get-tuple-element.19), channel_id=1, source_target_pairs={{0,4},{4,8},{8,12},{12,14},{14,10},{10,6},{6,2},{2,0},{1,5},{5,9},... | collective-permute-start | bytes 368648 | tf_op jit(solution)/shard_map/ppermute | solution.py:60
  9.9 6.6 %collective-permute-start.7 = (bf16[4,32,640]{2,1,0:T(8,128)(2,1)}, bf16[4,32,640]{2,1,0:T(8,128)(2,1)S(1)}, u32[]{:S(2)}, u32[]{:S(2)}) collective-permute-start(bf16[4,32,640]{2,1,0:T(8,128)(2,1)} %get-tuple-element.18), channel_id=1, source_target_pairs={{4,0},{8,4},{12,8},{14,12},{10,14},{6,10},{2,6},{0,2},{5,1},{9,5},... | collective-permute-start | bytes 491528 | tf_op jit(solution)/shard_map/ppermute | solution.py:55
  14.0 5.3 %collective-permute-start.10 = (bf16[2,32,640]{2,1,0:T(8,128)(2,1)S(1)}, bf16[2,32,640]{2,1,0:T(8,128)(2,1)S(1)}, u32[]{:S(2)}, u32[]{:S(2)}) collective-permute-start(bf16[2,32,640]{2,1,0:T(8,128)(2,1)S(1)} %slice.72), channel_id=1, source_target_pairs={{0,4},{4,8},{8,12},{12,14},{14,10},{10,6},{6,2},{2,0},{1,5},{5,9},... | collective-permute-start | bytes 245768 | tf_op jit(solution)/shard_map/ppermute | solution.py:60
  17.1 3.8 %collective-permute-start.15 = (bf16[2,32,640]{2,1,0:T(8,128)(2,1)S(1)}, bf16[2,32,640]{2,1,0:T(8,128)(2,1)S(1)}, u32[]{:S(2)}, u32[]{:S(2)}) collective-permute-start(bf16[2,32,640]{2,1,0:T(8,128)(2,1)S(1)} %pad_maximum_fusion), channel_id=1, source_target_pairs={{0,1},{1,0},{2,3},{3,2},{4,5},{5,4},{6,7},{7,6},{8,9},{9,8},{10,11... | collective-permute-start | bytes 245768 | tf_op jit(solution)/shard_map/ppermute | solution.py:64
  17.3 6.2 %collective-permute-start.9 = (bf16[3,32,640]{2,1,0:T(8,128)(2,1)S(1)}, bf16[3,32,640]{2,1,0:T(8,128)(2,1)S(1)}, u32[]{:S(2)}, u32[]{:S(2)}) collective-permute-start(bf16[3,32,640]{2,1,0:T(8,128)(2,1)S(1)} %slice.70), channel_id=1, source_target_pairs={{4,0},{8,4},{12,8},{14,12},{10,14},{6,10},{2,6},{0,2},{5,1},{9,5},... | collective-permute-start | bytes 368648 | tf_op jit(solution)/shard_map/ppermute | solution.py:55
  17.6 9.4 %collective-permute-start.3 = (bf16[160,512]{1,0:T(8,128)(2,1)S(1)}, bf16[160,512]{1,0:T(8,128)(2,1)S(1)}, u32[]{:S(2)}, u32[]{:S(2)}) collective-permute-start(bf16[160,512]{1,0:T(8,128)(2,1)S(1)} %collective-permute-done.1.refs_2_), channel_id=1, source_target_pairs={{4,0},{8,4},{12,8},{14,12},{10,14},{6,10},{2,6},{0,2},{5,1},{9,5},... | collective-permute-start | bytes 491528 | tf_op jit(solution)/shard_map/ppermute | solution.py:51
  19.3 7.7 %collective-permute-start.2 = (bf16[160,512]{1,0:T(8,128)(2,1)S(1)}, bf16[160,512]{1,0:T(8,128)(2,1)S(1)}, u32[]{:S(2)}, u32[]{:S(2)}) collective-permute-start(bf16[160,512]{1,0:T(8,128)(2,1)S(1)} %collective-permute-done.refs_1_), channel_id=1, source_target_pairs={{0,4},{4,8},{8,12},{12,14},{14,10},{10,6},{6,2},{2,0},{1,5},{5,9},... | collective-permute-start | bytes 491528 | tf_op jit(solution)/shard_map/ppermute | solution.py:47
  21.0 9.5 %collective-permute-start.12 = (bf16[1,32,640]{2,1,0:T(8,128)(2,1)S(1)}, bf16[1,32,640]{2,1,0:T(8,128)(2,1)S(1)}, u32[]{:S(2)}, u32[]{:S(2)}) collective-permute-start(bf16[1,32,640]{2,1,0:T(8,128)(2,1)S(1)} %get-tuple-element.52), channel_id=1, source_target_pairs={{0,4},{4,8},{8,12},{12,14},{14,10},{10,6},{6,2},{2,0},{1,5},{5,9},... | collective-permute-start | bytes 122888 | tf_op jit(solution)/shard_map/ppermute | solution.py:60
  23.4 4.9 %collective-permute-start.11 = (bf16[2,32,640]{2,1,0:T(8,128)(2,1)S(1)}, bf16[2,32,640]{2,1,0:T(8,128)(2,1)S(1)}, u32[]{:S(2)}, u32[]{:S(2)}) collective-permute-start(bf16[2,32,640]{2,1,0:T(8,128)(2,1)S(1)} %slice.74), channel_id=1, source_target_pairs={{4,0},{8,4},{12,8},{14,12},{10,14},{6,10},{2,6},{0,2},{5,1},{9,5},... | collective-permute-start | bytes 245768 | tf_op jit(solution)/shard_map/ppermute | solution.py:55
  27.0 4.0 %collective-permute-start.16 = (bf16[2,32,640]{2,1,0:T(8,128)(2,1)S(1)}, bf16[2,32,640]{2,1,0:T(8,128)(2,1)S(1)}, u32[]{:S(2)}, u32[]{:S(2)}) collective-permute-start(bf16[2,32,640]{2,1,0:T(8,128)(2,1)S(1)} %pad_maximum_fusion.1), channel_id=1, source_target_pairs={{0,1},{1,0},{2,3},{3,2},{4,5},{5,4},{6,7},{7,6},{8,9},{9,8},{10,11... | collective-permute-start | bytes 245768 | tf_op jit(solution)/shard_map/ppermute | solution.py:64
  27.0 9.8 %collective-permute-start.5 = (bf16[160,512]{1,0:T(8,128)(2,1)S(1)}, bf16[160,512]{1,0:T(8,128)(2,1)S(1)}, u32[]{:S(2)}, u32[]{:S(2)}) collective-permute-start(bf16[160,512]{1,0:T(8,128)(2,1)S(1)} %collective-permute-done.3.refs_4_), channel_id=1, source_target_pairs={{4,0},{8,4},{12,8},{14,12},{10,14},{6,10},{2,6},{0,2},{5,1},{9,5},... | collective-permute-start | bytes 491528 | tf_op jit(solution)/shard_map/ppermute | solution.py:51
  28.3 6.2 %collective-permute-start.4 = (bf16[160,512]{1,0:T(8,128)(2,1)S(1)}, bf16[160,512]{1,0:T(8,128)(2,1)S(1)}, u32[]{:S(2)}, u32[]{:S(2)}) collective-permute-start(bf16[160,512]{1,0:T(8,128)(2,1)S(1)} %collective-permute-done.2.refs_3_), channel_id=1, source_target_pairs={{0,4},{4,8},{8,12},{12,14},{14,10},{10,6},{6,2},{2,0},{1,5},{5,9},... | collective-permute-start | bytes 491528 | tf_op jit(solution)/shard_map/ppermute | solution.py:47
  30.5 4.0 %collective-permute-start.13 = (bf16[1,32,640]{2,1,0:T(8,128)(2,1)S(1)}, bf16[1,32,640]{2,1,0:T(8,128)(2,1)S(1)}, u32[]{:S(2)}, u32[]{:S(2)}) collective-permute-start(bf16[1,32,640]{2,1,0:T(8,128)(2,1)S(1)} %get-tuple-element.47), channel_id=1, source_target_pairs={{4,0},{8,4},{12,8},{14,12},{10,14},{6,10},{2,6},{0,2},{5,1},{9,5},... | collective-permute-start | bytes 122888 | tf_op jit(solution)/shard_map/ppermute | solution.py:55
  31.0 5.2 %collective-permute-start.17 = (bf16[2,32,640]{2,1,0:T(8,128)(2,1)S(1)}, bf16[2,32,640]{2,1,0:T(8,128)(2,1)S(1)}, u32[]{:S(2)}, u32[]{:S(2)}) collective-permute-start(bf16[2,32,640]{2,1,0:T(8,128)(2,1)S(1)} %pad_maximum_fusion.2), channel_id=1, source_target_pairs={{0,1},{1,0},{2,3},{3,2},{4,5},{5,4},{6,7},{7,6},{8,9},{9,8},{10,11... | collective-permute-start | bytes 245768 | tf_op jit(solution)/shard_map/ppermute | solution.py:64
  34.5 6.6 %collective-permute-start.6 = (bf16[160,512]{1,0:T(8,128)(2,1)S(1)}, bf16[160,512]{1,0:T(8,128)(2,1)S(1)}, u32[]{:S(2)}, u32[]{:S(2)}) collective-permute-start(bf16[160,512]{1,0:T(8,128)(2,1)S(1)} %collective-permute-done.4.refs_5_), channel_id=1, source_target_pairs={{0,4},{4,8},{8,12},{12,14},{14,10},{10,6},{6,2},{2,0},{1,5},{5,9},... | collective-permute-start | bytes 491528 | tf_op jit(solution)/shard_map/ppermute | solution.py:47
  50.8 4.3 %collective-permute-start.19 = (f32[8,1280]{1,0:T(8,128)}, f32[8,1280]{1,0:T(8,128)S(1)}, u32[]{:S(2)}, u32[]{:S(2)}) collective-permute-start(f32[8,1280]{1,0:T(8,128)} %get-tuple-element.25), channel_id=1, source_target_pairs={{0,2},{2,0},{4,6},{6,4},{8,10},{10,8},{12,14},{14,12},{1,3},{3,1},... | collective-permute-start | bytes 122888 | tf_op jit(solution)/shard_map/ppermute | solution.py:74
  55.8 4.0 %collective-permute-start.20 = (f32[8,1280]{1,0:T(8,128)S(1)}, f32[8,1280]{1,0:T(8,128)S(1)}, u32[]{:S(2)}, u32[]{:S(2)}) collective-permute-start(f32[8,1280]{1,0:T(8,128)S(1)} %add.18), channel_id=1, source_target_pairs={{0,4},{2,6},{4,0},{6,2},{8,12},{10,14},{12,8},{14,10},{1,5},{3,7},... | collective-permute-start | bytes 122888 | tf_op jit(solution)/shard_map/ppermute | solution.py:74
  59.8 4.9 %collective-permute-start.21 = (f32[8,1280]{1,0:T(8,128)S(1)}, f32[8,1280]{1,0:T(8,128)S(1)}, u32[]{:S(2)}, u32[]{:S(2)}) collective-permute-start(f32[8,1280]{1,0:T(8,128)S(1)} %add.19), channel_id=1, source_target_pairs={{0,8},{2,10},{4,12},{6,14},{8,0},{10,2},{12,4},{14,6},{1,9},{3,11}... | collective-permute-start | bytes 122888 | tf_op jit(solution)/shard_map/ppermute | solution.py:74
  64.7 6.8 %collective-permute-start.22 = (f32[8,1280]{1,0:T(8,128)S(1)}, f32[8,1280]{1,0:T(8,128)S(1)}, u32[]{:S(2)}, u32[]{:S(2)}) collective-permute-start(f32[8,1280]{1,0:T(8,128)S(1)} %add.20.refs_16_), channel_id=1, source_target_pairs={{0,16},{16,0},{1,17},{17,1},{2,18},{18,2},{3,19},{19,3},{4,20},{20... | collective-permute-start | bytes 122888 | tf_op jit(solution)/shard_map/ppermute | solution.py:598
  99.1 2.7 %collective-permute-start.23 = (bf16[8,64,640]{2,1,0:T(8,128)(2,1)S(1)}, bf16[8,64,640]{2,1,0:T(8,128)(2,1)S(1)}, u32[]{:S(2)}, u32[]{:S(2)}) collective-permute-start(bf16[8,64,640]{2,1,0:T(8,128)(2,1)S(1)} %all_to_all.5.mine), channel_id=1, source_target_pairs={{0,1},{1,0},{2,3},{3,2},{4,5},{5,4},{6,7},{7,6},{8,9},{9,8},{10,11... | collective-permute-start | bytes 1966088 | tf_op jit(solution)/shard_map/ppermute | solution.py:630
  99.1 2.7 %collective-permute-start.24 = (f32[192,512]{1,0:T(8,128)S(1)}, f32[192,512]{1,0:T(8,128)S(1)}, u32[]{:S(2)}, u32[]{:S(2)}) collective-permute-start(f32[192,512]{1,0:T(8,128)S(1)} %copy-done.9), channel_id=1, source_target_pairs={{0,1},{1,0},{2,3},{3,2},{4,5},{5,4},{6,7},{7,6},{8,9},{9,8},{10,11... | collective-permute-start | bytes 1179656 | tf_op jit(solution)/shard_map/ppermute | solution.py:630
  (19 other events, 165.2 us)

commit v4 on v3

--- a/solution.py
+++ b/solution.py
@@ -13,7 +13,6 @@
 NN = (((1,), (0,)), ((), ()))
 NT = (((1,), (1,)), ((), ()))
 TN = (((0,), (0,)), ((), ()))
-VMEM_BYTES = 56 * 1024 * 1024
 
 
 def up_to(value, multiple):
@@ -39,31 +38,34 @@
     count = lax.axis_size("sp")
     up, down = ring_maps(count)
     swap = [(0, 1), (1, 0)]
-    first = shard
     shards, shard_steps = [shard], [0]
-    mine, other, piece_steps = [own_piece], [lax.ppermute(own_piece, "dp", swap)], [0]
-    second = shard
+    mine, piece_steps, other = [own_piece], [0], []
+    first = second = shard
+
+    def meet():
+        fresh = mine[len(other) :]
+        both = lax.ppermute(jnp.stack(fresh), "dp", swap)
+        other.extend(both[i] for i in range(len(fresh)))
+
     for step in range(1, count // 2 + 1):
         first = lax.ppermute(first, "sp", up)
         shards.append(first)
         shard_steps.append(-step)
-        if step < count - step:
+        last = step == count - step
+        if not last:
             second = lax.ppermute(second, "sp", down)
             shards.append(second)
             shard_steps.append(step)
-        fresh = []
+            ahead = lax.ppermute(ahead, "sp", up)
+            mine.append(ahead[0])
+            piece_steps.append(-step)
+            ahead = ahead[1:]
         behind = lax.ppermute(behind, "sp", down)
-        fresh.append(behind[0])
+        mine.append(behind[0])
         piece_steps.append(step)
         behind = behind[1:]
-        if step < count - step:
-            ahead = lax.ppermute(ahead, "sp", up)
-            fresh.append(ahead[0])
-            piece_steps.append(-step)
-            ahead = ahead[1:]
-        both = lax.ppermute(jnp.stack(fresh), "dp", swap)
-        mine += fresh
-        other += [both[i] for i in range(len(fresh))]
+        if last or step % 2 == 0:
+            meet()
     return shards, shard_steps, mine, other, piece_steps
 
 
@@ -138,7 +140,8 @@
         self.row = frames * cols
         self.count = sp * self.row
         self.wide = up_to(9 * own, LANES)
-        self.thin = up_to(3 * own, LANES)
+        self.thin = up_to(3 * own + 8, LANES)
+        self.copies = min(3, LANES // own)
         self.half = own // 2
         code_rows = frames * lat
         self.code_rows = up_to(code_rows, 16)
@@ -152,38 +155,52 @@
         self.carries = self.wide - 9 * own >= LANES // 2 and own * (LANES // 2) >= 8 * chans
 
 
-def load_shards(z, steps, shards, v, sems):
+def place_shards(z, steps, shards, v):
     place = ring_place(lax.axis_index("sp"), z.sp)
-    started = []
-    for k, (shard, step) in enumerate(zip(shards, steps)):
-        row = ring_device(place + step, z.sp)
-        copy = pltpu.make_async_copy(shard, v.at[rows_at(row, z)], sems.at[k])
-        copy.start()
-        started.append(copy)
-    return started
-
-
-def load_pieces(z, steps, mine, other, halves, codes, sems):
+    for shard, step in zip(shards, steps):
+        v[rows_at(ring_device(place + step, z.sp), z)] = shard[...]
+
+
+def place_pieces(z, steps, mine, other, w_cat, codes):
     place = ring_place(lax.axis_index("sp"), z.sp)
     core = lax.axis_index("dp")
-    started = []
-    for k, (one, two, step) in enumerate(zip(mine, other, steps)):
-        row = ring_device(place + step, z.sp)
-        for at, (source, target) in enumerate(
-            (
-                (one.at[pl.ds(0, z.half_pad)], halves.at[row, core]),
-                (two.at[pl.ds(0, z.half_pad)], halves.at[row, 1 - core]),
-                (one.at[pl.ds(z.code_row, z.code_rows)], codes.at[row]),
-            )
-        ):
-            copy = pltpu.make_async_copy(source, target, sems.at[at, k])
-            copy.start()
-            started.append(copy)
-    return started
+    for one, two, step in zip(mine, other, steps):
+        device = ring_device(place + step, z.sp)
+        start = pl.multiple_of(device * z.own, z.own)
+        codes[device] = one[z.code_row : z.code_row + z.code_rows]
+        low = jnp.where(core == 0, one[: z.half], two[: z.half])
+        high = jnp.where(core == 0, two[: z.half], one[: z.half])
+        if z.half == z.half_pad:
+            w_cat[pl.ds(start, z.half)] = low
+            w_cat[pl.ds(start + z.half, z.half)] = high
+        else:
+            both = jnp.concatenate([low.astype(F32), high.astype(F32)], axis=0)
+            w_cat[pl.ds(start, z.own)] = both.astype(BF16)
+
+
+def each_row(z, body):
+    if z.sp <= 8:
+        for r in range(z.sp):
+            body(r)
+    else:
+
+        def step(r, carry):
+            body(r)
+            return carry
+
+        lax.fori_loop(0, z.sp, step, 0)
 
 
 def rows_at(r, z):
+    if isinstance(r, int):
+        return pl.ds(r * z.row, z.row)
     return pl.ds(pl.multiple_of(r * z.row, z.row), z.row)
+
+
+def rows_from(r0, rows, z):
+    if isinstance(r0, int):
+        return pl.ds(r0 * z.row, rows * z.row)
+    return pl.ds(pl.multiple_of(r0 * z.row, rows * z.row), rows * z.row)
 
 
 def conv_row(z, taps, r):
@@ -220,15 +237,14 @@
 
 
 def spread(z, shifts, inner_cat):
-    def body(r, carry):
+    def body(r):
         pieces = [
             shifts[j, r + 2 - i].astype(F32) for i in range(3) for j in range(3)
         ]
         for b, block in enumerate(merge(pieces, z.own)):
             inner_cat[rows_at(r, z), b * LANES : (b + 1) * LANES] = block.astype(BF16)
-        return carry
-
-    lax.fori_loop(0, z.sp, body, 0)
+
+    each_row(z, body)
 
 
 def zero_ends(z, padded):
@@ -252,7 +268,7 @@
 def position_codes(z, codes, out):
     block, offset = z.code_lane // LANES, z.code_lane % LANES
 
-    def body(r, carry):
+    def body(r):
         raw = codes[r, :, block * LANES : (block + 1) * LANES].astype(F32)
         raw = jnp.concatenate([raw, jnp.zeros((LANES - z.code_rows, LANES), F32)], axis=0)
         turned = raw.T[offset : offset + z.cols]
@@ -265,9 +281,8 @@
                 values + pltpu.roll(values, 16, 1) + pltpu.roll(values, 32, 1)
             )
         out[rows_at(r, z)] = jnp.concatenate(frames, axis=0).astype(BF16)
-        return carry
-
-    lax.fori_loop(0, z.sp, body, 0)
+
+    each_row(z, body)
 
 
 def piece_kernel(z, w, codes, ahead, behind, own_piece):
@@ -324,23 +339,13 @@
     n = z.sp
     shards, mine, other = refs[:n], refs[n : 2 * n], refs[2 * n : 3 * n]
     wt, proj, halves = refs[3 * n : 3 * n + 3]
-    part, hid_cat, slope, inner_out, w_cat, pos = refs[3 * n + 3 : 3 * n + 9]
-    v, w_halves, codes, taps, shifts, inner_cat, thin, sems, piece_sems = refs[3 * n + 9 :]
-    started = load_pieces(z, piece_steps, mine, other, w_halves, codes, piece_sems)
-    started += load_shards(z, steps, shards, v, sems)
+    part, hid_cat, slope, inner_out, w_cat, pos, v = refs[3 * n + 3 : 3 * n + 10]
+    codes, taps, back, spots_of, thin = refs[3 * n + 10 :]
     decoder = lax.axis_index("sec") == 1
     first = lax.axis_index("sp") == 0
     zero_ends(z, taps)
-    for copy in started:
-        copy.wait()
-    if z.half == z.half_pad:
-        w_cat[...] = w_halves[...].reshape(z.chans, z.wide)
-    else:
-        for j in range(z.sp):
-            for core in range(2):
-                rows = slice(j * z.own + core * z.half, j * z.own + (core + 1) * z.half)
-                w_cat[rows] = w_halves[j, core, : z.half]
-    whole = dot(proj[...], v[...], NT)[:8]
+    place_shards(z, steps, shards, v)
+    place_pieces(z, piece_steps, mine, other, w_cat, codes)
 
     def store_hidden(pre, logistic, r):
         hidden = keep_own(z, (pre * logistic).astype(BF16).astype(F32))
@@ -348,14 +353,9 @@
         for b, block in enumerate(merge(moved, z.own)):
             hid_cat[rows_at(r, z), b * LANES : (b + 1) * LANES] = block.astype(BF16)
 
-    def finish(weights, cat):
-        partial = sum3(dot(stack3(weights[:8]), cat, NT))
-        part[...] = partial + jnp.where(first, whole, 0.0)
-
     @pl.when(decoder)
     def _():
-        for j in range(3):
-            zero_ends(z, shifts.at[j])
+        zero_ends(z, back)
         p_cat = dot(proj[...], w_cat[...], NN)
         half = halves[:, :1]
         row = lax.broadcasted_iota(jnp.int32, p_cat.shape, 0)
@@ -366,62 +366,82 @@
             list(thirds(scaled)) + [jnp.zeros((LANES - 48, z.wide), F32)], axis=0
         ).astype(BF16)
         position_codes(z, codes, pos)
+        by_tap = [
+            keep_own(z, lanes_down(p_cat[:8, block * LANES : (block + 1) * LANES], offset))
+            for block, offset in spots(9, z.own)
+        ]
+        by_tap = jnp.concatenate(by_tap + [jnp.zeros((LANES - 72, LANES), F32)], axis=0)
+        by_tap = sum(
+            lanes_down(term, -c * z.own) for c, term in enumerate(thirds(by_tap)[: z.copies])
+        ).astype(BF16)
 
         def block(r0, rows):
-            place = pl.ds(pl.multiple_of(r0 * z.row, rows * z.row), rows * z.row)
+            place = rows_from(r0, rows, z)
             taps[pl.ds(r0 + 1, rows)] = dot(pos[place], table, NN).reshape(rows, z.row, z.wide)
             thin[place] = dot(v[place], wt[...], NT)
 
         in_blocks(z, block)
 
-        def body(r, carry):
+        def body(r):
             pre = conv_row(z, taps, r)
             logistic = 1.0 / (1.0 + jnp.exp(-pre))
             store_hidden(pre, logistic, r)
             rate = logistic * (1.0 + pre * (1.0 - logistic))
             inner = keep_own(z, (later_row(z, thin, r) * rate).astype(BF16).astype(F32))
-            put_shifts(z, inner, shifts, r)
             inner_out[r] = inner.astype(BF16)
-            return carry
-
-        lax.fori_loop(0, z.sp, body, 0)
-        spread(z, shifts, inner_cat)
-        finish(p_cat, inner_cat[...])
+            many = sum(lanes_down(inner, -c * z.own) for c in range(z.copies))
+            back[r + 1] = dot(many.astype(BF16), by_tap, NT)
+
+        each_row(z, body)
+        block_of, offset = (3 * z.own) // LANES, (3 * z.own) % LANES
+
+        def collect(r):
+            lane = lax.broadcasted_iota(jnp.int32, (z.row, LANES), 1)
+            value = jnp.where(lane < 24, back[r + 2], jnp.where(lane < 48, back[r + 1], back[r]))
+            j = (lane // 8) % 3
+            moved = jnp.where(
+                j == 0,
+                col_move(value, -1, z.cols),
+                jnp.where(j == 1, value, col_move(value, 1, z.cols)),
+            )
+            whole = thin[rows_at(r, z), block_of * LANES : (block_of + 1) * LANES]
+            whole = jnp.where(first, lanes_down(whole, offset - 72), 0.0)
+            spots_of[rows_at(r, z)] = jnp.where(lane < 72, moved, whole)
+
+        each_row(z, collect)
+        turned = spots_of[...].T
+        part[...] = sum(turned[8 * g : 8 * g + 8] for g in range(10))
 
     @pl.when(jnp.logical_not(decoder))
     def _():
         def block(r0, rows):
-            place = pl.ds(pl.multiple_of(r0 * z.row, rows * z.row), rows * z.row)
+            place = rows_from(r0, rows, z)
             taps[pl.ds(r0 + 1, rows)] = dot(v[place], w_cat[...], NN).reshape(
                 rows, z.row, z.wide
             )
 
         in_blocks(z, block)
 
-        def body(r, carry):
+        def body(r):
             pre = conv_row(z, taps, r)
             logistic = 1.0 / (1.0 + jnp.exp(-pre))
             store_hidden(pre, logistic, r)
             slope[r] = logistic * (1.0 + pre * (1.0 - logistic))
-            return carry
-
-        lax.fori_loop(0, z.sp, body, 0)
-        finish(dot(proj[...], wt[...], NT), hid_cat[...])
-
-
-def second_kernel(z, steps, scale, *refs):
-    n = len(steps)
-    shards = refs[:n]
-    w_cat, pos, wt, proj, halves, hid_cat, slope, inner_in, total, received = refs[n : n + 10]
-    big, time, part = refs[n + 10 : n + 13]
-    v, shifts, inner_cat, thin, sems = refs[n + 13 :]
-    started = load_shards(z, steps, shards, v, sems)
+
+        each_row(z, body)
+        weights = dot(proj[...], wt[...], NT)[:8]
+        whole = dot(proj[...], v[...], NT)[:8]
+        part[...] = sum3(dot(stack3(weights), hid_cat[...], NT)) + jnp.where(first, whole, 0.0)
+
+
+def second_kernel(z, scale, *refs):
+    v, w_cat, pos, wt, proj, halves, hid_cat, slope, inner_in, total, received = refs[:11]
+    big, time, part = refs[11:14]
+    shifts, inner_cat, thin = refs[14:]
     decoder = lax.axis_index("sec") == 1
     first = lax.axis_index("sp") == 0
     for j in range(3):
         zero_ends(z, shifts.at[j])
-    for copy in started:
-        copy.wait()
 
     def put_out(kernel_grad, proj_part):
         part[...] = proj_part
@@ -444,11 +464,10 @@
 
     @pl.when(decoder)
     def _():
-        def body(r, carry):
+        def body(r):
             put_shifts(z, inner_in[r].astype(F32), shifts, r)
-            return carry
-
-        lax.fori_loop(0, z.sp, body, 0)
+
+        each_row(z, body)
         spread(z, shifts, inner_cat)
         half = halves[:8, :1]
 
@@ -476,12 +495,11 @@
         right = jnp.concatenate([bh, bm, bh, bl, bh, bm], axis=0).astype(BF16)
         thin[...] = dot(left, right, TN)
 
-        def body(r, carry):
+        def body(r):
             inner = keep_own(z, later_row(z, thin, r) * slope[r])
             put_shifts(z, inner, shifts, r)
-            return carry
-
-        lax.fori_loop(0, z.sp, body, 0)
+
+        each_row(z, body)
         spread(z, shifts, inner_cat)
         kernel_grad = dot(v[...], inner_cat[...], TN) * scale
         grad3 = jnp.concatenate([gh, gm, gl], axis=0).astype(BF16)
@@ -506,7 +524,8 @@
         for m in range(z.chans // LANES):
             low = pltpu.roll(carried[16 * m : 16 * m + 8], LANES // 2, 1)
             high = carried[16 * m + 8 : 16 * m + 16]
-            part[:, m * LANES : (m + 1) * LANES] = jnp.where(lane < LANES // 2, low, high)
+            both = jnp.where(lane < LANES // 2, low, high)
+            part[:, m * LANES : (m + 1) * LANES] = both[: z.lat]
     else:
         part[...] = jnp.zeros(part.shape, F32)
     per = LANES // z.own
@@ -526,7 +545,6 @@
 
 
 VM = pl.BlockSpec(memory_space=pltpu.VMEM)
-ANY = pl.BlockSpec(memory_space=pl.ANY)
 
 
 def shaped(shape, dtype):
@@ -539,7 +557,8 @@
     z = Sizes(lax.axis_size("sp"), frames, cols, chans, own, lat)
     scale = float(lax.axis_size("dp") * z.count) ** (-0.5)
     decoder = lax.axis_index("sec") == 1
-    params = pltpu.CompilerParams(vmem_limit_bytes=VMEM_BYTES)
+    room = 20 * 1024 * 1024 + 5 * z.count * chans * 4 // 2 * (1 if z.sp > 8 else 0)
+    params = pltpu.CompilerParams(vmem_limit_bytes=min(room, 60 * 1024 * 1024))
 
     codes = jnp.transpose(code_index[0, :, :, 0], (1, 0, 2)).reshape(frames * lat, cols)
     left = z.code_lane % LANES
@@ -562,12 +581,13 @@
     shards, steps, mine, other, piece_steps = ring_exchange(
         block_data.reshape(z.row, chans), ahead, behind, own_piece
     )
-    wt = jnp.pad(w_time.reshape(3 * own, chans), ((0, z.thin - 3 * own), (0, 0)))
     proj = jnp.pad(jnp.where(decoder, dec_proj, enc_proj), ((0, 16 - lat), (0, 0)))
+    wt = jnp.concatenate([w_time.reshape(3 * own, chans), proj[:8]], axis=0)
+    wt = jnp.pad(wt, ((0, z.thin - 3 * own - 8), (0, 0)))
     half = jnp.pad((levels.astype(F32) - 1.0) * 0.5, (0, 16 - lat), constant_values=1.0)
     halves = jnp.broadcast_to(half[:, None], (16, LANES))
 
-    part, hid_cat, slope, inner, w_cat, pos = pl.pallas_call(
+    part, hid_cat, slope, inner, w_cat, pos, v = pl.pallas_call(
         functools.partial(first_kernel, z, steps, piece_steps),
         out_shape=(
             shaped((8, z.count), F32),
@@ -576,19 +596,16 @@
             shaped((z.sp, z.row, LANES), BF16),
             shaped((chans, z.wide), BF16),
             shaped((z.count, LANES), BF16),
+            shaped((z.count, chans), BF16),
         ),
-        in_specs=[ANY] * (3 * z.sp) + [VM] * 3,
-        out_specs=(VM,) * 6,
+        in_specs=[VM] * (3 * z.sp + 3),
+        out_specs=(VM,) * 7,
         scratch_shapes=[
-            pltpu.VMEM((z.count, chans), BF16),
-            pltpu.VMEM((z.sp, 2, z.half_pad, z.wide), BF16),
             pltpu.VMEM((z.sp, z.code_rows, z.wide), BF16),
             pltpu.VMEM((z.sp + 2, z.row, z.wide), F32),
-            pltpu.VMEM((3, z.sp + 2, z.row, LANES), BF16),
-            pltpu.VMEM((z.count, z.wide), BF16),
+            pltpu.VMEM((z.sp + 2, z.row, LANES), F32),
+            pltpu.VMEM((z.count, LANES), F32),
             pltpu.VMEM((z.count, z.thin), F32),
-            pltpu.SemaphoreType.DMA((z.sp,)),
-            pltpu.SemaphoreType.DMA((3, z.sp)),
         ],
         compiler_params=params,
         name="first",
@@ -597,31 +614,29 @@
     total = swap_sum(part, "sp")
     received = lax.ppermute(total, "sec", swap)
     big, time, part = pl.pallas_call(
-        functools.partial(second_kernel, z, steps, scale),
+        functools.partial(second_kernel, z, scale),
         out_shape=(
             shaped((chans, z.wide), BF16),
             shaped((3 * own, chans), F32),
             shaped((8, chans), F32),
         ),
-        in_specs=[ANY] * z.sp + [VM] * 10,
+        in_specs=[VM] * 11,
         out_specs=(VM,) * 3,
         scratch_shapes=[
-            pltpu.VMEM((z.count, chans), BF16),
             pltpu.VMEM((3, z.sp + 2, z.row, LANES), BF16),
             pltpu.VMEM((z.count, z.wide), BF16),
             pltpu.VMEM((z.count, z.thin), F32),
-            pltpu.SemaphoreType.DMA((z.sp,)),
         ],
         compiler_params=params,
         name="second",
-    )(*shards, w_cat, pos, wt, proj, halves, hid_cat, slope, inner, total, received)
+    )(v, w_cat, pos, wt, proj, halves, hid_cat, slope, inner, total, received)
     big = lax.all_to_all(big.reshape(z.sp, own, z.wide), "sp", 0, 0, tiled=True)
     space, time, carried = pl.pallas_call(
         functools.partial(last_kernel, z),
         out_shape=(
             shaped((9, own, chans), F32),
             shaped((3 * own, chans), F32),
-            shaped((8, chans), F32),
+            shaped((lat, chans), F32),
         ),
         in_specs=[VM] * 4,
         out_specs=(VM,) * 3,
@@ -632,8 +647,8 @@
         part = carried
     else:
         part = swap_sum(part, "sp")
-        part = part + lax.ppermute(part, "dp", swap)
-    return space[None], time.reshape(1, 3, own, chans), part[None, :lat]
+        part = (part + lax.ppermute(part, "dp", swap))[:lat]
+    return space[None], time.reshape(1, 3, own, chans), part[None]
 
 
 def solution(mesh):

time: 108 us -> 82.7 us (0.77)
  Pallas kernels: 23.1 us -> 8 us
  local copies, waits for them, and re-layouts: 12.2 us -> 1.98 us
  waiting for transfers between devices: 24.6 us -> 23.5 us
    pallas_call x1, Pallas kernels: 8.85 us -> 2.23 us  [local(): pl.pallas_call(functools.partial(first_kernel, z, steps, piece_steps), ou...]
    pallas_call x1, Pallas kernels: 8.45 us -> 3.28 us  [local(): pl.pallas_call(functools.partial(second_kernel, z, scale), out_shape=(sha...]
    slice x5 -> x2, local copies, waits for them, and re-layouts: 3.11 us -> 0.02 us  [the longest x1 0.01 us: ring_exchange(): mine.append(behind[0])]
    ppermute x4, starting transfers between devices: 1.1 us -> 2.97 us  [ring_exchange(): behind = lax.ppermute(behind, 'sp', down)]
    squeeze x3 -> x2, local copies, waits for them, and re-layouts: 1.89 us -> 0.03 us  [meet(): other.extend((both[i] for i in range(len(fresh))))]
    pallas_call x1, Pallas kernels: 2.74 us -> 0.96 us  [local(): pl.pallas_call(functools.partial(piece_kernel, z), out_shape=(shaped((z.s...]
    ppermute x3, waiting for transfers between devices: 2.6 us -> 0.88 us  [ring_exchange(): second = lax.ppermute(second, 'sp', down)]
    pad x1 -> x0, local copies, waits for them, and re-layouts: 1.65 us -> none  [local(): jnp.pad(w_time.reshape(3 * own, chans), ((0, z.thin - 3 * own), (0, 0)))]
  transfers between devices with their start and end apart: 25 -> 22, of which waited for: 11 -> 14; matrix products, arithmetic and copies ran while one was open for 9% -> 3% of each run, Pallas kernels for 3% -> 1%
where the time goes in v4:
time: 82.7 us; the launch traced here: 82.3 us
  starting transfers between devices  27.1 us (33%)
  waiting for transfers between devices  23.5 us (28%)
  blocking collectives  18.9 us (23%)
  Pallas kernels  8 us (10%)
  other arithmetic  2.14 us (3%)
  local copies, waits for them, and re-layouts  1.98 us (2%)
    all_to_all x1, blocking collectives, local(): big = lax.all_to_all(big.reshape(z.sp, own, z.wide), 'sp', 0, 0, tiled=True)  18.9 us
    ppermute x3, waiting for transfers between devices, swap_sum(): lax.ppermute(values, axis, [(i, i ^ bit) for i in range(count)])  7.36 us
    ppermute x3, starting transfers between devices, ring_exchange(): second = lax.ppermute(second, 'sp', down)  6.26 us
    ppermute x3, starting transfers between devices, swap_sum(): lax.ppermute(values, axis, [(i, i ^ bit) for i in range(count)])  5.57 us
    ppermute x3, starting transfers between devices, ring_exchange(): ahead = lax.ppermute(ahead, 'sp', up)  5.37 us
    ppermute x4, waiting for transfers between devices, ring_exchange(): first = lax.ppermute(first, 'sp', up)  4.62 us
    ppermute x4, waiting for transfers between devices, ring_exchange(): behind = lax.ppermute(behind, 'sp', down)  4.17 us
    ppermute x1, starting transfers between devices, local(): received = lax.ppermute(total, 'sec', swap)  3.47 us
  transfers between devices with their start and end apart: 22, of which 14 were waited for; matrix products, arithmetic and copies ran while one was open for 3% of the time, Pallas kernels for 1%

profile of v4, /device:TPU:0, one launch (start us, length us, event | category | flops | bytes accessed | tf_op | source)
XLA Modules:
  0.0 82.3 jit_solution(14524928951296494976)
XLA Ops:
  0.6 3.0 %collective-permute-start.1 = (bf16[160,512]{1,0:T(8,128)(2,1)}, bf16[160,512]{1,0:T(8,128)(2,1)S(1)}, u32[]{:S(2)}, u32[]{:S(2)}) collective-permute-start(bf16[160,512]{1,0:T(8,128)(2,1)} %bitcast.43), channel_id=1, source_target_pairs={{4,0},{8,4},{12,8},{14,12},{10,14},{6,10},{2,6},{0,2},{5,1},{9,5},... | collective-permute-start | bytes 491528 | tf_op jit(solution)/shard_map/ppermute | solution.py:56
  6.6 2.0 %collective-permute-start.7 = (bf16[3,32,640]{2,1,0:T(8,128)(2,1)S(1)}, bf16[3,32,640]{2,1,0:T(8,128)(2,1)S(1)}, u32[]{:S(2)}, u32[]{:S(2)}) collective-permute-start(bf16[3,32,640]{2,1,0:T(8,128)(2,1)S(1)} %get-tuple-element.19), channel_id=1, source_target_pairs={{0,4},{4,8},{8,12},{12,14},{14,10},{10,6},{6,2},{2,0},{1,5},{5,9},... | collective-permute-start | bytes 368648 | tf_op jit(solution)/shard_map/ppermute | solution.py:59
  10.1 2.1 %collective-permute-done.7 = bf16[3,32,640]{2,1,0:T(8,128)(2,1)S(1)} collective-permute-done((bf16[3,32,640]{2,1,0:T(8,128)(2,1)S(1)}, bf16[3,32,640]{2,1,0:T(8,128)(2,1)S(1)}, u32[]{:S(2)}, u32[]{:S(2)}) %collective-permute-start.7) | collective-permute-done | bytes 122912 | tf_op jit(solution)/shard_map/ppermute | solution.py:59
  12.2 1.4 %collective-permute-start.9 = (bf16[2,32,640]{2,1,0:T(8,128)(2,1)S(1)}, bf16[2,32,640]{2,1,0:T(8,128)(2,1)S(1)}, u32[]{:S(2)}, u32[]{:S(2)}) collective-permute-start(bf16[2,32,640]{2,1,0:T(8,128)(2,1)S(1)} %slice.78), channel_id=1, source_target_pairs={{0,4},{4,8},{8,12},{12,14},{14,10},{10,6},{6,2},{2,0},{1,5},{5,9},... | collective-permute-start | bytes 245768 | tf_op jit(solution)/shard_map/ppermute | solution.py:59
  14.4 1.6 %collective-permute-start.3 = (bf16[160,512]{1,0:T(8,128)(2,1)S(1)}, bf16[160,512]{1,0:T(8,128)(2,1)S(1)}, u32[]{:S(2)}, u32[]{:S(2)}) collective-permute-start(bf16[160,512]{1,0:T(8,128)(2,1)S(1)} %collective-permute-done.1.refs_2_), channel_id=1, source_target_pairs={{4,0},{8,4},{12,8},{14,12},{10,14},{6,10},{2,6},{0,2},{5,1},{9,5},... | collective-permute-start | bytes 491528 | tf_op jit(solution)/shard_map/ppermute | solution.py:56
  16.7 1.9 %collective-permute-start.11 = (bf16[1,32,640]{2,1,0:T(8,128)(2,1)S(1)}, bf16[1,32,640]{2,1,0:T(8,128)(2,1)S(1)}, u32[]{:S(2)}, u32[]{:S(2)}) collective-permute-start(bf16[1,32,640]{2,1,0:T(8,128)(2,1)S(1)} %get-tuple-element.57), channel_id=1, source_target_pairs={{0,4},{4,8},{8,12},{12,14},{14,10},{10,6},{6,2},{2,0},{1,5},{5,9},... | collective-permute-start | bytes 122888 | tf_op jit(solution)/shard_map/ppermute | solution.py:59
  19.4 1.3 %collective-permute-start.12 = (bf16[2,32,640]{2,1,0:T(8,128)(2,1)S(1)}, bf16[2,32,640]{2,1,0:T(8,128)(2,1)S(1)}, u32[]{:S(2)}, u32[]{:S(2)}) collective-permute-start(bf16[2,32,640]{2,1,0:T(8,128)(2,1)S(1)} %slice.83), channel_id=1, source_target_pairs={{4,0},{8,4},{12,8},{14,12},{10,14},{6,10},{2,6},{0,2},{5,1},{9,5},... | collective-permute-start | bytes 245768 | tf_op jit(solution)/shard_map/ppermute | solution.py:63
  22.0 1.9 %collective-permute-done.12 = bf16[2,32,640]{2,1,0:T(8,128)(2,1)S(1)} collective-permute-done((bf16[2,32,640]{2,1,0:T(8,128)(2,1)S(1)}, bf16[2,32,640]{2,1,0:T(8,128)(2,1)S(1)}, u32[]{:S(2)}, u32[]{:S(2)}) %collective-permute-start.12) | collective-permute-done | bytes 81952 | tf_op jit(solution)/shard_map/ppermute | solution.py:63
  25.2 1.6 %collective-permute-start.5 = (bf16[160,512]{1,0:T(8,128)(2,1)S(1)}, bf16[160,512]{1,0:T(8,128)(2,1)S(1)}, u32[]{:S(2)}, u32[]{:S(2)}) collective-permute-start(bf16[160,512]{1,0:T(8,128)(2,1)S(1)} %collective-permute-done.3.refs_4_), channel_id=1, source_target_pairs={{4,0},{8,4},{12,8},{14,12},{10,14},{6,10},{2,6},{0,2},{5,1},{9,5},... | collective-permute-start | bytes 491528 | tf_op jit(solution)/shard_map/ppermute | solution.py:56
  28.1 1.6 %collective-permute-start.6 = (bf16[160,512]{1,0:T(8,128)(2,1)S(1)}, bf16[160,512]{1,0:T(8,128)(2,1)S(1)}, u32[]{:S(2)}, u32[]{:S(2)}) collective-permute-start(bf16[160,512]{1,0:T(8,128)(2,1)S(1)} %collective-permute-done.4.refs_5_), channel_id=1, source_target_pairs={{0,4},{4,8},{8,12},{12,14},{14,10},{10,6},{6,2},{2,0},{1,5},{5,9},... | collective-permute-start | bytes 491528 | tf_op jit(solution)/shard_map/ppermute | solution.py:51
  30.6 4.1 %collective-permute-done.6.refs_7_ = bf16[160,512]{1,0:T(8,128)(2,1)S(1)} collective-permute-done((bf16[160,512]{1,0:T(8,128)(2,1)S(1)}, bf16[160,512]{1,0:T(8,128)(2,1)S(1)}, u32[]{:S(2)}, u32[]{:S(2)}) %collective-permute-start.6) | collective-permute-done | bytes 163872 | tf_op jit(solution)/shard_map/ppermute | solution.py:51
  34.8 2.2 %first.1 = (f32[8,1280]{1,0:T(8,128)S(1)}, bf16[1280,256]{1,0:T(8,128)(2,1)S(1)}, f32[8,160,128]{2,1,0:T(8,128)S(1)}, bf16[8,160,128]{2,1,0:T(8,128)(2,1)S(1)}, ...) custom-call(bf16[160,512]{1,0:T(8,128)(2,1)S(1)} %bitcast.45, ...), custom_call_target="tpu_custom_call" | custom-call | tf_op jit(solution)/shard_map/first/pallas_call | solution.py:590
  37.0 1.3 %collective-permute-start.16 = (f32[8,1280]{1,0:T(8,128)S(1)}, f32[8,1280]{1,0:T(8,128)S(1)}, u32[]{:S(2)}, u32[]{:S(2)}) collective-permute-start(f32[8,1280]{1,0:T(8,128)S(1)} %get-tuple-element.27), channel_id=1, source_target_pairs={{0,2},{2,0},{4,6},{6,4},{8,10},{10,8},{12,14},{14,12},{1,3},{3,1},... | collective-permute-start | bytes 122888 | tf_op jit(solution)/shard_map/ppermute | solution.py:76
  38.3 2.7 %collective-permute-done.16 = f32[8,1280]{1,0:T(8,128)S(1)} collective-permute-done((f32[8,1280]{1,0:T(8,128)S(1)}, f32[8,1280]{1,0:T(8,128)S(1)}, u32[]{:S(2)}, u32[]{:S(2)}) %collective-permute-start.16) | collective-permute-done | bytes 40992 | tf_op jit(solution)/shard_map/ppermute | solution.py:76
  41.0 1.5 %collective-permute-start.17 = (f32[8,1280]{1,0:T(8,128)S(1)}, f32[8,1280]{1,0:T(8,128)S(1)}, u32[]{:S(2)}, u32[]{:S(2)}) collective-permute-start(f32[8,1280]{1,0:T(8,128)S(1)} %add.18), channel_id=1, source_target_pairs={{0,4},{2,6},{4,0},{6,2},{8,12},{10,14},{12,8},{14,10},{1,5},{3,7},... | collective-permute-start | bytes 122888 | tf_op jit(solution)/shard_map/ppermute | solution.py:76
  42.6 2.5 %collective-permute-done.17 = f32[8,1280]{1,0:T(8,128)S(1)} collective-permute-done((f32[8,1280]{1,0:T(8,128)S(1)}, f32[8,1280]{1,0:T(8,128)S(1)}, u32[]{:S(2)}, u32[]{:S(2)}) %collective-permute-start.17) | collective-permute-done | bytes 40992 | tf_op jit(solution)/shard_map/ppermute | solution.py:76
  45.0 2.7 %collective-permute-start.18 = (f32[8,1280]{1,0:T(8,128)S(1)}, f32[8,1280]{1,0:T(8,128)S(1)}, u32[]{:S(2)}, u32[]{:S(2)}) collective-permute-start(f32[8,1280]{1,0:T(8,128)S(1)} %add.19), channel_id=1, source_target_pairs={{0,8},{2,10},{4,12},{6,14},{8,0},{10,2},{12,4},{14,6},{1,9},{3,11}... | collective-permute-start | bytes 122888 | tf_op jit(solution)/shard_map/ppermute | solution.py:76
  47.7 2.2 %collective-permute-done.18 = f32[8,1280]{1,0:T(8,128)S(1)} collective-permute-done((f32[8,1280]{1,0:T(8,128)S(1)}, f32[8,1280]{1,0:T(8,128)S(1)}, u32[]{:S(2)}, u32[]{:S(2)}) %collective-permute-start.18) | collective-permute-done | bytes 40992 | tf_op jit(solution)/shard_map/ppermute | solution.py:76
  49.9 3.5 %collective-permute-start.19 = (f32[8,1280]{1,0:T(8,128)S(1)}, f32[8,1280]{1,0:T(8,128)S(1)}, u32[]{:S(2)}, u32[]{:S(2)}) collective-permute-start(f32[8,1280]{1,0:T(8,128)S(1)} %add.20.refs_9_), channel_id=1, source_target_pairs={{0,16},{16,0},{1,17},{17,1},{2,18},{18,2},{3,19},{19,3},{4,20},{20... | collective-permute-start | bytes 122888 | tf_op jit(solution)/shard_map/ppermute | solution.py:615
  53.4 2.0 %collective-permute-done.19.refs_10_ = f32[8,1280]{1,0:T(8,128)S(1)} collective-permute-done((f32[8,1280]{1,0:T(8,128)S(1)}, f32[8,1280]{1,0:T(8,128)S(1)}, u32[]{:S(2)}, u32[]{:S(2)}) %collective-permute-start.19) | collective-permute-done | bytes 40992 | tf_op jit(solution)/shard_map/ppermute | solution.py:615
  55.4 3.3 %second.1 = (bf16[512,640]{1,0:T(8,128)(2,1)S(1)}, f32[192,512]{1,0:T(8,128)S(1)}, f32[8,512]{1,0:T(8,128)}) custom-call(bf16[1280,512]{1,0:T(8,128)(2,1)S(1)} %get-tuple-element.21.refs_0_, bf16[512,640]{1,0:T(8,128)(2,1)S(1)} %get-tuple-element.22.refs_1_, bf16[1280,128]{1,0:T(8,128)(2,1)S(1)} %get-tuple-element.23.refs_2_, ...), custom_call_target="tpu_custom_call" | custom-call | tf_op jit(solution)/shard_map/second/pallas_call | solution.py:616
  58.7 18.9 %all_to_all.5.mine = bf16[8,64,640]{2,1,0:T(8,128)(2,1)S(1)} all-to-all(bf16[8,64,640]{2,1,0:T(8,128)(2,1)S(1)} %bitcast.41), channel_id=1, replica_groups=mesh['sec'=2,'sp'=8,'dp'=2] {'sp'}, dimensions={0} | all-to-all | bytes 1310720 | tf_op jit(solution)/shard_map/all_to_all | solution.py:633
  78.0 2.1 %collective-permute-done.21.time_other = f32[192,512]{1,0:T(8,128)S(1)} collective-permute-done((f32[192,512]{1,0:T(8,128)S(1)}, f32[192,512]{1,0:T(8,128)S(1)}, u32[]{:S(2)}, u32[]{:S(2)}) %collective-permute-start.21) | collective-permute-done | bytes 393248 | tf_op jit(solution)/shard_map/ppermute | solution.py:645
  80.2 1.5 %last.1 = (f32[9,64,512]{2,1,0:T(8,128)}, f32[192,512]{1,0:T(8,128)}, f32[6,512]{1,0:T(8,128)S(1)}) custom-call(bf16[8,64,640]{2,1,0:T(8,128)(2,1)S(1)} %all_to_all.5.mine, bf16[8,64,640]{2,1,0:T(8,128)(2,1)S(1)} %collective-permute-done.20.other, f32[192,512]{1,0:T(8,128)S(1)} %get-tuple-element.29.time_mine, f32[192,512]{1,0:T(8,128)S(1)} %collective-permute-done.21.time_other), custom_call_target="tpu_custom_call" | custom-call | tf_op jit(solution)/shard_map/last/pallas_call | solution.py:634
  (57 shorter events, 12.6 us)
Async XLA Ops:
  0.6 13.7 %collective-permute-start.1 = (bf16[160,512]{1,0:T(8,128)(2,1)}, bf16[160,512]{1,0:T(8,128)(2,1)S(1)}, u32[]{:S(2)}, u32[]{:S(2)}) collective-permute-start(bf16[160,512]{1,0:T(8,128)(2,1)} %bitcast.43), channel_id=1, source_target_pairs={{4,0},{8,4},{12,8},{14,12},{10,14},{6,10},{2,6},{0,2},{5,1},{9,5},... | collective-permute-start | bytes 491528 | tf_op jit(solution)/shard_map/ppermute | solution.py:56
  3.6 12.3 %collective-permute-start = (bf16[160,512]{1,0:T(8,128)(2,1)}, bf16[160,512]{1,0:T(8,128)(2,1)S(1)}, u32[]{:S(2)}, u32[]{:S(2)}) collective-permute-start(bf16[160,512]{1,0:T(8,128)(2,1)} %bitcast.44), channel_id=1, source_target_pairs={{0,4},{4,8},{8,12},{12,14},{14,10},{10,6},{6,2},{2,0},{1,5},{5,9},... | collective-permute-start | bytes 491528 | tf_op jit(solution)/shard_map/ppermute | solution.py:51
  5.6 19.5 %copy-start.2 = (bf16[1,3,64,512]{3,2,1,0:T(8,128)(2,1)S(1)}, bf16[1,3,64,512]{3,2,1,0:T(8,128)(2,1)}, u32[]{:S(2)}) copy-start(bf16[1,3,64,512]{3,2,1,0:T(8,128)(2,1)} %param.11) | copy-start | bytes 589828
  6.6 5.5 %collective-permute-start.7 = (bf16[3,32,640]{2,1,0:T(8,128)(2,1)S(1)}, bf16[3,32,640]{2,1,0:T(8,128)(2,1)S(1)}, u32[]{:S(2)}, u32[]{:S(2)}) collective-permute-start(bf16[3,32,640]{2,1,0:T(8,128)(2,1)S(1)} %get-tuple-element.19), channel_id=1, source_target_pairs={{0,4},{4,8},{8,12},{12,14},{14,10},{10,6},{6,2},{2,0},{1,5},{5,9},... | collective-permute-start | bytes 368648 | tf_op jit(solution)/shard_map/ppermute | solution.py:59
  8.6 5.3 %collective-permute-start.8 = (bf16[4,32,640]{2,1,0:T(8,128)(2,1)S(1)}, bf16[4,32,640]{2,1,0:T(8,128)(2,1)S(1)}, u32[]{:S(2)}, u32[]{:S(2)}) collective-permute-start(bf16[4,32,640]{2,1,0:T(8,128)(2,1)S(1)} %get-tuple-element.20), channel_id=1, source_target_pairs={{4,0},{8,4},{12,8},{14,12},{10,14},{6,10},{2,6},{0,2},{5,1},{9,5},... | collective-permute-start | bytes 491528 | tf_op jit(solution)/shard_map/ppermute | solution.py:63
  12.2 22.6 %copy-start.1 = (bf16[1,1,5,1,32,512]{5,4,3,2,1,0:T(8,128)(2,1)S(1)}, bf16[1,1,5,1,32,512]{5,4,3,2,1,0:T(8,128)(2,1)}, u32[]{:S(2)}) copy-start(bf16[1,1,5,1,32,512]{5,4,3,2,1,0:T(8,128)(2,1)} %param.7) | copy-start | bytes 491524
  12.2 4.5 %collective-permute-start.9 = (bf16[2,32,640]{2,1,0:T(8,128)(2,1)S(1)}, bf16[2,32,640]{2,1,0:T(8,128)(2,1)S(1)}, u32[]{:S(2)}, u32[]{:S(2)}) collective-permute-start(bf16[2,32,640]{2,1,0:T(8,128)(2,1)S(1)} %slice.78), channel_id=1, source_target_pairs={{0,4},{4,8},{8,12},{12,14},{14,10},{10,6},{6,2},{2,0},{1,5},{5,9},... | collective-permute-start | bytes 245768 | tf_op jit(solution)/shard_map/ppermute | solution.py:59
  14.0 5.4 %collective-permute-start.10 = (bf16[3,32,640]{2,1,0:T(8,128)(2,1)S(1)}, bf16[3,32,640]{2,1,0:T(8,128)(2,1)S(1)}, u32[]{:S(2)}, u32[]{:S(2)}) collective-permute-start(bf16[3,32,640]{2,1,0:T(8,128)(2,1)S(1)} %slice.80), channel_id=1, source_target_pairs={{4,0},{8,4},{12,8},{14,12},{10,14},{6,10},{2,6},{0,2},{5,1},{9,5},... | collective-permute-start | bytes 368648 | tf_op jit(solution)/shard_map/ppermute | solution.py:63
  14.4 10.9 %collective-permute-start.3 = (bf16[160,512]{1,0:T(8,128)(2,1)S(1)}, bf16[160,512]{1,0:T(8,128)(2,1)S(1)}, u32[]{:S(2)}, u32[]{:S(2)}) collective-permute-start(bf16[160,512]{1,0:T(8,128)(2,1)S(1)} %collective-permute-done.1.refs_2_), channel_id=1, source_target_pairs={{4,0},{8,4},{12,8},{14,12},{10,14},{6,10},{2,6},{0,2},{5,1},{9,5},... | collective-permute-start | bytes 491528 | tf_op jit(solution)/shard_map/ppermute | solution.py:56
  16.0 5.3 %collective-permute-start.2 = (bf16[160,512]{1,0:T(8,128)(2,1)S(1)}, bf16[160,512]{1,0:T(8,128)(2,1)S(1)}, u32[]{:S(2)}, u32[]{:S(2)}) collective-permute-start(bf16[160,512]{1,0:T(8,128)(2,1)S(1)} %collective-permute-done.refs_1_), channel_id=1, source_target_pairs={{0,4},{4,8},{8,12},{12,14},{14,10},{10,6},{6,2},{2,0},{1,5},{5,9},... | collective-permute-start | bytes 491528 | tf_op jit(solution)/shard_map/ppermute | solution.py:51
  16.7 10.2 %collective-permute-start.11 = (bf16[1,32,640]{2,1,0:T(8,128)(2,1)S(1)}, bf16[1,32,640]{2,1,0:T(8,128)(2,1)S(1)}, u32[]{:S(2)}, u32[]{:S(2)}) collective-permute-start(bf16[1,32,640]{2,1,0:T(8,128)(2,1)S(1)} %get-tuple-element.57), channel_id=1, source_target_pairs={{0,4},{4,8},{8,12},{12,14},{14,10},{10,6},{6,2},{2,0},{1,5},{5,9},... | collective-permute-start | bytes 122888 | tf_op jit(solution)/shard_map/ppermute | solution.py:59
  19.4 4.5 %collective-permute-start.12 = (bf16[2,32,640]{2,1,0:T(8,128)(2,1)S(1)}, bf16[2,32,640]{2,1,0:T(8,128)(2,1)S(1)}, u32[]{:S(2)}, u32[]{:S(2)}) collective-permute-start(bf16[2,32,640]{2,1,0:T(8,128)(2,1)S(1)} %slice.83), channel_id=1, source_target_pairs={{4,0},{8,4},{12,8},{14,12},{10,14},{6,10},{2,6},{0,2},{5,1},{9,5},... | collective-permute-start | bytes 245768 | tf_op jit(solution)/shard_map/ppermute | solution.py:63
  20.7 9.0 %collective-permute-start.14 = (bf16[5,32,640]{2,1,0:T(8,128)(2,1)S(1)}, bf16[5,32,640]{2,1,0:T(8,128)(2,1)S(1)}, u32[]{:S(2)}, u32[]{:S(2)}) collective-permute-start(bf16[5,32,640]{2,1,0:T(8,128)(2,1)S(1)} %get-tuple-element.49), channel_id=1, source_target_pairs={{0,1},{1,0},{2,3},{3,2},{4,5},{5,4},{6,7},{7,6},{8,9},{9,8},{10,11... | collective-permute-start | bytes 614408 | tf_op jit(solution)/shard_map/ppermute | solution.py:47
  21.3 6.8 %collective-permute-start.4 = (bf16[160,512]{1,0:T(8,128)(2,1)S(1)}, bf16[160,512]{1,0:T(8,128)(2,1)S(1)}, u32[]{:S(2)}, u32[]{:S(2)}) collective-permute-start(bf16[160,512]{1,0:T(8,128)(2,1)S(1)} %collective-permute-done.2.refs_3_), channel_id=1, source_target_pairs={{0,4},{4,8},{8,12},{12,14},{14,10},{10,6},{6,2},{2,0},{1,5},{5,9},... | collective-permute-start | bytes 491528 | tf_op jit(solution)/shard_map/ppermute | solution.py:51
  23.9 4.1 %collective-permute-start.13 = (bf16[1,32,640]{2,1,0:T(8,128)(2,1)S(1)}, bf16[1,32,640]{2,1,0:T(8,128)(2,1)S(1)}, u32[]{:S(2)}, u32[]{:S(2)}) collective-permute-start(bf16[1,32,640]{2,1,0:T(8,128)(2,1)S(1)} %get-tuple-element.55), channel_id=1, source_target_pairs={{4,0},{8,4},{12,8},{14,12},{10,14},{6,10},{2,6},{0,2},{5,1},{9,5},... | collective-permute-start | bytes 122888 | tf_op jit(solution)/shard_map/ppermute | solution.py:63
  25.2 5.4 %collective-permute-start.5 = (bf16[160,512]{1,0:T(8,128)(2,1)S(1)}, bf16[160,512]{1,0:T(8,128)(2,1)S(1)}, u32[]{:S(2)}, u32[]{:S(2)}) collective-permute-start(bf16[160,512]{1,0:T(8,128)(2,1)S(1)} %collective-permute-done.3.refs_4_), channel_id=1, source_target_pairs={{4,0},{8,4},{12,8},{14,12},{10,14},{6,10},{2,6},{0,2},{5,1},{9,5},... | collective-permute-start | bytes 491528 | tf_op jit(solution)/shard_map/ppermute | solution.py:56
  28.0 1.7 %collective-permute-start.15 = (bf16[3,32,640]{2,1,0:T(8,128)(2,1)S(1)}, bf16[3,32,640]{2,1,0:T(8,128)(2,1)S(1)}, u32[]{:S(2)}, u32[]{:S(2)}) collective-permute-start(bf16[3,32,640]{2,1,0:T(8,128)(2,1)S(1)} %pad_maximum_fusion), channel_id=1, source_target_pairs={{0,1},{1,0},{2,3},{3,2},{4,5},{5,4},{6,7},{7,6},{8,9},{9,8},{10,11... | collective-permute-start | bytes 368648 | tf_op jit(solution)/shard_map/ppermute | solution.py:47
  28.1 6.6 %collective-permute-start.6 = (bf16[160,512]{1,0:T(8,128)(2,1)S(1)}, bf16[160,512]{1,0:T(8,128)(2,1)S(1)}, u32[]{:S(2)}, u32[]{:S(2)}) collective-permute-start(bf16[160,512]{1,0:T(8,128)(2,1)S(1)} %collective-permute-done.4.refs_5_), channel_id=1, source_target_pairs={{0,4},{4,8},{8,12},{12,14},{14,10},{10,6},{6,2},{2,0},{1,5},{5,9},... | collective-permute-start | bytes 491528 | tf_op jit(solution)/shard_map/ppermute | solution.py:51
  37.0 4.0 %collective-permute-start.16 = (f32[8,1280]{1,0:T(8,128)S(1)}, f32[8,1280]{1,0:T(8,128)S(1)}, u32[]{:S(2)}, u32[]{:S(2)}) collective-permute-start(f32[8,1280]{1,0:T(8,128)S(1)} %get-tuple-element.27), channel_id=1, source_target_pairs={{0,2},{2,0},{4,6},{6,4},{8,10},{10,8},{12,14},{14,12},{1,3},{3,1},... | collective-permute-start | bytes 122888 | tf_op jit(solution)/shard_map/ppermute | solution.py:76
  41.0 4.0 %collective-permute-start.17 = (f32[8,1280]{1,0:T(8,128)S(1)}, f32[8,1280]{1,0:T(8,128)S(1)}, u32[]{:S(2)}, u32[]{:S(2)}) collective-permute-start(f32[8,1280]{1,0:T(8,128)S(1)} %add.18), channel_id=1, source_target_pairs={{0,4},{2,6},{4,0},{6,2},{8,12},{10,14},{12,8},{14,10},{1,5},{3,7},... | collective-permute-start | bytes 122888 | tf_op jit(solution)/shard_map/ppermute | solution.py:76
  45.0 4.9 %collective-permute-start.18 = (f32[8,1280]{1,0:T(8,128)S(1)}, f32[8,1280]{1,0:T(8,128)S(1)}, u32[]{:S(2)}, u32[]{:S(2)}) collective-permute-start(f32[8,1280]{1,0:T(8,128)S(1)} %add.19), channel_id=1, source_target_pairs={{0,8},{2,10},{4,12},{6,14},{8,0},{10,2},{12,4},{14,6},{1,9},{3,11}... | collective-permute-start | bytes 122888 | tf_op jit(solution)/shard_map/ppermute | solution.py:76
  49.9 5.4 %collective-permute-start.19 = (f32[8,1280]{1,0:T(8,128)S(1)}, f32[8,1280]{1,0:T(8,128)S(1)}, u32[]{:S(2)}, u32[]{:S(2)}) collective-permute-start(f32[8,1280]{1,0:T(8,128)S(1)} %add.20.refs_9_), channel_id=1, source_target_pairs={{0,16},{16,0},{1,17},{17,1},{2,18},{18,2},{3,19},{19,3},{4,20},{20... | collective-permute-start | bytes 122888 | tf_op jit(solution)/shard_map/ppermute | solution.py:615
  77.5 2.7 %collective-permute-start.20 = (bf16[8,64,640]{2,1,0:T(8,128)(2,1)S(1)}, bf16[8,64,640]{2,1,0:T(8,128)(2,1)S(1)}, u32[]{:S(2)}, u32[]{:S(2)}) collective-permute-start(bf16[8,64,640]{2,1,0:T(8,128)(2,1)S(1)} %all_to_all.5.mine), channel_id=1, source_target_pairs={{0,1},{1,0},{2,3},{3,2},{4,5},{5,4},{6,7},{7,6},{8,9},{9,8},{10,11... | collective-permute-start | bytes 1966088 | tf_op jit(solution)/shard_map/ppermute | solution.py:645
  77.5 2.7 %collective-permute-start.21 = (f32[192,512]{1,0:T(8,128)S(1)}, f32[192,512]{1,0:T(8,128)S(1)}, u32[]{:S(2)}, u32[]{:S(2)}) collective-permute-start(f32[192,512]{1,0:T(8,128)S(1)} %get-tuple-element.29.time_mine), channel_id=1, source_target_pairs={{0,1},{1,0},{2,3},{3,2},{4,5},{5,4},{6,7},{7,6},{8,9},{9,8},{10,11... | collective-permute-start | bytes 1179656 | tf_op jit(solution)/shard_map/ppermute | solution.py:645
  (1 other events, 1.1 us)

commit v5 on v4

--- a/solution.py
+++ b/solution.py
@@ -143,15 +143,15 @@
         self.thin = up_to(3 * own + 8, LANES)
         self.copies = min(3, LANES // own)
         self.half = own // 2
-        code_rows = frames * lat
-        self.code_rows = up_to(code_rows, 16)
         self.half_pad = up_to(self.half, 16)
-        if self.wide - 9 * own >= cols and self.half >= code_rows:
+        self.code_rows = up_to(cols, 16)
+        if self.wide - 9 * own >= 8 * frames and self.half >= cols:
             self.code_row, self.code_lane = 0, 9 * own
             self.piece_rows = self.half
         else:
-            self.code_row, self.code_lane = up_to(self.half, 16), 0
-            self.piece_rows = self.code_row + up_to(code_rows, 16)
+            self.code_row, self.code_lane = self.half_pad, 0
+            self.piece_rows = self.code_row + self.code_rows
+        self.split = self.half == self.half_pad
         self.carries = self.wide - 9 * own >= LANES // 2 and own * (LANES // 2) >= 8 * chans
 
 
@@ -267,22 +267,22 @@
 
 def position_codes(z, codes, out):
     block, offset = z.code_lane // LANES, z.code_lane % LANES
+    run = 8 * z.frames
 
     def body(r):
-        raw = codes[r, :, block * LANES : (block + 1) * LANES].astype(F32)
-        raw = jnp.concatenate([raw, jnp.zeros((LANES - z.code_rows, LANES), F32)], axis=0)
-        turned = raw.T[offset : offset + z.cols]
-        lane = lax.broadcasted_iota(jnp.int32, turned.shape, 1)
-        frames = []
-        for t in range(z.frames):
-            values = lanes_down(turned, t * z.lat)
-            values = jnp.where(lane < z.lat, values, jnp.where(lane == z.lat, 1.0, 0.0))
-            frames.append(
-                values + pltpu.roll(values, 16, 1) + pltpu.roll(values, 32, 1)
-            )
-        out[rows_at(r, z)] = jnp.concatenate(frames, axis=0).astype(BF16)
+        raw = codes[r, : z.cols, block * LANES : (block + 1) * LANES].astype(F32)
+        lane = lax.broadcasted_iota(jnp.int32, raw.shape, 1)
+        raw = jnp.where(lane < run, lanes_down(raw, offset), 0.0)
+        raw = raw + pltpu.roll(raw, run, 1) + pltpu.roll(raw, 2 * run, 1)
+        frame = (lane % run) // 8
+        blocks = [jnp.where(frame == t, raw, 0.0) for t in range(z.frames)]
+        out[rows_at(r, z)] = jnp.concatenate(blocks, axis=0).astype(BF16)
 
     each_row(z, body)
+
+
+def frame_sum(z, raw):
+    return sum(raw[8 * t : 8 * t + 8] for t in range(z.frames))
 
 
 def piece_kernel(z, w, codes, ahead, behind, own_piece):
@@ -335,59 +335,94 @@
             store(behind, z.sp - distance - 1)
 
 
-def first_kernel(z, steps, piece_steps, *refs):
+def store_hidden(z, pre, logistic, hid_cat, r):
+    hidden = keep_own(z, (pre * logistic).astype(BF16).astype(F32))
+    moved = [frames_move(hidden, k, z.cols) for k in range(3)]
+    for b, block in enumerate(merge(moved, z.own)):
+        hid_cat[rows_at(r, z), b * LANES : (b + 1) * LANES] = block.astype(BF16)
+
+
+def activate(z, taps, hid_cat, slope):
+    def body(r):
+        pre = conv_row(z, taps, r)
+        logistic = 1.0 / (1.0 + jnp.exp(-pre))
+        store_hidden(z, pre, logistic, hid_cat, r)
+        slope[r] = logistic * (1.0 + pre * (1.0 - logistic))
+
+    each_row(z, body)
+
+
+def early_kernel(z, piece_steps, *refs):
     n = z.sp
-    shards, mine, other = refs[:n], refs[n : 2 * n], refs[2 * n : 3 * n]
-    wt, proj, halves = refs[3 * n : 3 * n + 3]
-    part, hid_cat, slope, inner_out, w_cat, pos, v = refs[3 * n + 3 : 3 * n + 10]
-    codes, taps, back, spots_of, thin = refs[3 * n + 10 :]
+    mine, other = refs[:n], refs[n : 2 * n]
+    wt, proj, halves = refs[2 * n : 2 * n + 3]
+    w_cat, pos, hid_cat, slope, table_out = refs[2 * n + 3 : 2 * n + 8]
+    codes, taps = refs[2 * n + 8 :]
+    decoder = lax.axis_index("sec") == 1
+    place_pieces(z, piece_steps, mine, other, w_cat, codes)
+
+    @pl.when(decoder)
+    def _():
+        zero_ends(z, taps)
+        p_cat = dot(proj[...], w_cat[...], NN)[:8]
+        half = halves[:8, :1]
+        row = lax.broadcasted_iota(jnp.int32, p_cat.shape, 0)
+        scaled = jnp.where(row == z.lat, -jnp.sum(p_cat, axis=0, keepdims=True), p_cat / half)
+        table = [term for term in thirds(scaled) for _ in range(z.frames)]
+        spare = jnp.zeros((LANES - 24 * z.frames, z.wide), F32)
+        table = jnp.concatenate(table + [spare], axis=0).astype(BF16)
+        position_codes(z, codes, pos)
+
+        def block(r0, rows):
+            place = rows_from(r0, rows, z)
+            taps[pl.ds(r0 + 1, rows)] = dot(pos[place], table, NN).reshape(rows, z.row, z.wide)
+
+        in_blocks(z, block)
+        activate(z, taps, hid_cat, slope)
+        by_tap = [
+            keep_own(z, lanes_down(p_cat[:, block * LANES : (block + 1) * LANES], offset))
+            for block, offset in spots(9, z.own)
+        ]
+        by_tap = jnp.concatenate(by_tap + [jnp.zeros((LANES - 72, LANES), F32)], axis=0)
+        table_out[...] = sum(
+            lanes_down(term, -c * z.own) for c, term in enumerate(thirds(by_tap)[: z.copies])
+        )
+
+    @pl.when(jnp.logical_not(decoder))
+    def _():
+        weights = dot(proj[...], wt[...], NT)[:8]
+        table_out[:8] = weights[:, :LANES]
+        table_out[8:16] = weights[:, LANES:] if z.thin > LANES else weights
+
+
+def back_weights(z, table):
+    if z.thin > LANES:
+        return jnp.concatenate([table[:8], table[8:16]], axis=1)
+    return table[:8]
+
+
+def first_kernel(z, steps, *refs):
+    n = z.sp
+    shards, (w_cat, wt, proj, table, rate) = refs[:n], refs[n : n + 5]
+    part, hid_cat, slope, inner_out, v = refs[n + 5 : n + 10]
+    taps, back, spots_of, thin = refs[n + 10 :]
     decoder = lax.axis_index("sec") == 1
     first = lax.axis_index("sp") == 0
-    zero_ends(z, taps)
     place_shards(z, steps, shards, v)
-    place_pieces(z, piece_steps, mine, other, w_cat, codes)
-
-    def store_hidden(pre, logistic, r):
-        hidden = keep_own(z, (pre * logistic).astype(BF16).astype(F32))
-        moved = [frames_move(hidden, k, z.cols) for k in range(3)]
-        for b, block in enumerate(merge(moved, z.own)):
-            hid_cat[rows_at(r, z), b * LANES : (b + 1) * LANES] = block.astype(BF16)
 
     @pl.when(decoder)
     def _():
         zero_ends(z, back)
-        p_cat = dot(proj[...], w_cat[...], NN)
-        half = halves[:, :1]
-        row = lax.broadcasted_iota(jnp.int32, p_cat.shape, 0)
-        scaled = jnp.where(
-            row == z.lat, -jnp.sum(p_cat, axis=0, keepdims=True), p_cat / half
-        )
-        table = jnp.concatenate(
-            list(thirds(scaled)) + [jnp.zeros((LANES - 48, z.wide), F32)], axis=0
-        ).astype(BF16)
-        position_codes(z, codes, pos)
-        by_tap = [
-            keep_own(z, lanes_down(p_cat[:8, block * LANES : (block + 1) * LANES], offset))
-            for block, offset in spots(9, z.own)
-        ]
-        by_tap = jnp.concatenate(by_tap + [jnp.zeros((LANES - 72, LANES), F32)], axis=0)
-        by_tap = sum(
-            lanes_down(term, -c * z.own) for c, term in enumerate(thirds(by_tap)[: z.copies])
-        ).astype(BF16)
+        by_tap = table[...].astype(BF16)
 
         def block(r0, rows):
             place = rows_from(r0, rows, z)
-            taps[pl.ds(r0 + 1, rows)] = dot(pos[place], table, NN).reshape(rows, z.row, z.wide)
             thin[place] = dot(v[place], wt[...], NT)
 
         in_blocks(z, block)
 
         def body(r):
-            pre = conv_row(z, taps, r)
-            logistic = 1.0 / (1.0 + jnp.exp(-pre))
-            store_hidden(pre, logistic, r)
-            rate = logistic * (1.0 + pre * (1.0 - logistic))
-            inner = keep_own(z, (later_row(z, thin, r) * rate).astype(BF16).astype(F32))
+            inner = keep_own(z, (later_row(z, thin, r) * rate[r]).astype(BF16).astype(F32))
             inner_out[r] = inner.astype(BF16)
             many = sum(lanes_down(inner, -c * z.own) for c in range(z.copies))
             back[r + 1] = dot(many.astype(BF16), by_tap, NT)
@@ -414,6 +449,8 @@
 
     @pl.when(jnp.logical_not(decoder))
     def _():
+        zero_ends(z, taps)
+
         def block(r0, rows):
             place = rows_from(r0, rows, z)
             taps[pl.ds(r0 + 1, rows)] = dot(v[place], w_cat[...], NN).reshape(
@@ -421,23 +458,17 @@
             )
 
         in_blocks(z, block)
-
-        def body(r):
-            pre = conv_row(z, taps, r)
-            logistic = 1.0 / (1.0 + jnp.exp(-pre))
-            store_hidden(pre, logistic, r)
-            slope[r] = logistic * (1.0 + pre * (1.0 - logistic))
-
-        each_row(z, body)
-        weights = dot(proj[...], wt[...], NT)[:8]
+        activate(z, taps, hid_cat, slope)
+        weights = back_weights(z, table)
         whole = dot(proj[...], v[...], NT)[:8]
         part[...] = sum3(dot(stack3(weights), hid_cat[...], NT)) + jnp.where(first, whole, 0.0)
 
 
 def second_kernel(z, scale, *refs):
-    v, w_cat, pos, wt, proj, halves, hid_cat, slope, inner_in, total, received = refs[:11]
-    big, time, part = refs[11:14]
-    shifts, inner_cat, thin = refs[14:]
+    v, w_cat, pos, wt, proj, halves, table, hid_dec, hid_cat, slope, inner_in, total, received = refs[:13]
+    big, send, time, part = refs[13:17]
+    shifts, inner_cat, thin = refs[17:]
+    core = lax.axis_index("dp")
     decoder = lax.axis_index("sec") == 1
     first = lax.axis_index("sp") == 0
     for j in range(3):
@@ -445,22 +476,24 @@
 
     def put_out(kernel_grad, proj_part):
         part[...] = proj_part
-        if not z.carries:
-            big[...] = kernel_grad.astype(BF16)
-            return
         side = z.wide - LANES
-        big[:, :side] = kernel_grad[:, :side].astype(BF16)
-        pieces = []
-        for b in range(2 * z.chans // LANES):
-            block = proj_part[:, (b // 2) * LANES : (b // 2 + 1) * LANES]
-            pieces.append(block if b % 2 else pltpu.roll(block, LANES // 2, 1))
-        carried = jnp.concatenate(pieces, axis=0)
-        lane = lax.broadcasted_iota(jnp.int32, carried.shape, 1)
+        if z.carries:
+            pieces = []
+            for b in range(2 * z.chans // LANES):
+                block = proj_part[:, (b // 2) * LANES : (b // 2 + 1) * LANES]
+                pieces.append(block if b % 2 else pltpu.roll(block, LANES // 2, 1))
+            carried = jnp.concatenate(pieces, axis=0)
+            lane = lax.broadcasted_iota(jnp.int32, carried.shape, 1)
         for j in range(z.sp):
-            rows = slice(j * z.own, (j + 1) * z.own)
-            big[rows, side:] = jnp.where(
-                lane < LANES // 2, kernel_grad[rows, side:], carried
-            ).astype(BF16)
+            rows = kernel_grad[j * z.own : (j + 1) * z.own]
+            if z.carries:
+                tail = jnp.where(lane < LANES // 2, rows[:, side:], carried)
+                rows = jnp.concatenate([rows[:, :side], tail], axis=1) if side else tail
+            if z.split:
+                big[j] = jnp.where(core == 0, rows[: z.half], rows[z.half :])
+                send[j] = jnp.where(core == 0, rows[z.half :], rows[: z.half]).astype(BF16)
+            else:
+                big[j] = rows
 
     @pl.when(decoder)
     def _():
@@ -475,12 +508,12 @@
             row = lax.broadcasted_iota(jnp.int32, raw.shape, 0)
             return jnp.where(row < z.lat, raw / half - raw[z.lat : z.lat + 1], 0.0)
 
-        short = latent_rows(dot(pos[...], inner_cat[...], TN)[:8])
+        short = latent_rows(frame_sum(z, dot(pos[...], inner_cat[...], TN)))
         proj8 = proj[:8].astype(F32)
         proj24 = jnp.concatenate([proj8] * 3, axis=0).astype(BF16)
         kernel_grad = dot(proj24, stack3(short), TN) * scale
-        time[...] = dot(hid_cat[...], v[...], TN)[: 3 * z.own] * scale
-        whole = latent_rows(dot(pos[...], v[...], TN)[:8])
+        time[...] = dot(hid_dec[...], v[...], TN)[: 3 * z.own] * scale
+        whole = latent_rows(frame_sum(z, dot(pos[...], v[...], TN)))
         partial = sum3(dot(stack3(short), w_cat[...], NT))
         put_out(kernel_grad, (partial + jnp.where(first, whole, 0.0)) * scale)
 
@@ -488,7 +521,7 @@
     def _():
         bounded = jnp.tanh(total[...])
         grad = received[...] * (1.0 - bounded * bounded)
-        back = dot(proj[...], wt[...], NT)[:8]
+        back = back_weights(z, table)
         gh, gm, gl = thirds(grad)
         bh, bm, bl = thirds(back)
         left = jnp.concatenate([gh, gh, gm, gh, gl, gm], axis=0).astype(BF16)
@@ -513,35 +546,53 @@
         put_out(kernel_grad, (partial + jnp.where(first, whole, 0.0)) * scale)
 
 
+def meet_kernel(mine, other, both):
+    both[...] = (mine[...] + other[...].astype(F32)).astype(BF16)
+
+
 def last_kernel(z, mine, other, time_mine, time_other, space, time, part):
     time[...] = time_mine[...] + time_other[...]
+    core = lax.axis_index("dp")
+    per = LANES // z.own
+    if z.split:
+        low = pl.ds(pl.multiple_of(core * z.half, z.half), z.half)
+        high = pl.ds(pl.multiple_of((1 - core) * z.half, z.half), z.half)
+        sources = ((low, lambda at: mine[at].astype(F32)), (high, lambda at: other[at].astype(F32)))
+    else:
+        sources = ((slice(0, z.own), lambda at: mine[at].astype(F32) + other[at].astype(F32)),)
+    for rows, source in sources:
+        for tap, (block, offset) in enumerate(spots(9, z.own)):
+            for m in range(z.chans // LANES):
+                total = None
+                for p in range(per):
+                    at = (m * per + p, slice(None), slice(block * LANES, (block + 1) * LANES))
+                    value = lanes_down(source(at), offset - p * z.own)
+                    if total is None:
+                        total = value
+                    else:
+                        lane = lax.broadcasted_iota(jnp.int32, value.shape, 1)
+                        total = jnp.where(lane < p * z.own, total, value)
+                space[tap, rows, m * LANES : (m + 1) * LANES] = total
     if z.carries:
         side = slice(z.wide - LANES, z.wide)
-        carried = 0.0
-        for j in range(z.sp):
-            carried = carried + (mine[j, :, side].astype(F32) + other[j, :, side].astype(F32))
+        one, two = (
+            sum(source[j, :, side].astype(F32) for j in range(z.sp)) for source in (mine, other)
+        )
+        if z.split:
+            carried = jnp.concatenate(
+                [jnp.where(core == 0, one, two), jnp.where(core == 0, two, one)], axis=0
+            )
+        else:
+            carried = one + two
         lane = lax.broadcasted_iota(jnp.int32, (8, LANES), 1)
         for m in range(z.chans // LANES):
             low = pltpu.roll(carried[16 * m : 16 * m + 8], LANES // 2, 1)
             high = carried[16 * m + 8 : 16 * m + 16]
             both = jnp.where(lane < LANES // 2, low, high)
-            part[:, m * LANES : (m + 1) * LANES] = both[: z.lat]
+            for l in range(z.lat):
+                part[l, :, m * LANES : (m + 1) * LANES] = both[l : l + 1]
     else:
         part[...] = jnp.zeros(part.shape, F32)
-    per = LANES // z.own
-    for tap, (block, offset) in enumerate(spots(9, z.own)):
-        for m in range(z.chans // LANES):
-            total = None
-            for p in range(per):
-                at = (m * per + p, slice(None), slice(block * LANES, (block + 1) * LANES))
-                value = mine[at].astype(F32) + other[at].astype(F32)
-                value = lanes_down(value, offset - p * z.own)
-                if total is None:
-                    total = value
-                else:
-                    lane = lax.broadcasted_iota(jnp.int32, value.shape, 1)
-                    total = jnp.where(lane < p * z.own, total, value)
-            space[tap, :, m * LANES : (m + 1) * LANES] = total
 
 
 VM = pl.BlockSpec(memory_space=pltpu.VMEM)
@@ -560,12 +611,12 @@
     room = 20 * 1024 * 1024 + 5 * z.count * chans * 4 // 2 * (1 if z.sp > 8 else 0)
     params = pltpu.CompilerParams(vmem_limit_bytes=min(room, 60 * 1024 * 1024))
 
-    codes = jnp.transpose(code_index[0, :, :, 0], (1, 0, 2)).reshape(frames * lat, cols)
+    codes = jnp.transpose(code_index[0, :, :, 0].astype(F32), (2, 1, 0))
+    codes = jnp.concatenate([codes, jnp.ones((cols, frames, 1), F32)], axis=2)
+    codes = jnp.pad(codes, ((0, 0), (0, 0), (0, 7 - lat))).reshape(cols, 8 * frames)
     left = z.code_lane % LANES
-    codes = jnp.pad(
-        codes.astype(F32),
-        ((0, (z.half if z.code_row == 0 else z.code_rows) - frames * lat), (left, LANES - left - cols)),
-    )
+    code_rows = z.half if z.code_row == 0 else z.code_rows
+    codes = jnp.pad(codes, ((0, code_rows - cols), (left, LANES - left - 8 * frames)))
     ahead, behind, own_piece = pl.pallas_call(
         functools.partial(piece_kernel, z),
         out_shape=(
@@ -587,21 +638,36 @@
     half = jnp.pad((levels.astype(F32) - 1.0) * 0.5, (0, 16 - lat), constant_values=1.0)
     halves = jnp.broadcast_to(half[:, None], (16, LANES))
 
-    part, hid_cat, slope, inner, w_cat, pos, v = pl.pallas_call(
-        functools.partial(first_kernel, z, steps, piece_steps),
+    w_cat, pos, hid_dec, rate, table = pl.pallas_call(
+        functools.partial(early_kernel, z, piece_steps),
+        out_shape=(
+            shaped((chans, z.wide), BF16),
+            shaped((z.count, LANES), BF16),
+            shaped((z.count, z.thin), BF16),
+            shaped((z.sp, z.row, LANES), F32),
+            shaped((LANES, LANES), F32),
+        ),
+        in_specs=[VM] * (2 * z.sp + 3),
+        out_specs=(VM,) * 5,
+        scratch_shapes=[
+            pltpu.VMEM((z.sp, z.code_rows, z.wide), BF16),
+            pltpu.VMEM((z.sp + 2, z.row, z.wide), F32),
+        ],
+        compiler_params=params,
+        name="early",
+    )(*mine, *other, wt, proj, halves)
+    part, hid_cat, slope, inner, v = pl.pallas_call(
+        functools.partial(first_kernel, z, steps),
         out_shape=(
             shaped((8, z.count), F32),
             shaped((z.count, z.thin), BF16),
             shaped((z.sp, z.row, LANES), F32),
             shaped((z.sp, z.row, LANES), BF16),
-            shaped((chans, z.wide), BF16),
-            shaped((z.count, LANES), BF16),
             shaped((z.count, chans), BF16),
         ),
-        in_specs=[VM] * (3 * z.sp + 3),
-        out_specs=(VM,) * 7,
+        in_specs=[VM] * (z.sp + 5),
+        out_specs=(VM,) * 5,
         scratch_shapes=[
-            pltpu.VMEM((z.sp, z.code_rows, z.wide), BF16),
             pltpu.VMEM((z.sp + 2, z.row, z.wide), F32),
             pltpu.VMEM((z.sp + 2, z.row, LANES), F32),
             pltpu.VMEM((z.count, LANES), F32),
@@ -609,19 +675,21 @@
         ],
         compiler_params=params,
         name="first",
-    )(*shards, *mine, *other, wt, proj, halves)
+    )(*shards, w_cat, wt, proj, table, rate)
     swap = [(0, 1), (1, 0)]
     total = swap_sum(part, "sp")
     received = lax.ppermute(total, "sec", swap)
-    big, time, part = pl.pallas_call(
+    part_rows = (z.sp, z.half if z.split else own, z.wide)
+    big, send, time, part = pl.pallas_call(
         functools.partial(second_kernel, z, scale),
         out_shape=(
-            shaped((chans, z.wide), BF16),
+            shaped(part_rows, F32),
+            shaped(part_rows, BF16),
             shaped((3 * own, chans), F32),
             shaped((8, chans), F32),
         ),
-        in_specs=[VM] * 11,
-        out_specs=(VM,) * 3,
+        in_specs=[VM] * 13,
+        out_specs=(VM,) * 4,
         scratch_shapes=[
             pltpu.VMEM((3, z.sp + 2, z.row, LANES), BF16),
             pltpu.VMEM((z.count, z.wide), BF16),
@@ -629,14 +697,23 @@
         ],
         compiler_params=params,
         name="second",
-    )(v, w_cat, pos, wt, proj, halves, hid_cat, slope, inner, total, received)
-    big = lax.all_to_all(big.reshape(z.sp, own, z.wide), "sp", 0, 0, tiled=True)
+    )(v, w_cat, pos, wt, proj, halves, table, hid_dec, hid_cat, slope, inner, total, received)
+    if z.split:
+        big = pl.pallas_call(
+            meet_kernel,
+            out_shape=shaped(part_rows, BF16),
+            in_specs=[VM] * 2,
+            out_specs=VM,
+            compiler_params=params,
+            name="meet",
+        )(big, lax.ppermute(send, "dp", swap))
+    big = lax.all_to_all(big.astype(BF16), "sp", 0, 0, tiled=True)
     space, time, carried = pl.pallas_call(
         functools.partial(last_kernel, z),
         out_shape=(
             shaped((9, own, chans), F32),
             shaped((3 * own, chans), F32),
-            shaped((lat, chans), F32),
+            shaped((lat, 1, chans), F32),
         ),
         in_specs=[VM] * 4,
         out_specs=(VM,) * 3,
@@ -644,7 +721,7 @@
         name="last",
     )(big, lax.ppermute(big, "dp", swap), time, lax.ppermute(time, "dp", swap))
     if z.carries:
-        part = carried
+        part = carried.reshape(lat, chans)
     else:
         part = swap_sum(part, "sp")
         part = (part + lax.ppermute(part, "dp", swap))[:lat]

time: 82.7 us -> 79.1 us (0.956)
  blocking collectives: 18.9 us -> 0 us
  waiting for transfers between devices: 23.5 us -> 36.4 us
  starting transfers between devices: 27.1 us -> 29.4 us
    all_to_all x1 -> x0, blocking collectives: 18.9 us -> none  [local(): big = lax.all_to_all(big.reshape(z.sp, own, z.wide), 'sp', 0, 0, tiled=True)]
    all_to_all x0 -> x1, waiting for transfers between devices: none -> 10.6 us  [local(): big = lax.all_to_all(big.astype(BF16), 'sp', 0, 0, tiled=True)]
    all_to_all x0 -> x1, starting transfers between devices: none -> 5.79 us  [local(): big = lax.all_to_all(big.astype(BF16), 'sp', 0, 0, tiled=True)]
    ppermute x1, starting transfers between devices: 3.47 us -> 0.77 us  [local(): received = lax.ppermute(total, 'sec', swap)]
    ppermute x1, waiting for transfers between devices: 2.15 us -> 0.01 us  [local(): lax.ppermute(time, 'dp', swap)]
    ppermute x0 -> x1, waiting for transfers between devices: none -> 1.63 us  [local(): lax.ppermute(send, 'dp', swap)]
    ppermute x1, waiting for transfers between devices: 0.01 us -> 1.62 us  [local(): lax.ppermute(big, 'dp', swap)]
    ppermute x1, waiting for transfers between devices: 1.98 us -> 3.24 us  [local(): received = lax.ppermute(total, 'sec', swap)]
  transfers between devices with their start and end apart: 22 -> 24, of which waited for: 14 -> 16; matrix products, arithmetic and copies ran while one was open for 3% -> 3% of each run, Pallas kernels for 1% -> 2%
where the time goes in v5:
time: 79.1 us; the launch traced here: 78.7 us
  waiting for transfers between devices  36.4 us (46%)
  starting transfers between devices  29.4 us (37%)
  Pallas kernels  8.55 us (11%)
  other arithmetic  2.15 us (3%)
  local copies, waits for them, and re-layouts  1.45 us (2%)
    all_to_all x1, waiting for transfers between devices, local(): big = lax.all_to_all(big.astype(BF16), 'sp', 0, 0, tiled=True)  10.6 us
    ppermute x3, waiting for transfers between devices, swap_sum(): lax.ppermute(values, axis, [(i, i ^ bit) for i in range(count)])  7.5 us
    ppermute x3, starting transfers between devices, ring_exchange(): second = lax.ppermute(second, 'sp', down)  6.29 us
    all_to_all x1, starting transfers between devices, local(): big = lax.all_to_all(big.astype(BF16), 'sp', 0, 0, tiled=True)  5.79 us
    ppermute x3, starting transfers between devices, ring_exchange(): ahead = lax.ppermute(ahead, 'sp', up)  5.61 us
    ppermute x3, starting transfers between devices, swap_sum(): lax.ppermute(values, axis, [(i, i ^ bit) for i in range(count)])  5.47 us
    ppermute x4, waiting for transfers between devices, ring_exchange(): first = lax.ppermute(first, 'sp', up)  4.8 us
    ppermute x4, waiting for transfers between devices, ring_exchange(): behind = lax.ppermute(behind, 'sp', down)  4.2 us
  transfers between devices with their start and end apart: 24, of which 16 were waited for; matrix products, arithmetic and copies ran while one was open for 3% of the time, Pallas kernels for 2%

profile of v5, /device:TPU:0, one launch (start us, length us, event | category | flops | bytes accessed | tf_op | source)
XLA Modules:
  0.0 78.7 jit_solution(3056637168173098465)
XLA Ops:
  0.6 3.0 %collective-permute-start.1 = (bf16[160,512]{1,0:T(8,128)(2,1)}, bf16[160,512]{1,0:T(8,128)(2,1)S(1)}, u32[]{:S(2)}, u32[]{:S(2)}) collective-permute-start(bf16[160,512]{1,0:T(8,128)(2,1)} %bitcast.43), channel_id=1, source_target_pairs={{4,0},{8,4},{12,8},{14,12},{10,14},{6,10},{2,6},{0,2},{5,1},{9,5},... | collective-permute-start | bytes 491528 | tf_op jit(solution)/shard_map/ppermute | solution.py:56
  6.7 2.0 %collective-permute-start.7 = (bf16[3,32,640]{2,1,0:T(8,128)(2,1)S(1)}, bf16[3,32,640]{2,1,0:T(8,128)(2,1)S(1)}, u32[]{:S(2)}, u32[]{:S(2)}) collective-permute-start(bf16[3,32,640]{2,1,0:T(8,128)(2,1)S(1)} %get-tuple-element.23), channel_id=1, source_target_pairs={{0,4},{4,8},{8,12},{12,14},{14,10},{10,6},{6,2},{2,0},{1,5},{5,9},... | collective-permute-start | bytes 368648 | tf_op jit(solution)/shard_map/ppermute | solution.py:59
  10.1 2.0 %collective-permute-done.7 = bf16[3,32,640]{2,1,0:T(8,128)(2,1)S(1)} collective-permute-done((bf16[3,32,640]{2,1,0:T(8,128)(2,1)S(1)}, bf16[3,32,640]{2,1,0:T(8,128)(2,1)S(1)}, u32[]{:S(2)}, u32[]{:S(2)}) %collective-permute-start.7) | collective-permute-done | bytes 122912 | tf_op jit(solution)/shard_map/ppermute | solution.py:59
  12.2 1.5 %collective-permute-start.9 = (bf16[2,32,640]{2,1,0:T(8,128)(2,1)S(1)}, bf16[2,32,640]{2,1,0:T(8,128)(2,1)S(1)}, u32[]{:S(2)}, u32[]{:S(2)}) collective-permute-start(bf16[2,32,640]{2,1,0:T(8,128)(2,1)S(1)} %slice.78), channel_id=1, source_target_pairs={{0,4},{4,8},{8,12},{12,14},{14,10},{10,6},{6,2},{2,0},{1,5},{5,9},... | collective-permute-start | bytes 245768 | tf_op jit(solution)/shard_map/ppermute | solution.py:59
  14.3 1.7 %collective-permute-start.3 = (bf16[160,512]{1,0:T(8,128)(2,1)S(1)}, bf16[160,512]{1,0:T(8,128)(2,1)S(1)}, u32[]{:S(2)}, u32[]{:S(2)}) collective-permute-start(bf16[160,512]{1,0:T(8,128)(2,1)S(1)} %collective-permute-done.1.refs_2_), channel_id=1, source_target_pairs={{4,0},{8,4},{12,8},{14,12},{10,14},{6,10},{2,6},{0,2},{5,1},{9,5},... | collective-permute-start | bytes 491528 | tf_op jit(solution)/shard_map/ppermute | solution.py:56
  16.8 2.1 %collective-permute-start.11 = (bf16[1,32,640]{2,1,0:T(8,128)(2,1)S(1)}, bf16[1,32,640]{2,1,0:T(8,128)(2,1)S(1)}, u32[]{:S(2)}, u32[]{:S(2)}) collective-permute-start(bf16[1,32,640]{2,1,0:T(8,128)(2,1)S(1)} %get-tuple-element.59), channel_id=1, source_target_pairs={{0,4},{4,8},{8,12},{12,14},{14,10},{10,6},{6,2},{2,0},{1,5},{5,9},... | collective-permute-start | bytes 122888 | tf_op jit(solution)/shard_map/ppermute | solution.py:59
  22.0 1.9 %collective-permute-done.12 = bf16[2,32,640]{2,1,0:T(8,128)(2,1)S(1)} collective-permute-done((bf16[2,32,640]{2,1,0:T(8,128)(2,1)S(1)}, bf16[2,32,640]{2,1,0:T(8,128)(2,1)S(1)}, u32[]{:S(2)}, u32[]{:S(2)}) %collective-permute-start.12) | collective-permute-done | bytes 81952 | tf_op jit(solution)/shard_map/ppermute | solution.py:63
  25.2 1.5 %collective-permute-start.5 = (bf16[160,512]{1,0:T(8,128)(2,1)S(1)}, bf16[160,512]{1,0:T(8,128)(2,1)S(1)}, u32[]{:S(2)}, u32[]{:S(2)}) collective-permute-start(bf16[160,512]{1,0:T(8,128)(2,1)S(1)} %collective-permute-done.3.refs_4_), channel_id=1, source_target_pairs={{4,0},{8,4},{12,8},{14,12},{10,14},{6,10},{2,6},{0,2},{5,1},{9,5},... | collective-permute-start | bytes 491528 | tf_op jit(solution)/shard_map/ppermute | solution.py:56
  26.8 1.3 %collective-permute-done.13 = bf16[1,32,640]{2,1,0:T(8,128)(2,1)S(1)} collective-permute-done((bf16[1,32,640]{2,1,0:T(8,128)(2,1)S(1)}, bf16[1,32,640]{2,1,0:T(8,128)(2,1)S(1)}, u32[]{:S(2)}, u32[]{:S(2)}) %collective-permute-start.13) | collective-permute-done | bytes 40992 | tf_op jit(solution)/shard_map/ppermute | solution.py:63
  28.2 1.6 %collective-permute-start.6 = (bf16[160,512]{1,0:T(8,128)(2,1)S(1)}, bf16[160,512]{1,0:T(8,128)(2,1)S(1)}, u32[]{:S(2)}, u32[]{:S(2)}) collective-permute-start(bf16[160,512]{1,0:T(8,128)(2,1)S(1)} %collective-permute-done.4.refs_5_), channel_id=1, source_target_pairs={{0,4},{4,8},{8,12},{12,14},{14,10},{10,6},{6,2},{2,0},{1,5},{5,9},... | collective-permute-start | bytes 491528 | tf_op jit(solution)/shard_map/ppermute | solution.py:51
  30.6 4.2 %collective-permute-done.6.refs_7_ = bf16[160,512]{1,0:T(8,128)(2,1)S(1)} collective-permute-done((bf16[160,512]{1,0:T(8,128)(2,1)S(1)}, bf16[160,512]{1,0:T(8,128)(2,1)S(1)}, u32[]{:S(2)}, u32[]{:S(2)}) %collective-permute-start.6) | collective-permute-done | bytes 163872 | tf_op jit(solution)/shard_map/ppermute | solution.py:51
  34.8 1.9 %first.1 = (f32[8,1280]{1,0:T(8,128)S(1)}, bf16[1280,256]{1,0:T(8,128)(2,1)S(1)}, f32[8,160,128]{2,1,0:T(8,128)S(1)}, bf16[8,160,128]{2,1,0:T(8,128)(2,1)S(1)}, bf16[1280,512]{1,0:T(8,128)(2,1)S(1)}) custom-call(bf16[160,512]{1,0:T(8,128)(2,1)S(1)} %bitcast.45, bf16[160,512]{1,0:T(8,128)(2,1)S(1)} %collective-permute-done.refs_1_, ...), custom_call_target="tpu_custom_call" | custom-call | tf_op jit(solution)/shard_map/first/pallas_call | solution.py:659
  37.9 2.9 %collective-permute-done.16 = f32[8,1280]{1,0:T(8,128)S(1)} collective-permute-done((f32[8,1280]{1,0:T(8,128)S(1)}, f32[8,1280]{1,0:T(8,128)S(1)}, u32[]{:S(2)}, u32[]{:S(2)}) %collective-permute-start.16) | collective-permute-done | bytes 40992 | tf_op jit(solution)/shard_map/ppermute | solution.py:76
  40.8 1.5 %collective-permute-start.17 = (f32[8,1280]{1,0:T(8,128)S(1)}, f32[8,1280]{1,0:T(8,128)S(1)}, u32[]{:S(2)}, u32[]{:S(2)}) collective-permute-start(f32[8,1280]{1,0:T(8,128)S(1)} %add.22), channel_id=1, source_target_pairs={{0,4},{2,6},{4,0},{6,2},{8,12},{10,14},{12,8},{14,10},{1,5},{3,7},... | collective-permute-start | bytes 122888 | tf_op jit(solution)/shard_map/ppermute | solution.py:76
  42.3 2.5 %collective-permute-done.17 = f32[8,1280]{1,0:T(8,128)S(1)} collective-permute-done((f32[8,1280]{1,0:T(8,128)S(1)}, f32[8,1280]{1,0:T(8,128)S(1)}, u32[]{:S(2)}, u32[]{:S(2)}) %collective-permute-start.17) | collective-permute-done | bytes 40992 | tf_op jit(solution)/shard_map/ppermute | solution.py:76
  44.8 2.7 %collective-permute-start.18 = (f32[8,1280]{1,0:T(8,128)S(1)}, f32[8,1280]{1,0:T(8,128)S(1)}, u32[]{:S(2)}, u32[]{:S(2)}) collective-permute-start(f32[8,1280]{1,0:T(8,128)S(1)} %add.23), channel_id=1, source_target_pairs={{0,8},{2,10},{4,12},{6,14},{8,0},{10,2},{12,4},{14,6},{1,9},{3,11}... | collective-permute-start | bytes 122888 | tf_op jit(solution)/shard_map/ppermute | solution.py:76
  47.5 2.2 %collective-permute-done.18 = f32[8,1280]{1,0:T(8,128)S(1)} collective-permute-done((f32[8,1280]{1,0:T(8,128)S(1)}, f32[8,1280]{1,0:T(8,128)S(1)}, u32[]{:S(2)}, u32[]{:S(2)}) %collective-permute-start.18) | collective-permute-done | bytes 40992 | tf_op jit(solution)/shard_map/ppermute | solution.py:76
  50.5 3.2 %collective-permute-done.19.refs_12_ = f32[8,1280]{1,0:T(8,128)S(1)} collective-permute-done((f32[8,1280]{1,0:T(8,128)S(1)}, f32[8,1280]{1,0:T(8,128)S(1)}, u32[]{:S(2)}, u32[]{:S(2)}) %collective-permute-start.19) | collective-permute-done | bytes 40992 | tf_op jit(solution)/shard_map/ppermute | solution.py:681
  53.7 3.2 %second.1 = (f32[8,32,640]{2,1,0:T(8,128)S(1)}, bf16[8,32,640]{2,1,0:T(8,128)(2,1)S(1)}, f32[192,512]{1,0:T(8,128)S(1)}, f32[8,512]{1,0:T(8,128)}) custom-call(bf16[1280,512]{1,0:T(8,128)(2,1)S(1)} %get-tuple-element.28.refs_0_, bf16[512,640]{1,0:T(8,128)(2,1)S(1)} %get-tuple-element.25.refs_8_.refs_1_, bf16[1280,128]{1,0:T(8,128)(2,1)S(1)} %get-tuple-element.29.refs_2_, ...), custom_call_target="tpu_custom_call" | custom-call | tf_op jit(solution)/shard_map/second/pallas_call | solution.py:683
  56.9 1.6 %collective-permute-done.20.other = bf16[8,32,640]{2,1,0:T(8,128)(2,1)S(1)} collective-permute-done((bf16[8,32,640]{2,1,0:T(8,128)(2,1)S(1)}, bf16[8,32,640]{2,1,0:T(8,128)(2,1)S(1)}, u32[]{:S(2)}, u32[]{:S(2)}) %collective-permute-start.20) | collective-permute-done | bytes 327712 | tf_op jit(solution)/shard_map/ppermute | solution.py:709
  59.3 5.8 %all-to-all-start = ((bf16[8,32,640]{2,1,0:T(8,128)(2,1)}), bf16[8,32,640]{2,1,0:T(8,128)(2,1)S(1)}, u32[]{:S(2)}, u32[]{:S(2)}) async-start(bf16[8,32,640]{2,1,0:T(8,128)(2,1)} %meet.1), calls=%async_computation | async-start | bytes 655360 | tf_op jit(solution)/shard_map/all_to_all | solution.py:710
  65.1 10.6 %all-to-all-done.mine = bf16[8,32,640]{2,1,0:T(8,128)(2,1)S(1)} async-done(((bf16[8,32,640]{2,1,0:T(8,128)(2,1)}), bf16[8,32,640]{2,1,0:T(8,128)(2,1)S(1)}, u32[]{:S(2)}, u32[]{:S(2)}) %all-to-all-start) | async-done | bytes 327712 | tf_op jit(solution)/shard_map/all_to_all | solution.py:710
  75.7 1.6 %collective-permute-done.21.other = bf16[8,32,640]{2,1,0:T(8,128)(2,1)S(1)} collective-permute-done((bf16[8,32,640]{2,1,0:T(8,128)(2,1)S(1)}, bf16[8,32,640]{2,1,0:T(8,128)(2,1)S(1)}, u32[]{:S(2)}, u32[]{:S(2)}) %collective-permute-start.21) | collective-permute-done | bytes 327712 | tf_op jit(solution)/shard_map/ppermute | solution.py:722
  77.3 1.4 %last.1 = (f32[9,64,512]{2,1,0:T(8,128)}, f32[192,512]{1,0:T(8,128)}, f32[6,1,512]{2,1,0:T(1,128)}) custom-call(bf16[8,32,640]{2,1,0:T(8,128)(2,1)S(1)} %all-to-all-done.mine, bf16[8,32,640]{2,1,0:T(8,128)(2,1)S(1)} %collective-permute-done.21.other, f32[192,512]{1,0:T(8,128)S(1)} %get-tuple-element.37.time_mine, ...), custom_call_target="tpu_custom_call" | custom-call | tf_op jit(solution)/shard_map/last/pallas_call | solution.py:711
  (62 shorter events, 13.9 us)
Async XLA Ops:
  0.6 13.7 %collective-permute-start.1 = (bf16[160,512]{1,0:T(8,128)(2,1)}, bf16[160,512]{1,0:T(8,128)(2,1)S(1)}, u32[]{:S(2)}, u32[]{:S(2)}) collective-permute-start(bf16[160,512]{1,0:T(8,128)(2,1)} %bitcast.43), channel_id=1, source_target_pairs={{4,0},{8,4},{12,8},{14,12},{10,14},{6,10},{2,6},{0,2},{5,1},{9,5},... | collective-permute-start | bytes 491528 | tf_op jit(solution)/shard_map/ppermute | solution.py:56
  3.6 12.4 %collective-permute-start = (bf16[160,512]{1,0:T(8,128)(2,1)}, bf16[160,512]{1,0:T(8,128)(2,1)S(1)}, u32[]{:S(2)}, u32[]{:S(2)}) collective-permute-start(bf16[160,512]{1,0:T(8,128)(2,1)} %bitcast.44), channel_id=1, source_target_pairs={{0,4},{4,8},{8,12},{12,14},{14,10},{10,6},{6,2},{2,0},{1,5},{5,9},... | collective-permute-start | bytes 491528 | tf_op jit(solution)/shard_map/ppermute | solution.py:51
  6.7 5.5 %collective-permute-start.7 = (bf16[3,32,640]{2,1,0:T(8,128)(2,1)S(1)}, bf16[3,32,640]{2,1,0:T(8,128)(2,1)S(1)}, u32[]{:S(2)}, u32[]{:S(2)}) collective-permute-start(bf16[3,32,640]{2,1,0:T(8,128)(2,1)S(1)} %get-tuple-element.23), channel_id=1, source_target_pairs={{0,4},{4,8},{8,12},{12,14},{14,10},{10,6},{6,2},{2,0},{1,5},{5,9},... | collective-permute-start | bytes 368648 | tf_op jit(solution)/shard_map/ppermute | solution.py:59
  8.7 5.3 %collective-permute-start.8 = (bf16[4,32,640]{2,1,0:T(8,128)(2,1)S(1)}, bf16[4,32,640]{2,1,0:T(8,128)(2,1)S(1)}, u32[]{:S(2)}, u32[]{:S(2)}) collective-permute-start(bf16[4,32,640]{2,1,0:T(8,128)(2,1)S(1)} %get-tuple-element.24), channel_id=1, source_target_pairs={{4,0},{8,4},{12,8},{14,12},{10,14},{6,10},{2,6},{0,2},{5,1},{9,5},... | collective-permute-start | bytes 491528 | tf_op jit(solution)/shard_map/ppermute | solution.py:63
  12.2 4.6 %collective-permute-start.9 = (bf16[2,32,640]{2,1,0:T(8,128)(2,1)S(1)}, bf16[2,32,640]{2,1,0:T(8,128)(2,1)S(1)}, u32[]{:S(2)}, u32[]{:S(2)}) collective-permute-start(bf16[2,32,640]{2,1,0:T(8,128)(2,1)S(1)} %slice.78), channel_id=1, source_target_pairs={{0,4},{4,8},{8,12},{12,14},{14,10},{10,6},{6,2},{2,0},{1,5},{5,9},... | collective-permute-start | bytes 245768 | tf_op jit(solution)/shard_map/ppermute | solution.py:59
  14.0 5.4 %collective-permute-start.10 = (bf16[3,32,640]{2,1,0:T(8,128)(2,1)S(1)}, bf16[3,32,640]{2,1,0:T(8,128)(2,1)S(1)}, u32[]{:S(2)}, u32[]{:S(2)}) collective-permute-start(bf16[3,32,640]{2,1,0:T(8,128)(2,1)S(1)} %slice.80), channel_id=1, source_target_pairs={{4,0},{8,4},{12,8},{14,12},{10,14},{6,10},{2,6},{0,2},{5,1},{9,5},... | collective-permute-start | bytes 368648 | tf_op jit(solution)/shard_map/ppermute | solution.py:63
  14.3 10.9 %collective-permute-start.3 = (bf16[160,512]{1,0:T(8,128)(2,1)S(1)}, bf16[160,512]{1,0:T(8,128)(2,1)S(1)}, u32[]{:S(2)}, u32[]{:S(2)}) collective-permute-start(bf16[160,512]{1,0:T(8,128)(2,1)S(1)} %collective-permute-done.1.refs_2_), channel_id=1, source_target_pairs={{4,0},{8,4},{12,8},{14,12},{10,14},{6,10},{2,6},{0,2},{5,1},{9,5},... | collective-permute-start | bytes 491528 | tf_op jit(solution)/shard_map/ppermute | solution.py:56
  16.1 5.3 %collective-permute-start.2 = (bf16[160,512]{1,0:T(8,128)(2,1)S(1)}, bf16[160,512]{1,0:T(8,128)(2,1)S(1)}, u32[]{:S(2)}, u32[]{:S(2)}) collective-permute-start(bf16[160,512]{1,0:T(8,128)(2,1)S(1)} %collective-permute-done.refs_1_), channel_id=1, source_target_pairs={{0,4},{4,8},{8,12},{12,14},{14,10},{10,6},{6,2},{2,0},{1,5},{5,9},... | collective-permute-start | bytes 491528 | tf_op jit(solution)/shard_map/ppermute | solution.py:51
  16.8 10.0 %collective-permute-start.11 = (bf16[1,32,640]{2,1,0:T(8,128)(2,1)S(1)}, bf16[1,32,640]{2,1,0:T(8,128)(2,1)S(1)}, u32[]{:S(2)}, u32[]{:S(2)}) collective-permute-start(bf16[1,32,640]{2,1,0:T(8,128)(2,1)S(1)} %get-tuple-element.59), channel_id=1, source_target_pairs={{0,4},{4,8},{8,12},{12,14},{14,10},{10,6},{6,2},{2,0},{1,5},{5,9},... | collective-permute-start | bytes 122888 | tf_op jit(solution)/shard_map/ppermute | solution.py:59
  19.5 4.5 %collective-permute-start.12 = (bf16[2,32,640]{2,1,0:T(8,128)(2,1)S(1)}, bf16[2,32,640]{2,1,0:T(8,128)(2,1)S(1)}, u32[]{:S(2)}, u32[]{:S(2)}) collective-permute-start(bf16[2,32,640]{2,1,0:T(8,128)(2,1)S(1)} %slice.83), channel_id=1, source_target_pairs={{4,0},{8,4},{12,8},{14,12},{10,14},{6,10},{2,6},{0,2},{5,1},{9,5},... | collective-permute-start | bytes 245768 | tf_op jit(solution)/shard_map/ppermute | solution.py:63
  20.7 9.1 %collective-permute-start.14 = (bf16[5,32,640]{2,1,0:T(8,128)(2,1)S(1)}, bf16[5,32,640]{2,1,0:T(8,128)(2,1)S(1)}, u32[]{:S(2)}, u32[]{:S(2)}) collective-permute-start(bf16[5,32,640]{2,1,0:T(8,128)(2,1)S(1)} %get-tuple-element.51), channel_id=1, source_target_pairs={{0,1},{1,0},{2,3},{3,2},{4,5},{5,4},{6,7},{7,6},{8,9},{9,8},{10,11... | collective-permute-start | bytes 614408 | tf_op jit(solution)/shard_map/ppermute | solution.py:47
  21.4 6.8 %collective-permute-start.4 = (bf16[160,512]{1,0:T(8,128)(2,1)S(1)}, bf16[160,512]{1,0:T(8,128)(2,1)S(1)}, u32[]{:S(2)}, u32[]{:S(2)}) collective-permute-start(bf16[160,512]{1,0:T(8,128)(2,1)S(1)} %collective-permute-done.2.refs_3_), channel_id=1, source_target_pairs={{0,4},{4,8},{8,12},{12,14},{14,10},{10,6},{6,2},{2,0},{1,5},{5,9},... | collective-permute-start | bytes 491528 | tf_op jit(solution)/shard_map/ppermute | solution.py:51
  24.0 4.1 %collective-permute-start.13 = (bf16[1,32,640]{2,1,0:T(8,128)(2,1)S(1)}, bf16[1,32,640]{2,1,0:T(8,128)(2,1)S(1)}, u32[]{:S(2)}, u32[]{:S(2)}) collective-permute-start(bf16[1,32,640]{2,1,0:T(8,128)(2,1)S(1)} %get-tuple-element.57), channel_id=1, source_target_pairs={{4,0},{8,4},{12,8},{14,12},{10,14},{6,10},{2,6},{0,2},{5,1},{9,5},... | collective-permute-start | bytes 122888 | tf_op jit(solution)/shard_map/ppermute | solution.py:63
  25.2 5.4 %collective-permute-start.5 = (bf16[160,512]{1,0:T(8,128)(2,1)S(1)}, bf16[160,512]{1,0:T(8,128)(2,1)S(1)}, u32[]{:S(2)}, u32[]{:S(2)}) collective-permute-start(bf16[160,512]{1,0:T(8,128)(2,1)S(1)} %collective-permute-done.3.refs_4_), channel_id=1, source_target_pairs={{4,0},{8,4},{12,8},{14,12},{10,14},{6,10},{2,6},{0,2},{5,1},{9,5},... | collective-permute-start | bytes 491528 | tf_op jit(solution)/shard_map/ppermute | solution.py:56
  28.1 1.7 %collective-permute-start.15 = (bf16[3,32,640]{2,1,0:T(8,128)(2,1)S(1)}, bf16[3,32,640]{2,1,0:T(8,128)(2,1)S(1)}, u32[]{:S(2)}, u32[]{:S(2)}) collective-permute-start(bf16[3,32,640]{2,1,0:T(8,128)(2,1)S(1)} %pad_maximum_fusion), channel_id=1, source_target_pairs={{0,1},{1,0},{2,3},{3,2},{4,5},{5,4},{6,7},{7,6},{8,9},{9,8},{10,11... | collective-permute-start | bytes 368648 | tf_op jit(solution)/shard_map/ppermute | solution.py:47
  28.2 6.6 %collective-permute-start.6 = (bf16[160,512]{1,0:T(8,128)(2,1)S(1)}, bf16[160,512]{1,0:T(8,128)(2,1)S(1)}, u32[]{:S(2)}, u32[]{:S(2)}) collective-permute-start(bf16[160,512]{1,0:T(8,128)(2,1)S(1)} %collective-permute-done.4.refs_5_), channel_id=1, source_target_pairs={{0,4},{4,8},{8,12},{12,14},{14,10},{10,6},{6,2},{2,0},{1,5},{5,9},... | collective-permute-start | bytes 491528 | tf_op jit(solution)/shard_map/ppermute | solution.py:51
  36.7 4.1 %collective-permute-start.16 = (f32[8,1280]{1,0:T(8,128)S(1)}, f32[8,1280]{1,0:T(8,128)S(1)}, u32[]{:S(2)}, u32[]{:S(2)}) collective-permute-start(f32[8,1280]{1,0:T(8,128)S(1)} %get-tuple-element.34), channel_id=1, source_target_pairs={{0,2},{2,0},{4,6},{6,4},{8,10},{10,8},{12,14},{14,12},{1,3},{3,1},... | collective-permute-start | bytes 122888 | tf_op jit(solution)/shard_map/ppermute | solution.py:76
  40.8 4.0 %collective-permute-start.17 = (f32[8,1280]{1,0:T(8,128)S(1)}, f32[8,1280]{1,0:T(8,128)S(1)}, u32[]{:S(2)}, u32[]{:S(2)}) collective-permute-start(f32[8,1280]{1,0:T(8,128)S(1)} %add.22), channel_id=1, source_target_pairs={{0,4},{2,6},{4,0},{6,2},{8,12},{10,14},{12,8},{14,10},{1,5},{3,7},... | collective-permute-start | bytes 122888 | tf_op jit(solution)/shard_map/ppermute | solution.py:76
  44.8 4.9 %collective-permute-start.18 = (f32[8,1280]{1,0:T(8,128)S(1)}, f32[8,1280]{1,0:T(8,128)S(1)}, u32[]{:S(2)}, u32[]{:S(2)}) collective-permute-start(f32[8,1280]{1,0:T(8,128)S(1)} %add.23), channel_id=1, source_target_pairs={{0,8},{2,10},{4,12},{6,14},{8,0},{10,2},{12,4},{14,6},{1,9},{3,11}... | collective-permute-start | bytes 122888 | tf_op jit(solution)/shard_map/ppermute | solution.py:76
  49.7 4.0 %collective-permute-start.19 = (f32[8,1280]{1,0:T(8,128)S(1)}, f32[8,1280]{1,0:T(8,128)S(1)}, u32[]{:S(2)}, u32[]{:S(2)}) collective-permute-start(f32[8,1280]{1,0:T(8,128)S(1)} %add.24.refs_11_), channel_id=1, source_target_pairs={{0,16},{16,0},{1,17},{17,1},{2,18},{18,2},{3,19},{19,3},{4,20},{20... | collective-permute-start | bytes 122888 | tf_op jit(solution)/shard_map/ppermute | solution.py:681
  56.9 1.6 %collective-permute-start.20 = (bf16[8,32,640]{2,1,0:T(8,128)(2,1)S(1)}, bf16[8,32,640]{2,1,0:T(8,128)(2,1)S(1)}, u32[]{:S(2)}, u32[]{:S(2)}) collective-permute-start(bf16[8,32,640]{2,1,0:T(8,128)(2,1)S(1)} %get-tuple-element.36), channel_id=1, source_target_pairs={{0,1},{1,0},{2,3},{3,2},{4,5},{5,4},{6,7},{7,6},{8,9},{9,8},{10,11... | collective-permute-start | bytes 983048 | tf_op jit(solution)/shard_map/ppermute | solution.py:709
  59.3 16.4 %all-to-all-start = ((bf16[8,32,640]{2,1,0:T(8,128)(2,1)}), bf16[8,32,640]{2,1,0:T(8,128)(2,1)S(1)}, u32[]{:S(2)}, u32[]{:S(2)}) async-start(bf16[8,32,640]{2,1,0:T(8,128)(2,1)} %meet.1), calls=%async_computation | async-start | bytes 655360 | tf_op jit(solution)/shard_map/all_to_all | solution.py:710
  65.1 10.6 %collective-permute-start.22 = (f32[192,512]{1,0:T(8,128)S(1)}, f32[192,512]{1,0:T(8,128)S(1)}, u32[]{:S(2)}, u32[]{:S(2)}) collective-permute-start(f32[192,512]{1,0:T(8,128)S(1)} %get-tuple-element.37.time_mine), channel_id=1, source_target_pairs={{0,1},{1,0},{2,3},{3,2},{4,5},{5,4},{6,7},{7,6},{8,9},{9,8},{10,11... | collective-permute-start | bytes 1179656 | tf_op jit(solution)/shard_map/ppermute | solution.py:722
  75.7 1.6 %collective-permute-start.21 = (bf16[8,32,640]{2,1,0:T(8,128)(2,1)S(1)}, bf16[8,32,640]{2,1,0:T(8,128)(2,1)S(1)}, u32[]{:S(2)}, u32[]{:S(2)}) collective-permute-start(bf16[8,32,640]{2,1,0:T(8,128)(2,1)S(1)} %all-to-all-done.mine), channel_id=1, source_target_pairs={{0,1},{1,0},{2,3},{3,2},{4,5},{5,4},{6,7},{7,6},{8,9},{9,8},{10,11... | collective-permute-start | bytes 983048 | tf_op jit(solution)/shard_map/ppermute | solution.py:722
  (3 other events, 34.6 us)

commit v6 on v5

--- a/solution.py
+++ b/solution.py
@@ -34,48 +34,62 @@
     return forward, [(target, source) for source, target in forward]
 
 
-def ring_exchange(shard, ahead, behind, own_piece):
+def ring_gather(shard):
     count = lax.axis_size("sp")
     up, down = ring_maps(count)
-    swap = [(0, 1), (1, 0)]
-    shards, shard_steps = [shard], [0]
-    mine, piece_steps, other = [own_piece], [0], []
+    shards, steps = [shard], [0]
     first = second = shard
-
-    def meet():
-        fresh = mine[len(other) :]
-        both = lax.ppermute(jnp.stack(fresh), "dp", swap)
-        other.extend(both[i] for i in range(len(fresh)))
-
     for step in range(1, count // 2 + 1):
         first = lax.ppermute(first, "sp", up)
         shards.append(first)
-        shard_steps.append(-step)
-        last = step == count - step
-        if not last:
+        steps.append(-step)
+        if step < count - step:
             second = lax.ppermute(second, "sp", down)
             shards.append(second)
-            shard_steps.append(step)
-            ahead = lax.ppermute(ahead, "sp", up)
-            mine.append(ahead[0])
-            piece_steps.append(-step)
-            ahead = ahead[1:]
-        behind = lax.ppermute(behind, "sp", down)
-        mine.append(behind[0])
-        piece_steps.append(step)
-        behind = behind[1:]
-        if last or step % 2 == 0:
-            meet()
-    return shards, shard_steps, mine, other, piece_steps
-
-
-def swap_sum(values, axis):
-    count = lax.axis_size(axis)
-    bit = 1
-    while bit < count:
-        values = values + lax.ppermute(values, axis, [(i, i ^ bit) for i in range(count)])
-        bit *= 2
+            steps.append(step)
+    return shards, steps
+
+
+def exchange_pieces(pairs, shards):
+    arrived = [pairs[0]] + [swap(pair, 2 * k) for k, pair in enumerate(pairs) if k]
+    arrived = lax.optimization_barrier((arrived, shards[3]))[0]
+    even = jnp.stack([pair[0] for pair in arrived])
+    odd = swap(jnp.stack([pair[1] for pair in arrived]), 1)
+    return even, odd, swap_core(even), swap_core(odd)
+
+
+def swap(values, distance):
+    count = lax.axis_size("sp")
+    return lax.ppermute(values, "sp", [(i, i ^ distance) for i in range(count)])
+
+
+def swap_core(values):
+    return lax.ppermute(values, "dp", [(0, 1), (1, 0)])
+
+
+def sum_pairs(values, bits):
+    bits = list(bits)
+    while bits:
+        if len(bits) == 1:
+            values = values + swap(values, bits.pop())
+        else:
+            one, two = bits.pop(0), bits.pop(0)
+            values = values + (swap(values, one) + swap(values, two) + swap(values, one | two))
     return values
+
+
+def sum_and_cross(values):
+    count, sections = lax.axis_size("sp"), lax.axis_size("sec")
+    bits = [1 << b for b in range(count.bit_length() - 1)]
+    values = sum_pairs(values, bits[1:])
+    beside = swap(values, 1)
+    across = lax.ppermute(values, "sec", [(0, 1), (1, 0)])
+    corner = lax.ppermute(
+        values,
+        ("sec", "sp"),
+        [(s * count + i, (1 - s) * count + (i ^ 1)) for s in range(sections) for i in range(count)],
+    )
+    return values + beside, across + corner
 
 
 def dot(left, right, dims):
@@ -161,16 +175,17 @@
         v[rows_at(ring_device(place + step, z.sp), z)] = shard[...]
 
 
-def place_pieces(z, steps, mine, other, w_cat, codes):
-    place = ring_place(lax.axis_index("sp"), z.sp)
-    core = lax.axis_index("dp")
-    for one, two, step in zip(mine, other, steps):
-        device = ring_device(place + step, z.sp)
+def place_pieces(z, even, odd, even_other, odd_other, w_cat, codes):
+    me, core = lax.axis_index("sp"), lax.axis_index("dp")
+    for distance in range(z.sp):
+        mine, other = ((even, even_other), (odd, odd_other))[distance % 2]
+        device = lax.bitwise_xor(me, distance)
         start = pl.multiple_of(device * z.own, z.own)
-        codes[device] = one[z.code_row : z.code_row + z.code_rows]
-        low = jnp.where(core == 0, one[: z.half], two[: z.half])
-        high = jnp.where(core == 0, two[: z.half], one[: z.half])
-        if z.half == z.half_pad:
+        at = distance // 2
+        codes[device] = mine[at, z.code_row : z.code_row + z.code_rows]
+        one, two = mine[at, : z.half], other[at, : z.half]
+        low, high = jnp.where(core == 0, one, two), jnp.where(core == 0, two, one)
+        if z.split:
             w_cat[pl.ds(start, z.half)] = low
             w_cat[pl.ds(start + z.half, z.half)] = high
         else:
@@ -285,54 +300,34 @@
     return sum(raw[8 * t : 8 * t + 8] for t in range(z.frames))
 
 
-def piece_kernel(z, w, codes, ahead, behind, own_piece):
-    place = ring_place(lax.axis_index("sp"), z.sp)
+def piece_kernel(z, w, codes, *pairs):
+    me = lax.axis_index("sp")
     core = lax.axis_index("dp")
     lane = lax.broadcasted_iota(jnp.int32, (z.half, LANES), 1)
     code_block = codes[...]
-    for j in range(z.sp):
-        block, offset = (j * z.own) // LANES, (j * z.own) % LANES
+    for distance in range(z.sp):
+        begin = lax.bitwise_xor(me, distance) * z.own
+        block, offset = begin // LANES, begin % LANES
+        at = pl.ds(pl.multiple_of(block * LANES, LANES), LANES)
         taps = []
         for tap in range(9):
-            at = slice(block * LANES, (block + 1) * LANES)
-            if z.half == z.half_pad:
+            if z.split:
                 value = w[tap, pl.ds(pl.multiple_of(core * z.half, z.half), z.half), at]
                 value = value.astype(F32)
             else:
                 value = w[tap, :, at].astype(F32)
                 value = jnp.where(core == 0, value[: z.half], value[z.half :])
-            value = lanes_down(value, offset)
+            value = pltpu.roll(value, (LANES - offset) % LANES, 1)
             taps.append(jnp.where(lane < z.own, value, 0.0))
         blocks = merge(taps, z.own)
         if z.code_row == 0:
             blocks[-1] = blocks[-1] + code_block
-        distance = lax.rem(ring_place(jnp.int32(j), z.sp) - place + z.sp, z.sp)
-
-        def store(target, index):
-            for b, value in enumerate(blocks):
-                at = slice(b * LANES, (b + 1) * LANES)
-                if index is None:
-                    target[: z.half, at] = value.astype(BF16)
-                else:
-                    target[index, : z.half, at] = value.astype(BF16)
-            if z.code_row:
-                tail = slice(z.code_row, z.piece_rows)
-                if index is None:
-                    target[tail, :LANES] = code_block.astype(BF16)
-                else:
-                    target[index, tail, :LANES] = code_block.astype(BF16)
-
-        @pl.when(distance == 0)
-        def _():
-            store(own_piece, None)
-
-        @pl.when(jnp.logical_and(distance > 0, distance < z.sp // 2))
-        def _():
-            store(ahead, distance - 1)
-
-        @pl.when(distance >= z.sp // 2)
-        def _():
-            store(behind, z.sp - distance - 1)
+        target = pairs[distance // 2]
+        for b, value in enumerate(blocks):
+            lanes = slice(b * LANES, (b + 1) * LANES)
+            target[distance % 2, : z.half, lanes] = value.astype(BF16)
+        if z.code_row:
+            target[distance % 2, z.code_row : z.piece_rows, :LANES] = code_block.astype(BF16)
 
 
 def store_hidden(z, pre, logistic, hid_cat, r):
@@ -352,14 +347,12 @@
     each_row(z, body)
 
 
-def early_kernel(z, piece_steps, *refs):
-    n = z.sp
-    mine, other = refs[:n], refs[n : 2 * n]
-    wt, proj, halves = refs[2 * n : 2 * n + 3]
-    w_cat, pos, hid_cat, slope, table_out = refs[2 * n + 3 : 2 * n + 8]
-    codes, taps = refs[2 * n + 8 :]
+def early_kernel(z, *refs):
+    wt, proj, halves = refs[4:7]
+    w_cat, pos, hid_cat, slope, table_out = refs[7:12]
+    codes, taps = refs[12:]
     decoder = lax.axis_index("sec") == 1
-    place_pieces(z, piece_steps, mine, other, w_cat, codes)
+    place_pieces(z, *refs[:4], w_cat, codes)
 
     @pl.when(decoder)
     def _():
@@ -617,21 +610,16 @@
     left = z.code_lane % LANES
     code_rows = z.half if z.code_row == 0 else z.code_rows
     codes = jnp.pad(codes, ((0, code_rows - cols), (left, LANES - left - 8 * frames)))
-    ahead, behind, own_piece = pl.pallas_call(
+    pairs = pl.pallas_call(
         functools.partial(piece_kernel, z),
-        out_shape=(
-            shaped((z.sp // 2 - 1, z.piece_rows, z.wide), BF16),
-            shaped((z.sp // 2, z.piece_rows, z.wide), BF16),
-            shaped((z.piece_rows, z.wide), BF16),
-        ),
+        out_shape=[shaped((2, z.piece_rows, z.wide), BF16)] * (z.sp // 2),
         in_specs=[VM] * 2,
-        out_specs=(VM,) * 3,
+        out_specs=[VM] * (z.sp // 2),
         compiler_params=params,
         name="pieces",
     )(w_space[0], codes)
-    shards, steps, mine, other, piece_steps = ring_exchange(
-        block_data.reshape(z.row, chans), ahead, behind, own_piece
-    )
+    shards, steps = ring_gather(block_data.reshape(z.row, chans))
+    pieces = exchange_pieces(pairs, shards)
     proj = jnp.pad(jnp.where(decoder, dec_proj, enc_proj), ((0, 16 - lat), (0, 0)))
     wt = jnp.concatenate([w_time.reshape(3 * own, chans), proj[:8]], axis=0)
     wt = jnp.pad(wt, ((0, z.thin - 3 * own - 8), (0, 0)))
@@ -639,7 +627,7 @@
     halves = jnp.broadcast_to(half[:, None], (16, LANES))
 
     w_cat, pos, hid_dec, rate, table = pl.pallas_call(
-        functools.partial(early_kernel, z, piece_steps),
+        functools.partial(early_kernel, z),
         out_shape=(
             shaped((chans, z.wide), BF16),
             shaped((z.count, LANES), BF16),
@@ -647,7 +635,7 @@
             shaped((z.sp, z.row, LANES), F32),
             shaped((LANES, LANES), F32),
         ),
-        in_specs=[VM] * (2 * z.sp + 3),
+        in_specs=[VM] * 7,
         out_specs=(VM,) * 5,
         scratch_shapes=[
             pltpu.VMEM((z.sp, z.code_rows, z.wide), BF16),
@@ -655,7 +643,7 @@
         ],
         compiler_params=params,
         name="early",
-    )(*mine, *other, wt, proj, halves)
+    )(*pieces, wt, proj, halves)
     part, hid_cat, slope, inner, v = pl.pallas_call(
         functools.partial(first_kernel, z, steps),
         out_shape=(
@@ -676,9 +664,7 @@
         compiler_params=params,
         name="first",
     )(*shards, w_cat, wt, proj, table, rate)
-    swap = [(0, 1), (1, 0)]
-    total = swap_sum(part, "sp")
-    received = lax.ppermute(total, "sec", swap)
+    total, received = sum_and_cross(part)
     part_rows = (z.sp, z.half if z.split else own, z.wide)
     big, send, time, part = pl.pallas_call(
         functools.partial(second_kernel, z, scale),
@@ -706,7 +692,7 @@
             out_specs=VM,
             compiler_params=params,
             name="meet",
-        )(big, lax.ppermute(send, "dp", swap))
+        )(big, swap_core(send))
     big = lax.all_to_all(big.astype(BF16), "sp", 0, 0, tiled=True)
     space, time, carried = pl.pallas_call(
         functools.partial(last_kernel, z),
@@ -719,12 +705,12 @@
         out_specs=(VM,) * 3,
         compiler_params=params,
         name="last",
-    )(big, lax.ppermute(big, "dp", swap), time, lax.ppermute(time, "dp", swap))
+    )(big, swap_core(big), time, swap_core(time))
     if z.carries:
         part = carried.reshape(lat, chans)
     else:
-        part = swap_sum(part, "sp")
-        part = (part + lax.ppermute(part, "dp", swap))[:lat]
+        part = sum_pairs(part, [1 << b for b in range(z.sp.bit_length() - 1)])
+        part = (part + swap_core(part))[:lat]
     return space[None], time.reshape(1, 3, own, chans), part[None]
 
 

time: 79.1 us -> 71.7 us (0.906)
  waiting for transfers between devices: 36.4 us -> 29.6 us
    ppermute x23 -> x22, waiting for transfers between devices: 25.8 us -> 19 us  [the longest x8 8.45 us: swap(): return lax.ppermute(values, 'sp', [(i, i ^ distance) for i in range(count)])]
    ppermute x23 -> x22, starting transfers between devices: 23.6 us -> 26.5 us  [the longest x8 12 us: swap(): return lax.ppermute(values, 'sp', [(i, i ^ distance) for i in range(count)])]
    all_to_all x1, starting transfers between devices: 5.79 us -> 3.43 us  [local(): big = lax.all_to_all(big.astype(BF16), 'sp', 0, 0, tiled=True)]
  transfers between devices with their start and end apart: 24 -> 23, of which waited for: 16 -> 14; matrix products, arithmetic and copies ran while one was open for 3% -> 3% of each run, Pallas kernels for 2% -> 1%
where the time goes in v6:
time: 71.7 us; the launch traced here: 71.3 us
  starting transfers between devices  29.9 us (42%)
  waiting for transfers between devices  29.6 us (41%)
  Pallas kernels  8.17 us (11%)
  other arithmetic  1.54 us (2%)
  local copies, waits for them, and re-layouts  1.35 us (2%)
  between operations  0.78 us (1%)
    ppermute x8, starting transfers between devices, swap(): return lax.ppermute(values, 'sp', [(i, i ^ distance) for i in range(count)])  12 us
    all_to_all x1, waiting for transfers between devices, local(): big = lax.all_to_all(big.astype(BF16), 'sp', 0, 0, tiled=True)  10.6 us
    ppermute x8, waiting for transfers between devices, swap(): return lax.ppermute(values, 'sp', [(i, i ^ distance) for i in range(count)])  8.45 us
    ppermute x4, starting transfers between devices, ring_gather(): first = lax.ppermute(first, 'sp', up)  7.42 us
    ppermute x5, waiting for transfers between devices, swap_core(): return lax.ppermute(values, 'dp', [(0, 1), (1, 0)])  4.57 us
    ppermute x3, starting transfers between devices, ring_gather(): second = lax.ppermute(second, 'sp', down)  4.21 us
    ppermute x4, waiting for transfers between devices, ring_gather(): first = lax.ppermute(first, 'sp', up)  3.76 us
    all_to_all x1, starting transfers between devices, local(): big = lax.all_to_all(big.astype(BF16), 'sp', 0, 0, tiled=True)  3.43 us
  transfers between devices with their start and end apart: 23, of which 14 were waited for; matrix products, arithmetic and copies ran while one was open for 3% of the time, Pallas kernels for 1%

profile of v6, /device:TPU:0, one launch (start us, length us, event | category | flops | bytes accessed | tf_op | source)
XLA Modules:
  0.0 71.3 jit_solution(7951360908574322264)
XLA Ops:
  0.6 3.0 %collective-permute-start.1 = (bf16[160,512]{1,0:T(8,128)(2,1)}, bf16[160,512]{1,0:T(8,128)(2,1)S(1)}, u32[]{:S(2)}, u32[]{:S(2)}) collective-permute-start(bf16[160,512]{1,0:T(8,128)(2,1)} %bitcast.13), channel_id=1, source_target_pairs={{4,0},{8,4},{12,8},{14,12},{10,14},{6,10},{2,6},{0,2},{5,1},{9,5},... | collective-permute-start | bytes 491528 | tf_op jit(solution)/shard_map/ppermute | solution.py:47
  6.3 2.0 %collective-permute-start.7 = (bf16[2,32,640]{2,1,0:T(8,128)(2,1)S(1)}, bf16[2,32,640]{2,1,0:T(8,128)(2,1)S(1)}, u32[]{:S(2)}, u32[]{:S(2)}) collective-permute-start(bf16[2,32,640]{2,1,0:T(8,128)(2,1)S(1)} %get-tuple-element.28), channel_id=1, source_target_pairs={{0,4},{2,6},{4,0},{6,2},{8,12},{10,14},{12,8},{14,10},{1,5},{3,7},... | collective-permute-start | bytes 245768 | tf_op jit(solution)/shard_map/ppermute | solution.py:63
  8.3 2.6 %collective-permute-start.8 = (bf16[2,32,640]{2,1,0:T(8,128)(2,1)S(1)}, bf16[2,32,640]{2,1,0:T(8,128)(2,1)S(1)}, u32[]{:S(2)}, u32[]{:S(2)}) collective-permute-start(bf16[2,32,640]{2,1,0:T(8,128)(2,1)S(1)} %get-tuple-element.29), channel_id=1, source_target_pairs={{0,8},{2,10},{4,12},{6,14},{8,0},{10,2},{12,4},{14,6},{1,9},{3,11}... | collective-permute-start | bytes 245768 | tf_op jit(solution)/shard_map/ppermute | solution.py:63
  13.7 2.8 %collective-permute-done.8 = bf16[2,32,640]{2,1,0:T(8,128)(2,1)S(1)} collective-permute-done((bf16[2,32,640]{2,1,0:T(8,128)(2,1)S(1)}, bf16[2,32,640]{2,1,0:T(8,128)(2,1)S(1)}, u32[]{:S(2)}, u32[]{:S(2)}) %collective-permute-start.8) | collective-permute-done | bytes 81952 | tf_op jit(solution)/shard_map/ppermute | solution.py:63
  16.4 1.6 %collective-permute-done.9 = bf16[2,32,640]{2,1,0:T(8,128)(2,1)S(1)} collective-permute-done((bf16[2,32,640]{2,1,0:T(8,128)(2,1)S(1)}, bf16[2,32,640]{2,1,0:T(8,128)(2,1)S(1)}, u32[]{:S(2)}, u32[]{:S(2)}) %collective-permute-start.9) | collective-permute-done | bytes 81952 | tf_op jit(solution)/shard_map/ppermute | solution.py:63
  18.1 2.0 %collective-permute-start.10 = (bf16[4,32,640]{2,1,0:T(8,128)(2,1)S(1)}, bf16[4,32,640]{2,1,0:T(8,128)(2,1)S(1)}, u32[]{:S(2)}, u32[]{:S(2)}) collective-permute-start(bf16[4,32,640]{2,1,0:T(8,128)(2,1)S(1)} %pad_maximum_fusion.1), channel_id=1, source_target_pairs={{0,2},{2,0},{4,6},{6,4},{8,10},{10,8},{12,14},{14,12},{1,3},{3,1},... | collective-permute-start | bytes 491528 | tf_op jit(solution)/shard_map/ppermute | solution.py:63
  20.1 3.9 %collective-permute-start.4 = (bf16[160,512]{1,0:T(8,128)(2,1)S(1)}, bf16[160,512]{1,0:T(8,128)(2,1)S(1)}, u32[]{:S(2)}, u32[]{:S(2)}) collective-permute-start(bf16[160,512]{1,0:T(8,128)(2,1)S(1)} %collective-permute-done.2.refs_3_), channel_id=1, source_target_pairs={{0,4},{4,8},{8,12},{12,14},{14,10},{10,6},{6,2},{2,0},{1,5},{5,9},... | collective-permute-start | bytes 491528 | tf_op jit(solution)/shard_map/ppermute | solution.py:43
  24.2 2.6 %collective-permute-done.4.refs_5_ = bf16[160,512]{1,0:T(8,128)(2,1)S(1)} collective-permute-done((bf16[160,512]{1,0:T(8,128)(2,1)S(1)}, bf16[160,512]{1,0:T(8,128)(2,1)S(1)}, u32[]{:S(2)}, u32[]{:S(2)}) %collective-permute-start.4) | collective-permute-done | bytes 163872 | tf_op jit(solution)/shard_map/ppermute | solution.py:43
  26.8 2.5 %collective-permute-start.6 = (bf16[160,512]{1,0:T(8,128)(2,1)S(1)}, bf16[160,512]{1,0:T(8,128)(2,1)S(1)}, u32[]{:S(2)}, u32[]{:S(2)}) collective-permute-start(bf16[160,512]{1,0:T(8,128)(2,1)S(1)} %collective-permute-done.4.refs_5_), channel_id=1, source_target_pairs={{0,4},{4,8},{8,12},{12,14},{14,10},{10,6},{6,2},{2,0},{1,5},{5,9},... | collective-permute-start | bytes 491528 | tf_op jit(solution)/shard_map/ppermute | solution.py:43
  29.4 1.3 %collective-permute-done.12.refs_3_ = bf16[4,32,640]{2,1,0:T(8,128)(2,1)S(1)} collective-permute-done((bf16[4,32,640]{2,1,0:T(8,128)(2,1)S(1)}, bf16[4,32,640]{2,1,0:T(8,128)(2,1)S(1)}, u32[]{:S(2)}, u32[]{:S(2)}) %collective-permute-start.12) | collective-permute-done | bytes 163872 | tf_op jit(solution)/shard_map/ppermute | solution.py:67
  32.2 1.9 %first.1 = (f32[8,1280]{1,0:T(8,128)S(1)}, bf16[1280,256]{1,0:T(8,128)(2,1)S(1)}, f32[8,160,128]{2,1,0:T(8,128)S(1)}, bf16[8,160,128]{2,1,0:T(8,128)(2,1)S(1)}, bf16[1280,512]{1,0:T(8,128)(2,1)S(1)}) custom-call(bf16[160,512]{1,0:T(8,128)(2,1)S(1)} %bitcast.15, bf16[160,512]{1,0:T(8,128)(2,1)S(1)} %collective-permute-done.refs_1_, ...), custom_call_target="tpu_custom_call" | custom-call | tf_op jit(solution)/shard_map/first/pallas_call | solution.py:647
  34.1 1.4 %collective-permute-start.15 = (f32[8,1280]{1,0:T(8,128)S(1)}, f32[8,1280]{1,0:T(8,128)S(1)}, u32[]{:S(2)}, u32[]{:S(2)}) collective-permute-start(f32[8,1280]{1,0:T(8,128)S(1)} %get-tuple-element.44), channel_id=1, source_target_pairs={{0,12},{2,14},{4,8},{6,10},{8,4},{10,6},{12,0},{14,2},{1,13},{3,15... | collective-permute-start | bytes 122888 | tf_op jit(solution)/shard_map/ppermute | solution.py:63
  35.5 2.6 %collective-permute-start.14 = (f32[8,1280]{1,0:T(8,128)S(1)}, f32[8,1280]{1,0:T(8,128)S(1)}, u32[]{:S(2)}, u32[]{:S(2)}) collective-permute-start(f32[8,1280]{1,0:T(8,128)S(1)} %get-tuple-element.44), channel_id=1, source_target_pairs={{0,8},{2,10},{4,12},{6,14},{8,0},{10,2},{12,4},{14,6},{1,9},{3,11}... | collective-permute-start | bytes 122888 | tf_op jit(solution)/shard_map/ppermute | solution.py:63
  38.5 1.4 %collective-permute-done.15 = f32[8,1280]{1,0:T(8,128)S(1)} collective-permute-done((f32[8,1280]{1,0:T(8,128)S(1)}, f32[8,1280]{1,0:T(8,128)S(1)}, u32[]{:S(2)}, u32[]{:S(2)}) %collective-permute-start.15) | collective-permute-done | bytes 40992 | tf_op jit(solution)/shard_map/ppermute | solution.py:63
  40.0 1.3 %collective-permute-done.14 = f32[8,1280]{1,0:T(8,128)S(1)} collective-permute-done((f32[8,1280]{1,0:T(8,128)S(1)}, f32[8,1280]{1,0:T(8,128)S(1)}, u32[]{:S(2)}, u32[]{:S(2)}) %collective-permute-start.14) | collective-permute-done | bytes 40992 | tf_op jit(solution)/shard_map/ppermute | solution.py:63
  43.1 1.3 %collective-permute-start.18 = (f32[8,1280]{1,0:T(8,128)S(1)}, f32[8,1280]{1,0:T(8,128)S(1)}, u32[]{:S(2)}, u32[]{:S(2)}) collective-permute-start(f32[8,1280]{1,0:T(8,128)S(1)} %add_add_fusion), channel_id=1, source_target_pairs={{0,18},{2,16},{4,22},{6,20},{8,26},{10,24},{12,30},{14,28},{16,2},... | collective-permute-start | bytes 122888 | tf_op jit(solution)/shard_map/ppermute | solution.py:87
  44.4 1.3 %collective-permute-start.17 = (f32[8,1280]{1,0:T(8,128)S(1)}, f32[8,1280]{1,0:T(8,128)S(1)}, u32[]{:S(2)}, u32[]{:S(2)}) collective-permute-start(f32[8,1280]{1,0:T(8,128)S(1)} %add_add_fusion), channel_id=1, source_target_pairs={{0,16},{16,0},{1,17},{17,1},{2,18},{18,2},{3,19},{19,3},{4,20},{20... | collective-permute-start | bytes 122888 | tf_op jit(solution)/shard_map/ppermute | solution.py:86
  46.2 1.8 %collective-permute-done.18 = f32[8,1280]{1,0:T(8,128)S(1)} collective-permute-done((f32[8,1280]{1,0:T(8,128)S(1)}, f32[8,1280]{1,0:T(8,128)S(1)}, u32[]{:S(2)}, u32[]{:S(2)}) %collective-permute-start.18) | collective-permute-done | bytes 40992 | tf_op jit(solution)/shard_map/ppermute | solution.py:87
  48.4 3.2 %second.1 = (f32[8,32,640]{2,1,0:T(8,128)S(1)}, bf16[8,32,640]{2,1,0:T(8,128)(2,1)S(1)}, f32[192,512]{1,0:T(8,128)S(1)}, f32[8,512]{1,0:T(8,128)}) custom-call(bf16[1280,512]{1,0:T(8,128)(2,1)S(1)} %get-tuple-element.38.refs_0_, bf16[512,640]{1,0:T(8,128)(2,1)S(1)} %get-tuple-element.35.refs_8_.refs_1_, bf16[1280,128]{1,0:T(8,128)(2,1)S(1)} %get-tuple-element.39.refs_2_, ...), custom_call_target="tpu_custom_call" | custom-call | tf_op jit(solution)/shard_map/second/pallas_call | solution.py:669
  51.7 1.6 %collective-permute-done.19.other = bf16[8,32,640]{2,1,0:T(8,128)(2,1)S(1)} collective-permute-done((bf16[8,32,640]{2,1,0:T(8,128)(2,1)S(1)}, bf16[8,32,640]{2,1,0:T(8,128)(2,1)S(1)}, u32[]{:S(2)}, u32[]{:S(2)}) %collective-permute-start.19) | collective-permute-done | bytes 327712 | tf_op jit(solution)/shard_map/ppermute | solution.py:67
  54.1 3.4 %all-to-all-start = ((bf16[8,32,640]{2,1,0:T(8,128)(2,1)}), bf16[8,32,640]{2,1,0:T(8,128)(2,1)S(1)}, u32[]{:S(2)}, u32[]{:S(2)}) async-start(bf16[8,32,640]{2,1,0:T(8,128)(2,1)} %meet.1), calls=%async_computation | async-start | bytes 655360 | tf_op jit(solution)/shard_map/all_to_all | solution.py:696
  57.7 10.6 %all-to-all-done.mine = bf16[8,32,640]{2,1,0:T(8,128)(2,1)S(1)} async-done(((bf16[8,32,640]{2,1,0:T(8,128)(2,1)}), bf16[8,32,640]{2,1,0:T(8,128)(2,1)S(1)}, u32[]{:S(2)}, u32[]{:S(2)}) %all-to-all-start) | async-done | bytes 327712 | tf_op jit(solution)/shard_map/all_to_all | solution.py:696
  68.3 1.6 %collective-permute-done.20.other = bf16[8,32,640]{2,1,0:T(8,128)(2,1)S(1)} collective-permute-done((bf16[8,32,640]{2,1,0:T(8,128)(2,1)S(1)}, bf16[8,32,640]{2,1,0:T(8,128)(2,1)S(1)}, u32[]{:S(2)}, u32[]{:S(2)}) %collective-permute-start.20) | collective-permute-done | bytes 327712 | tf_op jit(solution)/shard_map/ppermute | solution.py:67
  69.9 1.4 %last.1 = (f32[9,64,512]{2,1,0:T(8,128)}, f32[192,512]{1,0:T(8,128)}, f32[6,1,512]{2,1,0:T(1,128)}) custom-call(bf16[8,32,640]{2,1,0:T(8,128)(2,1)S(1)} %all-to-all-done.mine, bf16[8,32,640]{2,1,0:T(8,128)(2,1)S(1)} %collective-permute-done.20.other, f32[192,512]{1,0:T(8,128)S(1)} %get-tuple-element.47.time_mine, ...), custom_call_target="tpu_custom_call" | custom-call | tf_op jit(solution)/shard_map/last/pallas_call | solution.py:697
  (54 shorter events, 11.4 us)
Async XLA Ops:
  0.6 11.9 %collective-permute-start.1 = (bf16[160,512]{1,0:T(8,128)(2,1)}, bf16[160,512]{1,0:T(8,128)(2,1)S(1)}, u32[]{:S(2)}, u32[]{:S(2)}) collective-permute-start(bf16[160,512]{1,0:T(8,128)(2,1)} %bitcast.13), channel_id=1, source_target_pairs={{4,0},{8,4},{12,8},{14,12},{10,14},{6,10},{2,6},{0,2},{5,1},{9,5},... | collective-permute-start | bytes 491528 | tf_op jit(solution)/shard_map/ppermute | solution.py:47
  3.7 7.3 %collective-permute-start = (bf16[160,512]{1,0:T(8,128)(2,1)}, bf16[160,512]{1,0:T(8,128)(2,1)S(1)}, u32[]{:S(2)}, u32[]{:S(2)}) collective-permute-start(bf16[160,512]{1,0:T(8,128)(2,1)} %bitcast.14), channel_id=1, source_target_pairs={{0,4},{4,8},{8,12},{12,14},{14,10},{10,6},{6,2},{2,0},{1,5},{5,9},... | collective-permute-start | bytes 491528 | tf_op jit(solution)/shard_map/ppermute | solution.py:43
  5.7 23.6 %copy-start.2 = (bf16[1,3,64,512]{3,2,1,0:T(8,128)(2,1)S(1)}, bf16[1,3,64,512]{3,2,1,0:T(8,128)(2,1)}, u32[]{:S(2)}) copy-start(bf16[1,3,64,512]{3,2,1,0:T(8,128)(2,1)} %param.11) | copy-start | bytes 589828
  6.3 7.3 %collective-permute-start.7 = (bf16[2,32,640]{2,1,0:T(8,128)(2,1)S(1)}, bf16[2,32,640]{2,1,0:T(8,128)(2,1)S(1)}, u32[]{:S(2)}, u32[]{:S(2)}) collective-permute-start(bf16[2,32,640]{2,1,0:T(8,128)(2,1)S(1)} %get-tuple-element.28), channel_id=1, source_target_pairs={{0,4},{2,6},{4,0},{6,2},{8,12},{10,14},{12,8},{14,10},{1,5},{3,7},... | collective-permute-start | bytes 245768 | tf_op jit(solution)/shard_map/ppermute | solution.py:63
  8.3 8.1 %collective-permute-start.8 = (bf16[2,32,640]{2,1,0:T(8,128)(2,1)S(1)}, bf16[2,32,640]{2,1,0:T(8,128)(2,1)S(1)}, u32[]{:S(2)}, u32[]{:S(2)}) collective-permute-start(bf16[2,32,640]{2,1,0:T(8,128)(2,1)S(1)} %get-tuple-element.29), channel_id=1, source_target_pairs={{0,8},{2,10},{4,12},{6,14},{8,0},{10,2},{12,4},{14,6},{1,9},{3,11}... | collective-permute-start | bytes 245768 | tf_op jit(solution)/shard_map/ppermute | solution.py:63
  10.9 7.1 %collective-permute-start.9 = (bf16[2,32,640]{2,1,0:T(8,128)(2,1)S(1)}, bf16[2,32,640]{2,1,0:T(8,128)(2,1)S(1)}, u32[]{:S(2)}, u32[]{:S(2)}) collective-permute-start(bf16[2,32,640]{2,1,0:T(8,128)(2,1)S(1)} %get-tuple-element.30), channel_id=1, source_target_pairs={{0,12},{2,14},{4,8},{6,10},{8,4},{10,6},{12,0},{14,2},{1,13},{3,15... | collective-permute-start | bytes 245768 | tf_op jit(solution)/shard_map/ppermute | solution.py:63
  10.9 7.1 %collective-permute-start.2 = (bf16[160,512]{1,0:T(8,128)(2,1)S(1)}, bf16[160,512]{1,0:T(8,128)(2,1)S(1)}, u32[]{:S(2)}, u32[]{:S(2)}) collective-permute-start(bf16[160,512]{1,0:T(8,128)(2,1)S(1)} %collective-permute-done.refs_1_), channel_id=1, source_target_pairs={{0,4},{4,8},{8,12},{12,14},{14,10},{10,6},{6,2},{2,0},{1,5},{5,9},... | collective-permute-start | bytes 491528 | tf_op jit(solution)/shard_map/ppermute | solution.py:43
  12.5 11.6 %collective-permute-start.3 = (bf16[160,512]{1,0:T(8,128)(2,1)S(1)}, bf16[160,512]{1,0:T(8,128)(2,1)S(1)}, u32[]{:S(2)}, u32[]{:S(2)}) collective-permute-start(bf16[160,512]{1,0:T(8,128)(2,1)S(1)} %collective-permute-done.1.refs_2_), channel_id=1, source_target_pairs={{4,0},{8,4},{12,8},{14,12},{10,14},{6,10},{2,6},{0,2},{5,1},{9,5},... | collective-permute-start | bytes 491528 | tf_op jit(solution)/shard_map/ppermute | solution.py:47
  18.1 11.2 %collective-permute-start.10 = (bf16[4,32,640]{2,1,0:T(8,128)(2,1)S(1)}, bf16[4,32,640]{2,1,0:T(8,128)(2,1)S(1)}, u32[]{:S(2)}, u32[]{:S(2)}) collective-permute-start(bf16[4,32,640]{2,1,0:T(8,128)(2,1)S(1)} %pad_maximum_fusion.1), channel_id=1, source_target_pairs={{0,2},{2,0},{4,6},{6,4},{8,10},{10,8},{12,14},{14,12},{1,3},{3,1},... | collective-permute-start | bytes 491528 | tf_op jit(solution)/shard_map/ppermute | solution.py:63
  20.1 6.8 %collective-permute-start.4 = (bf16[160,512]{1,0:T(8,128)(2,1)S(1)}, bf16[160,512]{1,0:T(8,128)(2,1)S(1)}, u32[]{:S(2)}, u32[]{:S(2)}) collective-permute-start(bf16[160,512]{1,0:T(8,128)(2,1)S(1)} %collective-permute-done.2.refs_3_), channel_id=1, source_target_pairs={{0,4},{4,8},{8,12},{12,14},{14,10},{10,6},{6,2},{2,0},{1,5},{5,9},... | collective-permute-start | bytes 491528 | tf_op jit(solution)/shard_map/ppermute | solution.py:43
  24.0 5.4 %collective-permute-start.11 = (bf16[4,32,640]{2,1,0:T(8,128)(2,1)S(1)}, bf16[4,32,640]{2,1,0:T(8,128)(2,1)S(1)}, u32[]{:S(2)}, u32[]{:S(2)}) collective-permute-start(bf16[4,32,640]{2,1,0:T(8,128)(2,1)S(1)} %pad_maximum_fusion.refs_0_), channel_id=1, source_target_pairs={{0,1},{1,0},{2,3},{3,2},{4,5},{5,4},{6,7},{7,6},{8,9},{9,8},{10,11... | collective-permute-start | bytes 491528 | tf_op jit(solution)/shard_map/ppermute | solution.py:67
  24.1 6.9 %collective-permute-start.5 = (bf16[160,512]{1,0:T(8,128)(2,1)S(1)}, bf16[160,512]{1,0:T(8,128)(2,1)S(1)}, u32[]{:S(2)}, u32[]{:S(2)}) collective-permute-start(bf16[160,512]{1,0:T(8,128)(2,1)S(1)} %collective-permute-done.3.refs_4_), channel_id=1, source_target_pairs={{4,0},{8,4},{12,8},{14,12},{10,14},{6,10},{2,6},{0,2},{5,1},{9,5},... | collective-permute-start | bytes 491528 | tf_op jit(solution)/shard_map/ppermute | solution.py:47
  26.8 5.3 %collective-permute-start.6 = (bf16[160,512]{1,0:T(8,128)(2,1)S(1)}, bf16[160,512]{1,0:T(8,128)(2,1)S(1)}, u32[]{:S(2)}, u32[]{:S(2)}) collective-permute-start(bf16[160,512]{1,0:T(8,128)(2,1)S(1)} %collective-permute-done.4.refs_5_), channel_id=1, source_target_pairs={{0,4},{4,8},{8,12},{12,14},{14,10},{10,6},{6,2},{2,0},{1,5},{5,9},... | collective-permute-start | bytes 491528 | tf_op jit(solution)/shard_map/ppermute | solution.py:43
  29.3 1.4 %collective-permute-start.12 = (bf16[4,32,640]{2,1,0:T(8,128)(2,1)S(1)}, bf16[4,32,640]{2,1,0:T(8,128)(2,1)S(1)}, u32[]{:S(2)}, u32[]{:S(2)}) collective-permute-start(bf16[4,32,640]{2,1,0:T(8,128)(2,1)S(1)} %collective-permute-done.10.refs_1_), channel_id=1, source_target_pairs={{0,1},{1,0},{2,3},{3,2},{4,5},{5,4},{6,7},{7,6},{8,9},{9,8},{10,11... | collective-permute-start | bytes 491528 | tf_op jit(solution)/shard_map/ppermute | solution.py:67
  34.1 5.9 %collective-permute-start.15 = (f32[8,1280]{1,0:T(8,128)S(1)}, f32[8,1280]{1,0:T(8,128)S(1)}, u32[]{:S(2)}, u32[]{:S(2)}) collective-permute-start(f32[8,1280]{1,0:T(8,128)S(1)} %get-tuple-element.44), channel_id=1, source_target_pairs={{0,12},{2,14},{4,8},{6,10},{8,4},{10,6},{12,0},{14,2},{1,13},{3,15... | collective-permute-start | bytes 122888 | tf_op jit(solution)/shard_map/ppermute | solution.py:63
  35.5 5.8 %collective-permute-start.14 = (f32[8,1280]{1,0:T(8,128)S(1)}, f32[8,1280]{1,0:T(8,128)S(1)}, u32[]{:S(2)}, u32[]{:S(2)}) collective-permute-start(f32[8,1280]{1,0:T(8,128)S(1)} %get-tuple-element.44), channel_id=1, source_target_pairs={{0,8},{2,10},{4,12},{6,14},{8,0},{10,2},{12,4},{14,6},{1,9},{3,11}... | collective-permute-start | bytes 122888 | tf_op jit(solution)/shard_map/ppermute | solution.py:63
  38.1 4.0 %collective-permute-start.13 = (f32[8,1280]{1,0:T(8,128)S(1)}, f32[8,1280]{1,0:T(8,128)S(1)}, u32[]{:S(2)}, u32[]{:S(2)}) collective-permute-start(f32[8,1280]{1,0:T(8,128)S(1)} %get-tuple-element.44), channel_id=1, source_target_pairs={{0,4},{2,6},{4,0},{6,2},{8,12},{10,14},{12,8},{14,10},{1,5},{3,7},... | collective-permute-start | bytes 122888 | tf_op jit(solution)/shard_map/ppermute | solution.py:63
  42.1 4.1 %collective-permute-start.16 = (f32[8,1280]{1,0:T(8,128)S(1)}, f32[8,1280]{1,0:T(8,128)S(1)}, u32[]{:S(2)}, u32[]{:S(2)}) collective-permute-start(f32[8,1280]{1,0:T(8,128)S(1)} %add_add_fusion), channel_id=1, source_target_pairs={{0,2},{2,0},{4,6},{6,4},{8,10},{10,8},{12,14},{14,12},{1,3},{3,1},... | collective-permute-start | bytes 122888 | tf_op jit(solution)/shard_map/ppermute | solution.py:63
  43.1 4.9 %collective-permute-start.18 = (f32[8,1280]{1,0:T(8,128)S(1)}, f32[8,1280]{1,0:T(8,128)S(1)}, u32[]{:S(2)}, u32[]{:S(2)}) collective-permute-start(f32[8,1280]{1,0:T(8,128)S(1)} %add_add_fusion), channel_id=1, source_target_pairs={{0,18},{2,16},{4,22},{6,20},{8,26},{10,24},{12,30},{14,28},{16,2},... | collective-permute-start | bytes 122888 | tf_op jit(solution)/shard_map/ppermute | solution.py:87
  44.4 4.0 %collective-permute-start.17 = (f32[8,1280]{1,0:T(8,128)S(1)}, f32[8,1280]{1,0:T(8,128)S(1)}, u32[]{:S(2)}, u32[]{:S(2)}) collective-permute-start(f32[8,1280]{1,0:T(8,128)S(1)} %add_add_fusion), channel_id=1, source_target_pairs={{0,16},{16,0},{1,17},{17,1},{2,18},{18,2},{3,19},{19,3},{4,20},{20... | collective-permute-start | bytes 122888 | tf_op jit(solution)/shard_map/ppermute | solution.py:86
  51.6 1.6 %collective-permute-start.19 = (bf16[8,32,640]{2,1,0:T(8,128)(2,1)S(1)}, bf16[8,32,640]{2,1,0:T(8,128)(2,1)S(1)}, u32[]{:S(2)}, u32[]{:S(2)}) collective-permute-start(bf16[8,32,640]{2,1,0:T(8,128)(2,1)S(1)} %get-tuple-element.46), channel_id=1, source_target_pairs={{0,1},{1,0},{2,3},{3,2},{4,5},{5,4},{6,7},{7,6},{8,9},{9,8},{10,11... | collective-permute-start | bytes 983048 | tf_op jit(solution)/shard_map/ppermute | solution.py:67
  54.1 14.2 %all-to-all-start = ((bf16[8,32,640]{2,1,0:T(8,128)(2,1)}), bf16[8,32,640]{2,1,0:T(8,128)(2,1)S(1)}, u32[]{:S(2)}, u32[]{:S(2)}) async-start(bf16[8,32,640]{2,1,0:T(8,128)(2,1)} %meet.1), calls=%async_computation | async-start | bytes 655360 | tf_op jit(solution)/shard_map/all_to_all | solution.py:696
  57.5 10.8 %collective-permute-start.21 = (f32[192,512]{1,0:T(8,128)S(1)}, f32[192,512]{1,0:T(8,128)S(1)}, u32[]{:S(2)}, u32[]{:S(2)}) collective-permute-start(f32[192,512]{1,0:T(8,128)S(1)} %get-tuple-element.47.time_mine), channel_id=1, source_target_pairs={{0,1},{1,0},{2,3},{3,2},{4,5},{5,4},{6,7},{7,6},{8,9},{9,8},{10,11... | collective-permute-start | bytes 1179656 | tf_op jit(solution)/shard_map/ppermute | solution.py:67
  68.3 1.6 %collective-permute-start.20 = (bf16[8,32,640]{2,1,0:T(8,128)(2,1)S(1)}, bf16[8,32,640]{2,1,0:T(8,128)(2,1)S(1)}, u32[]{:S(2)}, u32[]{:S(2)}) collective-permute-start(bf16[8,32,640]{2,1,0:T(8,128)(2,1)S(1)} %all-to-all-done.mine), channel_id=1, source_target_pairs={{0,1},{1,0},{2,3},{3,2},{4,5},{5,4},{6,7},{7,6},{8,9},{9,8},{10,11... | collective-permute-start | bytes 983048 | tf_op jit(solution)/shard_map/ppermute | solution.py:67
  (3 other events, 38.6 us)

commit v7 on v6

--- a/solution.py
+++ b/solution.py
@@ -502,7 +502,7 @@
             return jnp.where(row < z.lat, raw / half - raw[z.lat : z.lat + 1], 0.0)
 
         short = latent_rows(frame_sum(z, dot(pos[...], inner_cat[...], TN)))
-        proj8 = proj[:8].astype(F32)
+        proj8 = proj[...].astype(F32)[:8]
         proj24 = jnp.concatenate([proj8] * 3, axis=0).astype(BF16)
         kernel_grad = dot(proj24, stack3(short), TN) * scale
         time[...] = dot(hid_dec[...], v[...], TN)[: 3 * z.own] * scale
@@ -531,7 +531,7 @@
         grad3 = jnp.concatenate([gh, gm, gl], axis=0).astype(BF16)
         short = sum3(dot(grad3, hid_cat[...], NN))
         short3 = stack3(short)
-        proj8 = proj[:8].astype(F32)
+        proj8 = proj[...].astype(F32)[:8]
         proj24 = jnp.concatenate([proj8] * 3, axis=0).astype(BF16)
         time[...] = dot(short3, proj24, TN)[: 3 * z.own] * scale
         whole = sum3(dot(grad3, v[...], NN))

time: 71.7 us -> 71.7 us (level)
  no operation moved by 1% of the time
where the time goes in v7:
time: 71.7 us; the launch traced here: 71.3 us
  starting transfers between devices  29.9 us (42%)
  waiting for transfers between devices  29.6 us (41%)
  Pallas kernels  8.17 us (11%)
  other arithmetic  1.54 us (2%)
  local copies, waits for them, and re-layouts  1.35 us (2%)
  between operations  0.78 us (1%)
    ppermute x8, starting transfers between devices, swap(): return lax.ppermute(values, 'sp', [(i, i ^ distance) for i in range(count)])  12 us
    all_to_all x1, waiting for transfers between devices, local(): big = lax.all_to_all(big.astype(BF16), 'sp', 0, 0, tiled=True)  10.6 us
    ppermute x8, waiting for transfers between devices, swap(): return lax.ppermute(values, 'sp', [(i, i ^ distance) for i in range(count)])  8.45 us
    ppermute x4, starting transfers between devices, ring_gather(): first = lax.ppermute(first, 'sp', up)  7.42 us
    ppermute x5, waiting for transfers between devices, swap_core(): return lax.ppermute(values, 'dp', [(0, 1), (1, 0)])  4.57 us
    ppermute x3, starting transfers between devices, ring_gather(): second = lax.ppermute(second, 'sp', down)  4.21 us
    ppermute x4, waiting for transfers between devices, ring_gather(): first = lax.ppermute(first, 'sp', up)  3.76 us
    all_to_all x1, starting transfers between devices, local(): big = lax.all_to_all(big.astype(BF16), 'sp', 0, 0, tiled=True)  3.43 us
  transfers between devices with their start and end apart: 23, of which 14 were waited for; matrix products, arithmetic and copies ran while one was open for 3% of the time, Pallas kernels for 1%

profile of v7, /device:TPU:0, one launch (start us, length us, event | category | flops | bytes accessed | tf_op | source)
XLA Modules:
  0.0 71.3 jit_solution(7951360908574322264)
XLA Ops:
  0.6 3.0 %collective-permute-start.1 = (bf16[160,512]{1,0:T(8,128)(2,1)}, bf16[160,512]{1,0:T(8,128)(2,1)S(1)}, u32[]{:S(2)}, u32[]{:S(2)}) collective-permute-start(bf16[160,512]{1,0:T(8,128)(2,1)} %bitcast.13), channel_id=1, source_target_pairs={{4,0},{8,4},{12,8},{14,12},{10,14},{6,10},{2,6},{0,2},{5,1},{9,5},... | collective-permute-start | bytes 491528 | tf_op jit(solution)/shard_map/ppermute | solution.py:47
  6.3 2.0 %collective-permute-start.7 = (bf16[2,32,640]{2,1,0:T(8,128)(2,1)S(1)}, bf16[2,32,640]{2,1,0:T(8,128)(2,1)S(1)}, u32[]{:S(2)}, u32[]{:S(2)}) collective-permute-start(bf16[2,32,640]{2,1,0:T(8,128)(2,1)S(1)} %get-tuple-element.28), channel_id=1, source_target_pairs={{0,4},{2,6},{4,0},{6,2},{8,12},{10,14},{12,8},{14,10},{1,5},{3,7},... | collective-permute-start | bytes 245768 | tf_op jit(solution)/shard_map/ppermute | solution.py:63
  8.3 2.6 %collective-permute-start.8 = (bf16[2,32,640]{2,1,0:T(8,128)(2,1)S(1)}, bf16[2,32,640]{2,1,0:T(8,128)(2,1)S(1)}, u32[]{:S(2)}, u32[]{:S(2)}) collective-permute-start(bf16[2,32,640]{2,1,0:T(8,128)(2,1)S(1)} %get-tuple-element.29), channel_id=1, source_target_pairs={{0,8},{2,10},{4,12},{6,14},{8,0},{10,2},{12,4},{14,6},{1,9},{3,11}... | collective-permute-start | bytes 245768 | tf_op jit(solution)/shard_map/ppermute | solution.py:63
  13.7 2.8 %collective-permute-done.8 = bf16[2,32,640]{2,1,0:T(8,128)(2,1)S(1)} collective-permute-done((bf16[2,32,640]{2,1,0:T(8,128)(2,1)S(1)}, bf16[2,32,640]{2,1,0:T(8,128)(2,1)S(1)}, u32[]{:S(2)}, u32[]{:S(2)}) %collective-permute-start.8) | collective-permute-done | bytes 81952 | tf_op jit(solution)/shard_map/ppermute | solution.py:63
  16.4 1.6 %collective-permute-done.9 = bf16[2,32,640]{2,1,0:T(8,128)(2,1)S(1)} collective-permute-done((bf16[2,32,640]{2,1,0:T(8,128)(2,1)S(1)}, bf16[2,32,640]{2,1,0:T(8,128)(2,1)S(1)}, u32[]{:S(2)}, u32[]{:S(2)}) %collective-permute-start.9) | collective-permute-done | bytes 81952 | tf_op jit(solution)/shard_map/ppermute | solution.py:63
  18.1 2.0 %collective-permute-start.10 = (bf16[4,32,640]{2,1,0:T(8,128)(2,1)S(1)}, bf16[4,32,640]{2,1,0:T(8,128)(2,1)S(1)}, u32[]{:S(2)}, u32[]{:S(2)}) collective-permute-start(bf16[4,32,640]{2,1,0:T(8,128)(2,1)S(1)} %pad_maximum_fusion.1), channel_id=1, source_target_pairs={{0,2},{2,0},{4,6},{6,4},{8,10},{10,8},{12,14},{14,12},{1,3},{3,1},... | collective-permute-start | bytes 491528 | tf_op jit(solution)/shard_map/ppermute | solution.py:63
  20.1 3.9 %collective-permute-start.4 = (bf16[160,512]{1,0:T(8,128)(2,1)S(1)}, bf16[160,512]{1,0:T(8,128)(2,1)S(1)}, u32[]{:S(2)}, u32[]{:S(2)}) collective-permute-start(bf16[160,512]{1,0:T(8,128)(2,1)S(1)} %collective-permute-done.2.refs_3_), channel_id=1, source_target_pairs={{0,4},{4,8},{8,12},{12,14},{14,10},{10,6},{6,2},{2,0},{1,5},{5,9},... | collective-permute-start | bytes 491528 | tf_op jit(solution)/shard_map/ppermute | solution.py:43
  24.2 2.6 %collective-permute-done.4.refs_5_ = bf16[160,512]{1,0:T(8,128)(2,1)S(1)} collective-permute-done((bf16[160,512]{1,0:T(8,128)(2,1)S(1)}, bf16[160,512]{1,0:T(8,128)(2,1)S(1)}, u32[]{:S(2)}, u32[]{:S(2)}) %collective-permute-start.4) | collective-permute-done | bytes 163872 | tf_op jit(solution)/shard_map/ppermute | solution.py:43
  26.8 2.5 %collective-permute-start.6 = (bf16[160,512]{1,0:T(8,128)(2,1)S(1)}, bf16[160,512]{1,0:T(8,128)(2,1)S(1)}, u32[]{:S(2)}, u32[]{:S(2)}) collective-permute-start(bf16[160,512]{1,0:T(8,128)(2,1)S(1)} %collective-permute-done.4.refs_5_), channel_id=1, source_target_pairs={{0,4},{4,8},{8,12},{12,14},{14,10},{10,6},{6,2},{2,0},{1,5},{5,9},... | collective-permute-start | bytes 491528 | tf_op jit(solution)/shard_map/ppermute | solution.py:43
  29.4 1.3 %collective-permute-done.12.refs_3_ = bf16[4,32,640]{2,1,0:T(8,128)(2,1)S(1)} collective-permute-done((bf16[4,32,640]{2,1,0:T(8,128)(2,1)S(1)}, bf16[4,32,640]{2,1,0:T(8,128)(2,1)S(1)}, u32[]{:S(2)}, u32[]{:S(2)}) %collective-permute-start.12) | collective-permute-done | bytes 163872 | tf_op jit(solution)/shard_map/ppermute | solution.py:67
  32.2 1.9 %first.1 = (f32[8,1280]{1,0:T(8,128)S(1)}, bf16[1280,256]{1,0:T(8,128)(2,1)S(1)}, f32[8,160,128]{2,1,0:T(8,128)S(1)}, bf16[8,160,128]{2,1,0:T(8,128)(2,1)S(1)}, bf16[1280,512]{1,0:T(8,128)(2,1)S(1)}) custom-call(bf16[160,512]{1,0:T(8,128)(2,1)S(1)} %bitcast.15, bf16[160,512]{1,0:T(8,128)(2,1)S(1)} %collective-permute-done.refs_1_, ...), custom_call_target="tpu_custom_call" | custom-call | tf_op jit(solution)/shard_map/first/pallas_call | solution.py:647
  34.1 1.4 %collective-permute-start.15 = (f32[8,1280]{1,0:T(8,128)S(1)}, f32[8,1280]{1,0:T(8,128)S(1)}, u32[]{:S(2)}, u32[]{:S(2)}) collective-permute-start(f32[8,1280]{1,0:T(8,128)S(1)} %get-tuple-element.44), channel_id=1, source_target_pairs={{0,12},{2,14},{4,8},{6,10},{8,4},{10,6},{12,0},{14,2},{1,13},{3,15... | collective-permute-start | bytes 122888 | tf_op jit(solution)/shard_map/ppermute | solution.py:63
  35.5 2.6 %collective-permute-start.14 = (f32[8,1280]{1,0:T(8,128)S(1)}, f32[8,1280]{1,0:T(8,128)S(1)}, u32[]{:S(2)}, u32[]{:S(2)}) collective-permute-start(f32[8,1280]{1,0:T(8,128)S(1)} %get-tuple-element.44), channel_id=1, source_target_pairs={{0,8},{2,10},{4,12},{6,14},{8,0},{10,2},{12,4},{14,6},{1,9},{3,11}... | collective-permute-start | bytes 122888 | tf_op jit(solution)/shard_map/ppermute | solution.py:63
  38.5 1.4 %collective-permute-done.15 = f32[8,1280]{1,0:T(8,128)S(1)} collective-permute-done((f32[8,1280]{1,0:T(8,128)S(1)}, f32[8,1280]{1,0:T(8,128)S(1)}, u32[]{:S(2)}, u32[]{:S(2)}) %collective-permute-start.15) | collective-permute-done | bytes 40992 | tf_op jit(solution)/shard_map/ppermute | solution.py:63
  40.0 1.3 %collective-permute-done.14 = f32[8,1280]{1,0:T(8,128)S(1)} collective-permute-done((f32[8,1280]{1,0:T(8,128)S(1)}, f32[8,1280]{1,0:T(8,128)S(1)}, u32[]{:S(2)}, u32[]{:S(2)}) %collective-permute-start.14) | collective-permute-done | bytes 40992 | tf_op jit(solution)/shard_map/ppermute | solution.py:63
  43.1 1.3 %collective-permute-start.18 = (f32[8,1280]{1,0:T(8,128)S(1)}, f32[8,1280]{1,0:T(8,128)S(1)}, u32[]{:S(2)}, u32[]{:S(2)}) collective-permute-start(f32[8,1280]{1,0:T(8,128)S(1)} %add_add_fusion), channel_id=1, source_target_pairs={{0,18},{2,16},{4,22},{6,20},{8,26},{10,24},{12,30},{14,28},{16,2},... | collective-permute-start | bytes 122888 | tf_op jit(solution)/shard_map/ppermute | solution.py:87
  44.4 1.3 %collective-permute-start.17 = (f32[8,1280]{1,0:T(8,128)S(1)}, f32[8,1280]{1,0:T(8,128)S(1)}, u32[]{:S(2)}, u32[]{:S(2)}) collective-permute-start(f32[8,1280]{1,0:T(8,128)S(1)} %add_add_fusion), channel_id=1, source_target_pairs={{0,16},{16,0},{1,17},{17,1},{2,18},{18,2},{3,19},{19,3},{4,20},{20... | collective-permute-start | bytes 122888 | tf_op jit(solution)/shard_map/ppermute | solution.py:86
  46.2 1.8 %collective-permute-done.18 = f32[8,1280]{1,0:T(8,128)S(1)} collective-permute-done((f32[8,1280]{1,0:T(8,128)S(1)}, f32[8,1280]{1,0:T(8,128)S(1)}, u32[]{:S(2)}, u32[]{:S(2)}) %collective-permute-start.18) | collective-permute-done | bytes 40992 | tf_op jit(solution)/shard_map/ppermute | solution.py:87
  48.4 3.2 %second.1 = (f32[8,32,640]{2,1,0:T(8,128)S(1)}, bf16[8,32,640]{2,1,0:T(8,128)(2,1)S(1)}, f32[192,512]{1,0:T(8,128)S(1)}, f32[8,512]{1,0:T(8,128)}) custom-call(bf16[1280,512]{1,0:T(8,128)(2,1)S(1)} %get-tuple-element.38.refs_0_, bf16[512,640]{1,0:T(8,128)(2,1)S(1)} %get-tuple-element.35.refs_8_.refs_1_, bf16[1280,128]{1,0:T(8,128)(2,1)S(1)} %get-tuple-element.39.refs_2_, ...), custom_call_target="tpu_custom_call" | custom-call | tf_op jit(solution)/shard_map/second/pallas_call | solution.py:669
  51.7 1.6 %collective-permute-done.19.other = bf16[8,32,640]{2,1,0:T(8,128)(2,1)S(1)} collective-permute-done((bf16[8,32,640]{2,1,0:T(8,128)(2,1)S(1)}, bf16[8,32,640]{2,1,0:T(8,128)(2,1)S(1)}, u32[]{:S(2)}, u32[]{:S(2)}) %collective-permute-start.19) | collective-permute-done | bytes 327712 | tf_op jit(solution)/shard_map/ppermute | solution.py:67
  54.1 3.4 %all-to-all-start = ((bf16[8,32,640]{2,1,0:T(8,128)(2,1)}), bf16[8,32,640]{2,1,0:T(8,128)(2,1)S(1)}, u32[]{:S(2)}, u32[]{:S(2)}) async-start(bf16[8,32,640]{2,1,0:T(8,128)(2,1)} %meet.1), calls=%async_computation | async-start | bytes 655360 | tf_op jit(solution)/shard_map/all_to_all | solution.py:696
  57.7 10.6 %all-to-all-done.mine = bf16[8,32,640]{2,1,0:T(8,128)(2,1)S(1)} async-done(((bf16[8,32,640]{2,1,0:T(8,128)(2,1)}), bf16[8,32,640]{2,1,0:T(8,128)(2,1)S(1)}, u32[]{:S(2)}, u32[]{:S(2)}) %all-to-all-start) | async-done | bytes 327712 | tf_op jit(solution)/shard_map/all_to_all | solution.py:696
  68.3 1.6 %collective-permute-done.20.other = bf16[8,32,640]{2,1,0:T(8,128)(2,1)S(1)} collective-permute-done((bf16[8,32,640]{2,1,0:T(8,128)(2,1)S(1)}, bf16[8,32,640]{2,1,0:T(8,128)(2,1)S(1)}, u32[]{:S(2)}, u32[]{:S(2)}) %collective-permute-start.20) | collective-permute-done | bytes 327712 | tf_op jit(solution)/shard_map/ppermute | solution.py:67
  69.9 1.4 %last.1 = (f32[9,64,512]{2,1,0:T(8,128)}, f32[192,512]{1,0:T(8,128)}, f32[6,1,512]{2,1,0:T(1,128)}) custom-call(bf16[8,32,640]{2,1,0:T(8,128)(2,1)S(1)} %all-to-all-done.mine, bf16[8,32,640]{2,1,0:T(8,128)(2,1)S(1)} %collective-permute-done.20.other, f32[192,512]{1,0:T(8,128)S(1)} %get-tuple-element.47.time_mine, ...), custom_call_target="tpu_custom_call" | custom-call | tf_op jit(solution)/shard_map/last/pallas_call | solution.py:697
  (54 shorter events, 11.4 us)
Async XLA Ops:
  0.6 11.9 %collective-permute-start.1 = (bf16[160,512]{1,0:T(8,128)(2,1)}, bf16[160,512]{1,0:T(8,128)(2,1)S(1)}, u32[]{:S(2)}, u32[]{:S(2)}) collective-permute-start(bf16[160,512]{1,0:T(8,128)(2,1)} %bitcast.13), channel_id=1, source_target_pairs={{4,0},{8,4},{12,8},{14,12},{10,14},{6,10},{2,6},{0,2},{5,1},{9,5},... | collective-permute-start | bytes 491528 | tf_op jit(solution)/shard_map/ppermute | solution.py:47
  3.7 7.3 %collective-permute-start = (bf16[160,512]{1,0:T(8,128)(2,1)}, bf16[160,512]{1,0:T(8,128)(2,1)S(1)}, u32[]{:S(2)}, u32[]{:S(2)}) collective-permute-start(bf16[160,512]{1,0:T(8,128)(2,1)} %bitcast.14), channel_id=1, source_target_pairs={{0,4},{4,8},{8,12},{12,14},{14,10},{10,6},{6,2},{2,0},{1,5},{5,9},... | collective-permute-start | bytes 491528 | tf_op jit(solution)/shard_map/ppermute | solution.py:43
  5.7 23.6 %copy-start.2 = (bf16[1,3,64,512]{3,2,1,0:T(8,128)(2,1)S(1)}, bf16[1,3,64,512]{3,2,1,0:T(8,128)(2,1)}, u32[]{:S(2)}) copy-start(bf16[1,3,64,512]{3,2,1,0:T(8,128)(2,1)} %param.11) | copy-start | bytes 589828
  6.3 7.3 %collective-permute-start.7 = (bf16[2,32,640]{2,1,0:T(8,128)(2,1)S(1)}, bf16[2,32,640]{2,1,0:T(8,128)(2,1)S(1)}, u32[]{:S(2)}, u32[]{:S(2)}) collective-permute-start(bf16[2,32,640]{2,1,0:T(8,128)(2,1)S(1)} %get-tuple-element.28), channel_id=1, source_target_pairs={{0,4},{2,6},{4,0},{6,2},{8,12},{10,14},{12,8},{14,10},{1,5},{3,7},... | collective-permute-start | bytes 245768 | tf_op jit(solution)/shard_map/ppermute | solution.py:63
  8.3 8.1 %collective-permute-start.8 = (bf16[2,32,640]{2,1,0:T(8,128)(2,1)S(1)}, bf16[2,32,640]{2,1,0:T(8,128)(2,1)S(1)}, u32[]{:S(2)}, u32[]{:S(2)}) collective-permute-start(bf16[2,32,640]{2,1,0:T(8,128)(2,1)S(1)} %get-tuple-element.29), channel_id=1, source_target_pairs={{0,8},{2,10},{4,12},{6,14},{8,0},{10,2},{12,4},{14,6},{1,9},{3,11}... | collective-permute-start | bytes 245768 | tf_op jit(solution)/shard_map/ppermute | solution.py:63
  10.9 7.1 %collective-permute-start.9 = (bf16[2,32,640]{2,1,0:T(8,128)(2,1)S(1)}, bf16[2,32,640]{2,1,0:T(8,128)(2,1)S(1)}, u32[]{:S(2)}, u32[]{:S(2)}) collective-permute-start(bf16[2,32,640]{2,1,0:T(8,128)(2,1)S(1)} %get-tuple-element.30), channel_id=1, source_target_pairs={{0,12},{2,14},{4,8},{6,10},{8,4},{10,6},{12,0},{14,2},{1,13},{3,15... | collective-permute-start | bytes 245768 | tf_op jit(solution)/shard_map/ppermute | solution.py:63
  10.9 7.1 %collective-permute-start.2 = (bf16[160,512]{1,0:T(8,128)(2,1)S(1)}, bf16[160,512]{1,0:T(8,128)(2,1)S(1)}, u32[]{:S(2)}, u32[]{:S(2)}) collective-permute-start(bf16[160,512]{1,0:T(8,128)(2,1)S(1)} %collective-permute-done.refs_1_), channel_id=1, source_target_pairs={{0,4},{4,8},{8,12},{12,14},{14,10},{10,6},{6,2},{2,0},{1,5},{5,9},... | collective-permute-start | bytes 491528 | tf_op jit(solution)/shard_map/ppermute | solution.py:43
  12.5 11.6 %collective-permute-start.3 = (bf16[160,512]{1,0:T(8,128)(2,1)S(1)}, bf16[160,512]{1,0:T(8,128)(2,1)S(1)}, u32[]{:S(2)}, u32[]{:S(2)}) collective-permute-start(bf16[160,512]{1,0:T(8,128)(2,1)S(1)} %collective-permute-done.1.refs_2_), channel_id=1, source_target_pairs={{4,0},{8,4},{12,8},{14,12},{10,14},{6,10},{2,6},{0,2},{5,1},{9,5},... | collective-permute-start | bytes 491528 | tf_op jit(solution)/shard_map/ppermute | solution.py:47
  18.1 11.2 %collective-permute-start.10 = (bf16[4,32,640]{2,1,0:T(8,128)(2,1)S(1)}, bf16[4,32,640]{2,1,0:T(8,128)(2,1)S(1)}, u32[]{:S(2)}, u32[]{:S(2)}) collective-permute-start(bf16[4,32,640]{2,1,0:T(8,128)(2,1)S(1)} %pad_maximum_fusion.1), channel_id=1, source_target_pairs={{0,2},{2,0},{4,6},{6,4},{8,10},{10,8},{12,14},{14,12},{1,3},{3,1},... | collective-permute-start | bytes 491528 | tf_op jit(solution)/shard_map/ppermute | solution.py:63
  20.1 6.8 %collective-permute-start.4 = (bf16[160,512]{1,0:T(8,128)(2,1)S(1)}, bf16[160,512]{1,0:T(8,128)(2,1)S(1)}, u32[]{:S(2)}, u32[]{:S(2)}) collective-permute-start(bf16[160,512]{1,0:T(8,128)(2,1)S(1)} %collective-permute-done.2.refs_3_), channel_id=1, source_target_pairs={{0,4},{4,8},{8,12},{12,14},{14,10},{10,6},{6,2},{2,0},{1,5},{5,9},... | collective-permute-start | bytes 491528 | tf_op jit(solution)/shard_map/ppermute | solution.py:43
  24.0 5.4 %collective-permute-start.11 = (bf16[4,32,640]{2,1,0:T(8,128)(2,1)S(1)}, bf16[4,32,640]{2,1,0:T(8,128)(2,1)S(1)}, u32[]{:S(2)}, u32[]{:S(2)}) collective-permute-start(bf16[4,32,640]{2,1,0:T(8,128)(2,1)S(1)} %pad_maximum_fusion.refs_0_), channel_id=1, source_target_pairs={{0,1},{1,0},{2,3},{3,2},{4,5},{5,4},{6,7},{7,6},{8,9},{9,8},{10,11... | collective-permute-start | bytes 491528 | tf_op jit(solution)/shard_map/ppermute | solution.py:67
  24.1 6.9 %collective-permute-start.5 = (bf16[160,512]{1,0:T(8,128)(2,1)S(1)}, bf16[160,512]{1,0:T(8,128)(2,1)S(1)}, u32[]{:S(2)}, u32[]{:S(2)}) collective-permute-start(bf16[160,512]{1,0:T(8,128)(2,1)S(1)} %collective-permute-done.3.refs_4_), channel_id=1, source_target_pairs={{4,0},{8,4},{12,8},{14,12},{10,14},{6,10},{2,6},{0,2},{5,1},{9,5},... | collective-permute-start | bytes 491528 | tf_op jit(solution)/shard_map/ppermute | solution.py:47
  26.8 5.3 %collective-permute-start.6 = (bf16[160,512]{1,0:T(8,128)(2,1)S(1)}, bf16[160,512]{1,0:T(8,128)(2,1)S(1)}, u32[]{:S(2)}, u32[]{:S(2)}) collective-permute-start(bf16[160,512]{1,0:T(8,128)(2,1)S(1)} %collective-permute-done.4.refs_5_), channel_id=1, source_target_pairs={{0,4},{4,8},{8,12},{12,14},{14,10},{10,6},{6,2},{2,0},{1,5},{5,9},... | collective-permute-start | bytes 491528 | tf_op jit(solution)/shard_map/ppermute | solution.py:43
  29.3 1.4 %collective-permute-start.12 = (bf16[4,32,640]{2,1,0:T(8,128)(2,1)S(1)}, bf16[4,32,640]{2,1,0:T(8,128)(2,1)S(1)}, u32[]{:S(2)}, u32[]{:S(2)}) collective-permute-start(bf16[4,32,640]{2,1,0:T(8,128)(2,1)S(1)} %collective-permute-done.10.refs_1_), channel_id=1, source_target_pairs={{0,1},{1,0},{2,3},{3,2},{4,5},{5,4},{6,7},{7,6},{8,9},{9,8},{10,11... | collective-permute-start | bytes 491528 | tf_op jit(solution)/shard_map/ppermute | solution.py:67
  34.1 5.9 %collective-permute-start.15 = (f32[8,1280]{1,0:T(8,128)S(1)}, f32[8,1280]{1,0:T(8,128)S(1)}, u32[]{:S(2)}, u32[]{:S(2)}) collective-permute-start(f32[8,1280]{1,0:T(8,128)S(1)} %get-tuple-element.44), channel_id=1, source_target_pairs={{0,12},{2,14},{4,8},{6,10},{8,4},{10,6},{12,0},{14,2},{1,13},{3,15... | collective-permute-start | bytes 122888 | tf_op jit(solution)/shard_map/ppermute | solution.py:63
  35.5 5.8 %collective-permute-start.14 = (f32[8,1280]{1,0:T(8,128)S(1)}, f32[8,1280]{1,0:T(8,128)S(1)}, u32[]{:S(2)}, u32[]{:S(2)}) collective-permute-start(f32[8,1280]{1,0:T(8,128)S(1)} %get-tuple-element.44), channel_id=1, source_target_pairs={{0,8},{2,10},{4,12},{6,14},{8,0},{10,2},{12,4},{14,6},{1,9},{3,11}... | collective-permute-start | bytes 122888 | tf_op jit(solution)/shard_map/ppermute | solution.py:63
  38.1 4.0 %collective-permute-start.13 = (f32[8,1280]{1,0:T(8,128)S(1)}, f32[8,1280]{1,0:T(8,128)S(1)}, u32[]{:S(2)}, u32[]{:S(2)}) collective-permute-start(f32[8,1280]{1,0:T(8,128)S(1)} %get-tuple-element.44), channel_id=1, source_target_pairs={{0,4},{2,6},{4,0},{6,2},{8,12},{10,14},{12,8},{14,10},{1,5},{3,7},... | collective-permute-start | bytes 122888 | tf_op jit(solution)/shard_map/ppermute | solution.py:63
  42.1 4.1 %collective-permute-start.16 = (f32[8,1280]{1,0:T(8,128)S(1)}, f32[8,1280]{1,0:T(8,128)S(1)}, u32[]{:S(2)}, u32[]{:S(2)}) collective-permute-start(f32[8,1280]{1,0:T(8,128)S(1)} %add_add_fusion), channel_id=1, source_target_pairs={{0,2},{2,0},{4,6},{6,4},{8,10},{10,8},{12,14},{14,12},{1,3},{3,1},... | collective-permute-start | bytes 122888 | tf_op jit(solution)/shard_map/ppermute | solution.py:63
  43.1 4.9 %collective-permute-start.18 = (f32[8,1280]{1,0:T(8,128)S(1)}, f32[8,1280]{1,0:T(8,128)S(1)}, u32[]{:S(2)}, u32[]{:S(2)}) collective-permute-start(f32[8,1280]{1,0:T(8,128)S(1)} %add_add_fusion), channel_id=1, source_target_pairs={{0,18},{2,16},{4,22},{6,20},{8,26},{10,24},{12,30},{14,28},{16,2},... | collective-permute-start | bytes 122888 | tf_op jit(solution)/shard_map/ppermute | solution.py:87
  44.4 4.0 %collective-permute-start.17 = (f32[8,1280]{1,0:T(8,128)S(1)}, f32[8,1280]{1,0:T(8,128)S(1)}, u32[]{:S(2)}, u32[]{:S(2)}) collective-permute-start(f32[8,1280]{1,0:T(8,128)S(1)} %add_add_fusion), channel_id=1, source_target_pairs={{0,16},{16,0},{1,17},{17,1},{2,18},{18,2},{3,19},{19,3},{4,20},{20... | collective-permute-start | bytes 122888 | tf_op jit(solution)/shard_map/ppermute | solution.py:86
  51.6 1.6 %collective-permute-start.19 = (bf16[8,32,640]{2,1,0:T(8,128)(2,1)S(1)}, bf16[8,32,640]{2,1,0:T(8,128)(2,1)S(1)}, u32[]{:S(2)}, u32[]{:S(2)}) collective-permute-start(bf16[8,32,640]{2,1,0:T(8,128)(2,1)S(1)} %get-tuple-element.46), channel_id=1, source_target_pairs={{0,1},{1,0},{2,3},{3,2},{4,5},{5,4},{6,7},{7,6},{8,9},{9,8},{10,11... | collective-permute-start | bytes 983048 | tf_op jit(solution)/shard_map/ppermute | solution.py:67
  54.1 14.2 %all-to-all-start = ((bf16[8,32,640]{2,1,0:T(8,128)(2,1)}), bf16[8,32,640]{2,1,0:T(8,128)(2,1)S(1)}, u32[]{:S(2)}, u32[]{:S(2)}) async-start(bf16[8,32,640]{2,1,0:T(8,128)(2,1)} %meet.1), calls=%async_computation | async-start | bytes 655360 | tf_op jit(solution)/shard_map/all_to_all | solution.py:696
  57.5 10.8 %collective-permute-start.21 = (f32[192,512]{1,0:T(8,128)S(1)}, f32[192,512]{1,0:T(8,128)S(1)}, u32[]{:S(2)}, u32[]{:S(2)}) collective-permute-start(f32[192,512]{1,0:T(8,128)S(1)} %get-tuple-element.47.time_mine), channel_id=1, source_target_pairs={{0,1},{1,0},{2,3},{3,2},{4,5},{5,4},{6,7},{7,6},{8,9},{9,8},{10,11... | collective-permute-start | bytes 1179656 | tf_op jit(solution)/shard_map/ppermute | solution.py:67
  68.3 1.6 %collective-permute-start.20 = (bf16[8,32,640]{2,1,0:T(8,128)(2,1)S(1)}, bf16[8,32,640]{2,1,0:T(8,128)(2,1)S(1)}, u32[]{:S(2)}, u32[]{:S(2)}) collective-permute-start(bf16[8,32,640]{2,1,0:T(8,128)(2,1)S(1)} %all-to-all-done.mine), channel_id=1, source_target_pairs={{0,1},{1,0},{2,3},{3,2},{4,5},{5,4},{6,7},{7,6},{8,9},{9,8},{10,11... | collective-permute-start | bytes 983048 | tf_op jit(solution)/shard_map/ppermute | solution.py:67
  (3 other events, 38.6 us)

commit v8 on v7

--- a/solution.py
+++ b/solution.py
@@ -40,11 +40,12 @@
     shards, steps = [shard], [0]
     first = second = shard
     for step in range(1, count // 2 + 1):
+        if step < count - step:
+            second = lax.ppermute(second, "sp", down)
         first = lax.ppermute(first, "sp", up)
         shards.append(first)
         steps.append(-step)
         if step < count - step:
-            second = lax.ppermute(second, "sp", down)
             shards.append(second)
             steps.append(step)
     return shards, steps
@@ -304,7 +305,15 @@
     me = lax.axis_index("sp")
     core = lax.axis_index("dp")
     lane = lax.broadcasted_iota(jnp.int32, (z.half, LANES), 1)
-    code_block = codes[...]
+    code_rows = []
+    for t in range(z.frames):
+        code_rows += [codes[l * z.frames + t] for l in range(z.lat)]
+        code_rows += [jnp.ones((1, z.cols), jnp.int32), jnp.zeros((7 - z.lat, z.cols), jnp.int32)]
+    code_rows.append(jnp.zeros((LANES - 8 * z.frames, z.cols), jnp.int32))
+    code_block = jnp.concatenate(code_rows, axis=0).astype(F32)
+    code_block = jnp.concatenate([code_block, jnp.zeros((LANES, LANES - z.cols), F32)], axis=1)
+    code_block = code_block.T[: z.half if z.code_row == 0 else z.code_rows]
+    code_block = lanes_down(code_block, -z.code_lane)
     for distance in range(z.sp):
         begin = lax.bitwise_xor(me, distance) * z.own
         block, offset = begin // LANES, begin % LANES
@@ -604,12 +613,7 @@
     room = 20 * 1024 * 1024 + 5 * z.count * chans * 4 // 2 * (1 if z.sp > 8 else 0)
     params = pltpu.CompilerParams(vmem_limit_bytes=min(room, 60 * 1024 * 1024))
 
-    codes = jnp.transpose(code_index[0, :, :, 0].astype(F32), (2, 1, 0))
-    codes = jnp.concatenate([codes, jnp.ones((cols, frames, 1), F32)], axis=2)
-    codes = jnp.pad(codes, ((0, 0), (0, 0), (0, 7 - lat))).reshape(cols, 8 * frames)
-    left = z.code_lane % LANES
-    code_rows = z.half if z.code_row == 0 else z.code_rows
-    codes = jnp.pad(codes, ((0, code_rows - cols), (left, LANES - left - 8 * frames)))
+    codes = code_index.reshape(lat * frames, 1, cols)
     pairs = pl.pallas_call(
         functools.partial(piece_kernel, z),
         out_shape=[shaped((2, z.piece_rows, z.wide), BF16)] * (z.sp // 2),

time: 71.7 us -> 71.3 us (level)
  other arithmetic: 1.54 us -> 0.81 us
    ppermute x3, starting transfers between devices: 4.21 us -> 1.2 us  [ring_gather(): second = lax.ppermute(second, 'sp', down)]
    ppermute x4, starting transfers between devices: 7.42 us -> 9.92 us  [ring_gather(): first = lax.ppermute(first, 'sp', up)]
    transpose x1 -> x0, other arithmetic: 0.72 us -> none  [local(): codes = jnp.transpose(code_index[0, :, :, 0].astype(F32), (2, 1, 0))]
    unnamed x8 -> x10, local copies, waits for them, and re-layouts: 1.09 us -> 1.79 us
  transfers between devices with their start and end apart: 23 -> 23, of which waited for: 14 -> 14; matrix products, arithmetic and copies ran while one was open for 3% -> 1% of each run, Pallas kernels for 1% -> 1%
where the time goes in v8:
time: 71.3 us; the launch traced here: 70.9 us
  waiting for transfers between devices  29.7 us (42%)
  starting transfers between devices  29.5 us (41%)
  Pallas kernels  8.23 us (12%)
  local copies, waits for them, and re-layouts  1.91 us (3%)
  other arithmetic  0.81 us (1%)
  between operations  0.78 us (1%)
    ppermute x8, starting transfers between devices, swap(): return lax.ppermute(values, 'sp', [(i, i ^ distance) for i in range(count)])  12.5 us
    all_to_all x1, waiting for transfers between devices, local(): big = lax.all_to_all(big.astype(BF16), 'sp', 0, 0, tiled=True)  10.6 us
    ppermute x4, starting transfers between devices, ring_gather(): first = lax.ppermute(first, 'sp', up)  9.92 us
    ppermute x8, waiting for transfers between devices, swap(): return lax.ppermute(values, 'sp', [(i, i ^ distance) for i in range(count)])  8.45 us
    ppermute x5, waiting for transfers between devices, swap_core(): return lax.ppermute(values, 'dp', [(0, 1), (1, 0)])  4.57 us
    ppermute x4, waiting for transfers between devices, ring_gather(): first = lax.ppermute(first, 'sp', up)  3.76 us
    all_to_all x1, starting transfers between devices, local(): big = lax.all_to_all(big.astype(BF16), 'sp', 0, 0, tiled=True)  3.52 us
    pallas_call x1, Pallas kernels, local(): pl.pallas_call(functools.partial(second_kernel, z, scale), out_shape=(sha...  3.22 us
  transfers between devices with their start and end apart: 23, of which 14 were waited for; matrix products, arithmetic and copies ran while one was open for 1% of the time, Pallas kernels for 1%

profile of v8, /device:TPU:0, one launch (start us, length us, event | category | flops | bytes accessed | tf_op | source)
XLA Modules:
  0.0 70.9 jit_solution(9339290912036699986)
XLA Ops:
  0.6 3.1 %collective-permute-start = (bf16[160,512]{1,0:T(8,128)(2,1)}, bf16[160,512]{1,0:T(8,128)(2,1)S(1)}, u32[]{:S(2)}, u32[]{:S(2)}) collective-permute-start(bf16[160,512]{1,0:T(8,128)(2,1)} %bitcast.8), channel_id=1, source_target_pairs={{0,4},{4,8},{8,12},{12,14},{14,10},{10,6},{6,2},{2,0},{1,5},{5,9},... | collective-permute-start | bytes 491528 | tf_op jit(solution)/shard_map/ppermute | solution.py:45
  6.2 2.0 %collective-permute-start.7 = (bf16[2,32,640]{2,1,0:T(8,128)(2,1)S(1)}, bf16[2,32,640]{2,1,0:T(8,128)(2,1)S(1)}, u32[]{:S(2)}, u32[]{:S(2)}) collective-permute-start(bf16[2,32,640]{2,1,0:T(8,128)(2,1)S(1)} %get-tuple-element.28), channel_id=1, source_target_pairs={{0,4},{2,6},{4,0},{6,2},{8,12},{10,14},{12,8},{14,10},{1,5},{3,7},... | collective-permute-start | bytes 245768 | tf_op jit(solution)/shard_map/ppermute | solution.py:64
  8.2 2.6 %collective-permute-start.8 = (bf16[2,32,640]{2,1,0:T(8,128)(2,1)S(1)}, bf16[2,32,640]{2,1,0:T(8,128)(2,1)S(1)}, u32[]{:S(2)}, u32[]{:S(2)}) collective-permute-start(bf16[2,32,640]{2,1,0:T(8,128)(2,1)S(1)} %get-tuple-element.29), channel_id=1, source_target_pairs={{0,8},{2,10},{4,12},{6,14},{8,0},{10,2},{12,4},{14,6},{1,9},{3,11}... | collective-permute-start | bytes 245768 | tf_op jit(solution)/shard_map/ppermute | solution.py:64
  12.4 1.1 %collective-permute-start.3 = (bf16[160,512]{1,0:T(8,128)(2,1)S(1)}, bf16[160,512]{1,0:T(8,128)(2,1)S(1)}, u32[]{:S(2)}, u32[]{:S(2)}) collective-permute-start(bf16[160,512]{1,0:T(8,128)(2,1)S(1)} %collective-permute-done.1.refs_2_), channel_id=1, source_target_pairs={{4,0},{8,4},{12,8},{14,12},{10,14},{6,10},{2,6},{0,2},{5,1},{9,5},... | collective-permute-start | bytes 491528 | tf_op jit(solution)/shard_map/ppermute | solution.py:44
  13.5 3.5 %collective-permute-done.8 = bf16[2,32,640]{2,1,0:T(8,128)(2,1)S(1)} collective-permute-done((bf16[2,32,640]{2,1,0:T(8,128)(2,1)S(1)}, bf16[2,32,640]{2,1,0:T(8,128)(2,1)S(1)}, u32[]{:S(2)}, u32[]{:S(2)}) %collective-permute-start.8) | collective-permute-done | bytes 81952 | tf_op jit(solution)/shard_map/ppermute | solution.py:64
  18.0 2.0 %collective-permute-start.10 = (bf16[4,32,640]{2,1,0:T(8,128)(2,1)S(1)}, bf16[4,32,640]{2,1,0:T(8,128)(2,1)S(1)}, u32[]{:S(2)}, u32[]{:S(2)}) collective-permute-start(bf16[4,32,640]{2,1,0:T(8,128)(2,1)S(1)} %pad_maximum_fusion.1), channel_id=1, source_target_pairs={{0,2},{2,0},{4,6},{6,4},{8,10},{10,8},{12,14},{14,12},{1,3},{3,1},... | collective-permute-start | bytes 491528 | tf_op jit(solution)/shard_map/ppermute | solution.py:64
  20.0 3.5 %collective-permute-start.4 = (bf16[160,512]{1,0:T(8,128)(2,1)S(1)}, bf16[160,512]{1,0:T(8,128)(2,1)S(1)}, u32[]{:S(2)}, u32[]{:S(2)}) collective-permute-start(bf16[160,512]{1,0:T(8,128)(2,1)S(1)} %collective-permute-done.2.refs_3_), channel_id=1, source_target_pairs={{0,4},{4,8},{8,12},{12,14},{14,10},{10,6},{6,2},{2,0},{1,5},{5,9},... | collective-permute-start | bytes 491528 | tf_op jit(solution)/shard_map/ppermute | solution.py:45
  23.7 2.6 %collective-permute-done.4.refs_5_ = bf16[160,512]{1,0:T(8,128)(2,1)S(1)} collective-permute-done((bf16[160,512]{1,0:T(8,128)(2,1)S(1)}, bf16[160,512]{1,0:T(8,128)(2,1)S(1)}, u32[]{:S(2)}, u32[]{:S(2)}) %collective-permute-start.4) | collective-permute-done | bytes 163872 | tf_op jit(solution)/shard_map/ppermute | solution.py:45
  26.3 2.5 %collective-permute-start.6 = (bf16[160,512]{1,0:T(8,128)(2,1)S(1)}, bf16[160,512]{1,0:T(8,128)(2,1)S(1)}, u32[]{:S(2)}, u32[]{:S(2)}) collective-permute-start(bf16[160,512]{1,0:T(8,128)(2,1)S(1)} %collective-permute-done.4.refs_5_), channel_id=1, source_target_pairs={{0,4},{4,8},{8,12},{12,14},{14,10},{10,6},{6,2},{2,0},{1,5},{5,9},... | collective-permute-start | bytes 491528 | tf_op jit(solution)/shard_map/ppermute | solution.py:45
  28.9 1.3 %collective-permute-done.12.refs_3_ = bf16[4,32,640]{2,1,0:T(8,128)(2,1)S(1)} collective-permute-done((bf16[4,32,640]{2,1,0:T(8,128)(2,1)S(1)}, bf16[4,32,640]{2,1,0:T(8,128)(2,1)S(1)}, u32[]{:S(2)}, u32[]{:S(2)}) %collective-permute-start.12) | collective-permute-done | bytes 163872 | tf_op jit(solution)/shard_map/ppermute | solution.py:68
  30.5 1.1 %collective-permute-done.6.refs_7_ = bf16[160,512]{1,0:T(8,128)(2,1)S(1)} collective-permute-done((bf16[160,512]{1,0:T(8,128)(2,1)S(1)}, bf16[160,512]{1,0:T(8,128)(2,1)S(1)}, u32[]{:S(2)}, u32[]{:S(2)}) %collective-permute-start.6) | collective-permute-done | bytes 163872 | tf_op jit(solution)/shard_map/ppermute | solution.py:45
  31.6 1.9 %first.1 = (f32[8,1280]{1,0:T(8,128)S(1)}, bf16[1280,256]{1,0:T(8,128)(2,1)S(1)}, f32[8,160,128]{2,1,0:T(8,128)S(1)}, bf16[8,160,128]{2,1,0:T(8,128)(2,1)S(1)}, bf16[1280,512]{1,0:T(8,128)(2,1)S(1)}) custom-call(bf16[160,512]{1,0:T(8,128)(2,1)S(1)} %bitcast.10, bf16[160,512]{1,0:T(8,128)(2,1)S(1)} %collective-permute-done.refs_1_, ...), custom_call_target="tpu_custom_call" | custom-call | tf_op jit(solution)/shard_map/first/pallas_call | solution.py:651
  33.6 1.5 %collective-permute-start.15 = (f32[8,1280]{1,0:T(8,128)S(1)}, f32[8,1280]{1,0:T(8,128)S(1)}, u32[]{:S(2)}, u32[]{:S(2)}) collective-permute-start(f32[8,1280]{1,0:T(8,128)S(1)} %get-tuple-element.44), channel_id=1, source_target_pairs={{0,12},{2,14},{4,8},{6,10},{8,4},{10,6},{12,0},{14,2},{1,13},{3,15... | collective-permute-start | bytes 122888 | tf_op jit(solution)/shard_map/ppermute | solution.py:64
  35.1 2.5 %collective-permute-start.14 = (f32[8,1280]{1,0:T(8,128)S(1)}, f32[8,1280]{1,0:T(8,128)S(1)}, u32[]{:S(2)}, u32[]{:S(2)}) collective-permute-start(f32[8,1280]{1,0:T(8,128)S(1)} %get-tuple-element.44), channel_id=1, source_target_pairs={{0,8},{2,10},{4,12},{6,14},{8,0},{10,2},{12,4},{14,6},{1,9},{3,11}... | collective-permute-start | bytes 122888 | tf_op jit(solution)/shard_map/ppermute | solution.py:64
  38.0 1.4 %collective-permute-done.15 = f32[8,1280]{1,0:T(8,128)S(1)} collective-permute-done((f32[8,1280]{1,0:T(8,128)S(1)}, f32[8,1280]{1,0:T(8,128)S(1)}, u32[]{:S(2)}, u32[]{:S(2)}) %collective-permute-start.15) | collective-permute-done | bytes 40992 | tf_op jit(solution)/shard_map/ppermute | solution.py:64
  39.5 1.3 %collective-permute-done.14 = f32[8,1280]{1,0:T(8,128)S(1)} collective-permute-done((f32[8,1280]{1,0:T(8,128)S(1)}, f32[8,1280]{1,0:T(8,128)S(1)}, u32[]{:S(2)}, u32[]{:S(2)}) %collective-permute-start.14) | collective-permute-done | bytes 40992 | tf_op jit(solution)/shard_map/ppermute | solution.py:64
  41.6 1.4 %collective-permute-start.16 = (f32[8,1280]{1,0:T(8,128)S(1)}, f32[8,1280]{1,0:T(8,128)S(1)}, u32[]{:S(2)}, u32[]{:S(2)}) collective-permute-start(f32[8,1280]{1,0:T(8,128)S(1)} %add_add_fusion), channel_id=1, source_target_pairs={{0,2},{2,0},{4,6},{6,4},{8,10},{10,8},{12,14},{14,12},{1,3},{3,1},... | collective-permute-start | bytes 122888 | tf_op jit(solution)/shard_map/ppermute | solution.py:64
  45.7 2.2 %collective-permute-done.18 = f32[8,1280]{1,0:T(8,128)S(1)} collective-permute-done((f32[8,1280]{1,0:T(8,128)S(1)}, f32[8,1280]{1,0:T(8,128)S(1)}, u32[]{:S(2)}, u32[]{:S(2)}) %collective-permute-start.18) | collective-permute-done | bytes 40992 | tf_op jit(solution)/shard_map/ppermute | solution.py:88
  48.1 3.2 %second.1 = (f32[8,32,640]{2,1,0:T(8,128)S(1)}, bf16[8,32,640]{2,1,0:T(8,128)(2,1)S(1)}, f32[192,512]{1,0:T(8,128)S(1)}, f32[8,512]{1,0:T(8,128)}) custom-call(bf16[1280,512]{1,0:T(8,128)(2,1)S(1)} %get-tuple-element.38.refs_0_, bf16[512,640]{1,0:T(8,128)(2,1)S(1)} %get-tuple-element.35.refs_8_.refs_1_, bf16[1280,128]{1,0:T(8,128)(2,1)S(1)} %get-tuple-element.39.refs_2_, ...), custom_call_target="tpu_custom_call" | custom-call | tf_op jit(solution)/shard_map/second/pallas_call | solution.py:673
  51.3 1.6 %collective-permute-done.19.other = bf16[8,32,640]{2,1,0:T(8,128)(2,1)S(1)} collective-permute-done((bf16[8,32,640]{2,1,0:T(8,128)(2,1)S(1)}, bf16[8,32,640]{2,1,0:T(8,128)(2,1)S(1)}, u32[]{:S(2)}, u32[]{:S(2)}) %collective-permute-start.19) | collective-permute-done | bytes 327712 | tf_op jit(solution)/shard_map/ppermute | solution.py:68
  53.7 3.5 %all-to-all-start = ((bf16[8,32,640]{2,1,0:T(8,128)(2,1)}), bf16[8,32,640]{2,1,0:T(8,128)(2,1)S(1)}, u32[]{:S(2)}, u32[]{:S(2)}) async-start(bf16[8,32,640]{2,1,0:T(8,128)(2,1)} %meet.1), calls=%async_computation | async-start | bytes 655360 | tf_op jit(solution)/shard_map/all_to_all | solution.py:700
  57.4 10.6 %all-to-all-done.mine = bf16[8,32,640]{2,1,0:T(8,128)(2,1)S(1)} async-done(((bf16[8,32,640]{2,1,0:T(8,128)(2,1)}), bf16[8,32,640]{2,1,0:T(8,128)(2,1)S(1)}, u32[]{:S(2)}, u32[]{:S(2)}) %all-to-all-start) | async-done | bytes 327712 | tf_op jit(solution)/shard_map/all_to_all | solution.py:700
  67.9 1.6 %collective-permute-done.20.other = bf16[8,32,640]{2,1,0:T(8,128)(2,1)S(1)} collective-permute-done((bf16[8,32,640]{2,1,0:T(8,128)(2,1)S(1)}, bf16[8,32,640]{2,1,0:T(8,128)(2,1)S(1)}, u32[]{:S(2)}, u32[]{:S(2)}) %collective-permute-start.20) | collective-permute-done | bytes 327712 | tf_op jit(solution)/shard_map/ppermute | solution.py:68
  69.6 1.4 %last.1 = (f32[9,64,512]{2,1,0:T(8,128)}, f32[192,512]{1,0:T(8,128)}, f32[6,1,512]{2,1,0:T(1,128)}) custom-call(bf16[8,32,640]{2,1,0:T(8,128)(2,1)S(1)} %all-to-all-done.mine, bf16[8,32,640]{2,1,0:T(8,128)(2,1)S(1)} %collective-permute-done.20.other, f32[192,512]{1,0:T(8,128)S(1)} %get-tuple-element.47.time_mine, ...), custom_call_target="tpu_custom_call" | custom-call | tf_op jit(solution)/shard_map/last/pallas_call | solution.py:701
  (52 shorter events, 10.7 us)
Async XLA Ops:
  0.6 10.2 %collective-permute-start = (bf16[160,512]{1,0:T(8,128)(2,1)}, bf16[160,512]{1,0:T(8,128)(2,1)S(1)}, u32[]{:S(2)}, u32[]{:S(2)}) collective-permute-start(bf16[160,512]{1,0:T(8,128)(2,1)} %bitcast.8), channel_id=1, source_target_pairs={{0,4},{4,8},{8,12},{12,14},{14,10},{10,6},{6,2},{2,0},{1,5},{5,9},... | collective-permute-start | bytes 491528 | tf_op jit(solution)/shard_map/ppermute | solution.py:45
  3.7 8.7 %collective-permute-start.1 = (bf16[160,512]{1,0:T(8,128)(2,1)}, bf16[160,512]{1,0:T(8,128)(2,1)S(1)}, u32[]{:S(2)}, u32[]{:S(2)}) collective-permute-start(bf16[160,512]{1,0:T(8,128)(2,1)} %bitcast.9), channel_id=1, source_target_pairs={{4,0},{8,4},{12,8},{14,12},{10,14},{6,10},{2,6},{0,2},{5,1},{9,5},... | collective-permute-start | bytes 491528 | tf_op jit(solution)/shard_map/ppermute | solution.py:44
  5.5 23.3 %copy-start.3 = (bf16[1,3,64,512]{3,2,1,0:T(8,128)(2,1)S(1)}, bf16[1,3,64,512]{3,2,1,0:T(8,128)(2,1)}, u32[]{:S(2)}) copy-start(bf16[1,3,64,512]{3,2,1,0:T(8,128)(2,1)} %param.11) | copy-start | bytes 589828
  6.2 7.4 %collective-permute-start.7 = (bf16[2,32,640]{2,1,0:T(8,128)(2,1)S(1)}, bf16[2,32,640]{2,1,0:T(8,128)(2,1)S(1)}, u32[]{:S(2)}, u32[]{:S(2)}) collective-permute-start(bf16[2,32,640]{2,1,0:T(8,128)(2,1)S(1)} %get-tuple-element.28), channel_id=1, source_target_pairs={{0,4},{2,6},{4,0},{6,2},{8,12},{10,14},{12,8},{14,10},{1,5},{3,7},... | collective-permute-start | bytes 245768 | tf_op jit(solution)/shard_map/ppermute | solution.py:64
  8.2 8.8 %collective-permute-start.8 = (bf16[2,32,640]{2,1,0:T(8,128)(2,1)S(1)}, bf16[2,32,640]{2,1,0:T(8,128)(2,1)S(1)}, u32[]{:S(2)}, u32[]{:S(2)}) collective-permute-start(bf16[2,32,640]{2,1,0:T(8,128)(2,1)S(1)} %get-tuple-element.29), channel_id=1, source_target_pairs={{0,8},{2,10},{4,12},{6,14},{8,0},{10,2},{12,4},{14,6},{1,9},{3,11}... | collective-permute-start | bytes 245768 | tf_op jit(solution)/shard_map/ppermute | solution.py:64
  10.8 7.1 %collective-permute-start.9 = (bf16[2,32,640]{2,1,0:T(8,128)(2,1)S(1)}, bf16[2,32,640]{2,1,0:T(8,128)(2,1)S(1)}, u32[]{:S(2)}, u32[]{:S(2)}) collective-permute-start(bf16[2,32,640]{2,1,0:T(8,128)(2,1)S(1)} %get-tuple-element.30), channel_id=1, source_target_pairs={{0,12},{2,14},{4,8},{6,10},{8,4},{10,6},{12,0},{14,2},{1,13},{3,15... | collective-permute-start | bytes 245768 | tf_op jit(solution)/shard_map/ppermute | solution.py:64
  10.8 7.1 %collective-permute-start.2 = (bf16[160,512]{1,0:T(8,128)(2,1)S(1)}, bf16[160,512]{1,0:T(8,128)(2,1)S(1)}, u32[]{:S(2)}, u32[]{:S(2)}) collective-permute-start(bf16[160,512]{1,0:T(8,128)(2,1)S(1)} %collective-permute-done.refs_1_), channel_id=1, source_target_pairs={{0,4},{4,8},{8,12},{12,14},{14,10},{10,6},{6,2},{2,0},{1,5},{5,9},... | collective-permute-start | bytes 491528 | tf_op jit(solution)/shard_map/ppermute | solution.py:45
  12.4 11.2 %collective-permute-start.3 = (bf16[160,512]{1,0:T(8,128)(2,1)S(1)}, bf16[160,512]{1,0:T(8,128)(2,1)S(1)}, u32[]{:S(2)}, u32[]{:S(2)}) collective-permute-start(bf16[160,512]{1,0:T(8,128)(2,1)S(1)} %collective-permute-done.1.refs_2_), channel_id=1, source_target_pairs={{4,0},{8,4},{12,8},{14,12},{10,14},{6,10},{2,6},{0,2},{5,1},{9,5},... | collective-permute-start | bytes 491528 | tf_op jit(solution)/shard_map/ppermute | solution.py:44
  18.0 10.8 %collective-permute-start.10 = (bf16[4,32,640]{2,1,0:T(8,128)(2,1)S(1)}, bf16[4,32,640]{2,1,0:T(8,128)(2,1)S(1)}, u32[]{:S(2)}, u32[]{:S(2)}) collective-permute-start(bf16[4,32,640]{2,1,0:T(8,128)(2,1)S(1)} %pad_maximum_fusion.1), channel_id=1, source_target_pairs={{0,2},{2,0},{4,6},{6,4},{8,10},{10,8},{12,14},{14,12},{1,3},{3,1},... | collective-permute-start | bytes 491528 | tf_op jit(solution)/shard_map/ppermute | solution.py:64
  20.0 6.3 %collective-permute-start.4 = (bf16[160,512]{1,0:T(8,128)(2,1)S(1)}, bf16[160,512]{1,0:T(8,128)(2,1)S(1)}, u32[]{:S(2)}, u32[]{:S(2)}) collective-permute-start(bf16[160,512]{1,0:T(8,128)(2,1)S(1)} %collective-permute-done.2.refs_3_), channel_id=1, source_target_pairs={{0,4},{4,8},{8,12},{12,14},{14,10},{10,6},{6,2},{2,0},{1,5},{5,9},... | collective-permute-start | bytes 491528 | tf_op jit(solution)/shard_map/ppermute | solution.py:45
  23.5 5.4 %collective-permute-start.11 = (bf16[4,32,640]{2,1,0:T(8,128)(2,1)S(1)}, bf16[4,32,640]{2,1,0:T(8,128)(2,1)S(1)}, u32[]{:S(2)}, u32[]{:S(2)}) collective-permute-start(bf16[4,32,640]{2,1,0:T(8,128)(2,1)S(1)} %pad_maximum_fusion.refs_0_), channel_id=1, source_target_pairs={{0,1},{1,0},{2,3},{3,2},{4,5},{5,4},{6,7},{7,6},{8,9},{9,8},{10,11... | collective-permute-start | bytes 491528 | tf_op jit(solution)/shard_map/ppermute | solution.py:68
  23.6 6.9 %collective-permute-start.5 = (bf16[160,512]{1,0:T(8,128)(2,1)S(1)}, bf16[160,512]{1,0:T(8,128)(2,1)S(1)}, u32[]{:S(2)}, u32[]{:S(2)}) collective-permute-start(bf16[160,512]{1,0:T(8,128)(2,1)S(1)} %collective-permute-done.3.refs_4_), channel_id=1, source_target_pairs={{4,0},{8,4},{12,8},{14,12},{10,14},{6,10},{2,6},{0,2},{5,1},{9,5},... | collective-permute-start | bytes 491528 | tf_op jit(solution)/shard_map/ppermute | solution.py:44
  26.3 5.3 %collective-permute-start.6 = (bf16[160,512]{1,0:T(8,128)(2,1)S(1)}, bf16[160,512]{1,0:T(8,128)(2,1)S(1)}, u32[]{:S(2)}, u32[]{:S(2)}) collective-permute-start(bf16[160,512]{1,0:T(8,128)(2,1)S(1)} %collective-permute-done.4.refs_5_), channel_id=1, source_target_pairs={{0,4},{4,8},{8,12},{12,14},{14,10},{10,6},{6,2},{2,0},{1,5},{5,9},... | collective-permute-start | bytes 491528 | tf_op jit(solution)/shard_map/ppermute | solution.py:45
  28.8 1.4 %collective-permute-start.12 = (bf16[4,32,640]{2,1,0:T(8,128)(2,1)S(1)}, bf16[4,32,640]{2,1,0:T(8,128)(2,1)S(1)}, u32[]{:S(2)}, u32[]{:S(2)}) collective-permute-start(bf16[4,32,640]{2,1,0:T(8,128)(2,1)S(1)} %collective-permute-done.10.refs_1_), channel_id=1, source_target_pairs={{0,1},{1,0},{2,3},{3,2},{4,5},{5,4},{6,7},{7,6},{8,9},{9,8},{10,11... | collective-permute-start | bytes 491528 | tf_op jit(solution)/shard_map/ppermute | solution.py:68
  33.6 5.9 %collective-permute-start.15 = (f32[8,1280]{1,0:T(8,128)S(1)}, f32[8,1280]{1,0:T(8,128)S(1)}, u32[]{:S(2)}, u32[]{:S(2)}) collective-permute-start(f32[8,1280]{1,0:T(8,128)S(1)} %get-tuple-element.44), channel_id=1, source_target_pairs={{0,12},{2,14},{4,8},{6,10},{8,4},{10,6},{12,0},{14,2},{1,13},{3,15... | collective-permute-start | bytes 122888 | tf_op jit(solution)/shard_map/ppermute | solution.py:64
  35.1 5.6 %collective-permute-start.14 = (f32[8,1280]{1,0:T(8,128)S(1)}, f32[8,1280]{1,0:T(8,128)S(1)}, u32[]{:S(2)}, u32[]{:S(2)}) collective-permute-start(f32[8,1280]{1,0:T(8,128)S(1)} %get-tuple-element.44), channel_id=1, source_target_pairs={{0,8},{2,10},{4,12},{6,14},{8,0},{10,2},{12,4},{14,6},{1,9},{3,11}... | collective-permute-start | bytes 122888 | tf_op jit(solution)/shard_map/ppermute | solution.py:64
  37.6 4.0 %collective-permute-start.13 = (f32[8,1280]{1,0:T(8,128)S(1)}, f32[8,1280]{1,0:T(8,128)S(1)}, u32[]{:S(2)}, u32[]{:S(2)}) collective-permute-start(f32[8,1280]{1,0:T(8,128)S(1)} %get-tuple-element.44), channel_id=1, source_target_pairs={{0,4},{2,6},{4,0},{6,2},{8,12},{10,14},{12,8},{14,10},{1,5},{3,7},... | collective-permute-start | bytes 122888 | tf_op jit(solution)/shard_map/ppermute | solution.py:64
  41.6 4.1 %collective-permute-start.16 = (f32[8,1280]{1,0:T(8,128)S(1)}, f32[8,1280]{1,0:T(8,128)S(1)}, u32[]{:S(2)}, u32[]{:S(2)}) collective-permute-start(f32[8,1280]{1,0:T(8,128)S(1)} %add_add_fusion), channel_id=1, source_target_pairs={{0,2},{2,0},{4,6},{6,4},{8,10},{10,8},{12,14},{14,12},{1,3},{3,1},... | collective-permute-start | bytes 122888 | tf_op jit(solution)/shard_map/ppermute | solution.py:64
  43.0 4.9 %collective-permute-start.18 = (f32[8,1280]{1,0:T(8,128)S(1)}, f32[8,1280]{1,0:T(8,128)S(1)}, u32[]{:S(2)}, u32[]{:S(2)}) collective-permute-start(f32[8,1280]{1,0:T(8,128)S(1)} %add_add_fusion), channel_id=1, source_target_pairs={{0,18},{2,16},{4,22},{6,20},{8,26},{10,24},{12,30},{14,28},{16,2},... | collective-permute-start | bytes 122888 | tf_op jit(solution)/shard_map/ppermute | solution.py:88
  44.1 4.0 %collective-permute-start.17 = (f32[8,1280]{1,0:T(8,128)S(1)}, f32[8,1280]{1,0:T(8,128)S(1)}, u32[]{:S(2)}, u32[]{:S(2)}) collective-permute-start(f32[8,1280]{1,0:T(8,128)S(1)} %add_add_fusion), channel_id=1, source_target_pairs={{0,16},{16,0},{1,17},{17,1},{2,18},{18,2},{3,19},{19,3},{4,20},{20... | collective-permute-start | bytes 122888 | tf_op jit(solution)/shard_map/ppermute | solution.py:87
  51.3 1.6 %collective-permute-start.19 = (bf16[8,32,640]{2,1,0:T(8,128)(2,1)S(1)}, bf16[8,32,640]{2,1,0:T(8,128)(2,1)S(1)}, u32[]{:S(2)}, u32[]{:S(2)}) collective-permute-start(bf16[8,32,640]{2,1,0:T(8,128)(2,1)S(1)} %get-tuple-element.46), channel_id=1, source_target_pairs={{0,1},{1,0},{2,3},{3,2},{4,5},{5,4},{6,7},{7,6},{8,9},{9,8},{10,11... | collective-permute-start | bytes 983048 | tf_op jit(solution)/shard_map/ppermute | solution.py:68
  53.7 14.2 %all-to-all-start = ((bf16[8,32,640]{2,1,0:T(8,128)(2,1)}), bf16[8,32,640]{2,1,0:T(8,128)(2,1)S(1)}, u32[]{:S(2)}, u32[]{:S(2)}) async-start(bf16[8,32,640]{2,1,0:T(8,128)(2,1)} %meet.1), calls=%async_computation | async-start | bytes 655360 | tf_op jit(solution)/shard_map/all_to_all | solution.py:700
  57.2 10.7 %collective-permute-start.21 = (f32[192,512]{1,0:T(8,128)S(1)}, f32[192,512]{1,0:T(8,128)S(1)}, u32[]{:S(2)}, u32[]{:S(2)}) collective-permute-start(f32[192,512]{1,0:T(8,128)S(1)} %get-tuple-element.47.time_mine), channel_id=1, source_target_pairs={{0,1},{1,0},{2,3},{3,2},{4,5},{5,4},{6,7},{7,6},{8,9},{9,8},{10,11... | collective-permute-start | bytes 1179656 | tf_op jit(solution)/shard_map/ppermute | solution.py:68
  67.9 1.6 %collective-permute-start.20 = (bf16[8,32,640]{2,1,0:T(8,128)(2,1)S(1)}, bf16[8,32,640]{2,1,0:T(8,128)(2,1)S(1)}, u32[]{:S(2)}, u32[]{:S(2)}) collective-permute-start(bf16[8,32,640]{2,1,0:T(8,128)(2,1)S(1)} %all-to-all-done.mine), channel_id=1, source_target_pairs={{0,1},{1,0},{2,3},{3,2},{4,5},{5,4},{6,7},{7,6},{8,9},{9,8},{10,11... | collective-permute-start | bytes 983048 | tf_op jit(solution)/shard_map/ppermute | solution.py:68
  (4 other events, 38.3 us)
